TPU v7x, 512 devices: a whole 4x8x8 slice. The times are simulated.
512 devices in a mesh: prefix: 16 (over z_lo, x), dec: 16 (over z_hi, y), tp: 2 (over core).
Axes of the slice: x: 4, y: 8, z: 8 (z_hi: 2, z_lo: 4; z = z_hi * 4 + z_lo), core: 2. Of those that a mesh axis runs over, the one named last changes fastest.
Arguments:
- queries: bfloat16 [4096, 4096], P(('prefix', 'dec'), 'tp'), may hold values from -12 to 12
- prefix_kv: bfloat16 [16, 2, 16384, 512], P('prefix', None, 'dec', 'tp'), may hold values from -12 to 12
- suffix_kv: bfloat16 [4096, 2, 64, 512], P(('prefix', 'dec'), None, None, 'tp'), may hold values from -12 to 12
- prefix_map: int32 [4096, 1], P(('prefix', 'dec')), may hold values from 0 to 15; in each aligned block of 16 rows (0 to 15, 16 to 31, ...) at most 2 rows name the same one
- suffix_len: int32 [256, 16], P(('prefix', 'dec')), may hold values from 1 to 64, 512 in all within a row
Outputs:
- attended: bfloat16 [4096, 4096], P(('prefix', 'dec', 'tp'))
Inputs may be any that keep to these rules, and one draw needn't show every extreme that they name: `prefix_map`: among the 16 requests of one device no prefix is named more than 2 times, and on some devices one prefix exactly 2 times. `suffix_len`: the 16 lengths of one device sum to 512, and the longest of them is 64.
All inputs are finite; a program needn't handle non-finite values.
Results may differ from a plain program's by a relative error of at most 0.025.
Values may be sent and summed in bfloat16 or wider, within the bound.
No kernel may reach another device: no remote copies, remote signals or barrier semaphores. Data moves between devices by JAX's collectives and lax.ppermute only.
A program may use at most 64 MiB of HBM per device.

v0:
```python
import functools
import math

import jax
import jax.numpy as jnp
from jax import lax
from jax.experimental import pallas as pl
from jax.experimental.pallas import tpu as pltpu
from jax.sharding import Mesh, PartitionSpec as P

HEAD = 128
GROUP = 8
SLOTS = 2
ROWS = SLOTS * GROUP
SCALE = HEAD ** (-0.5)
LOG2E = math.log2(math.e)
STATS = 16
Z_HALVES = 2
VMEM_LIMIT = 48 * 1024 * 1024


def iota(shape, dim):
    return lax.broadcasted_iota(jnp.int32, shape, dim)


def diagonal(size):
    return iota((size, size), 0) == iota((size, size), 1)


def to_lanes(column, eye):
    return jnp.sum(jnp.where(eye, column, 0.0), axis=0, keepdims=True)


def to_column(lanes, eye):
    return jnp.sum(jnp.where(eye, lanes, 0.0), axis=1, keepdims=True)


def slots_of(owners):
    count = owners.shape[0]
    owner_column = owners.astype(jnp.float32)
    owner_lanes = to_lanes(owner_column, diagonal(count))
    same = owner_column == owner_lanes
    row, lane = iota((count, count), 0), iota((count, count), 1)
    rank_lanes = jnp.sum(jnp.where(same & (row < lane), 1.0, 0.0), axis=0, keepdims=True)
    rank_column = jnp.sum(jnp.where(same & (lane < row), 1.0, 0.0), axis=1, keepdims=True)
    return owner_lanes * SLOTS + rank_lanes, owner_column * SLOTS + rank_column


def pieces_of(value):
    first = value.astype(jnp.bfloat16).astype(jnp.float32)
    second = (value - first).astype(jnp.bfloat16).astype(jnp.float32)
    return first, second, value - first - second


def place_kernel(owners_ref, queries_ref, out_ref):
    requests, heads = queries_ref.shape[0], queries_ref.shape[1] // HEAD
    slot_lanes, _ = slots_of(owners_ref[...])
    width = heads * requests
    spread = jnp.where(iota((requests, width), 1) % requests == iota((requests, width), 0), 1.0, 0.0)
    slot_wide = jnp.dot(
        jnp.broadcast_to(slot_lanes, (8, requests)).astype(jnp.bfloat16),
        spread.astype(jnp.bfloat16),
        preferred_element_type=jnp.float32,
    )[0:1]
    lane_code = slot_wide.astype(jnp.int32) * heads + iota((1, width), 1) // requests
    owners, halves, rows = out_ref.shape[:3]
    row = iota((owners * rows, 1), 0)
    slot = (row // rows) * SLOTS + (row // GROUP) % SLOTS
    row_code = slot * heads + (row // ROWS) % (heads // GROUP) * GROUP + row % GROUP
    pick = jnp.where(row_code == lane_code, 1.0, 0.0).astype(jnp.bfloat16)
    stacked = jnp.concatenate(
        [queries_ref[:, h * HEAD:(h + 1) * HEAD] for h in range(heads)], axis=0
    )
    placed = jnp.dot(pick, stacked, preferred_element_type=jnp.float32).astype(out_ref.dtype)
    placed = placed.reshape(owners, rows, HEAD)
    for half in range(halves):
        out_ref[:, half] = placed


def attend_kernel(count, key_ref, value_ref, *refs):
    key, value = key_ref[0, 0], value_ref[0, 0]
    wide = jnp.concatenate([value, jnp.ones_like(value)], axis=1)
    eye = diagonal(HEAD)
    blocks = HEAD // ROWS
    for query_ref, out_ref in zip(refs[:count], refs[count:]):
        size = query_ref.shape[0]
        levels = []
        for start in range(0, size, blocks):
            scores = lax.dot_general(
                query_ref[start:start + blocks].reshape(HEAD, HEAD),
                key,
                (((1,), (1,)), ((), ())),
                preferred_element_type=jnp.float32,
            )
            top = jnp.max(scores, axis=1, keepdims=True)
            weights = jnp.exp2((scores - top) * (SCALE * LOG2E))
            result = jnp.dot(weights.astype(jnp.bfloat16), wide, preferred_element_type=jnp.float32)
            total = result[:, HEAD:]
            out_ref[start:start + blocks] = (
                (result[:, :HEAD] / total).astype(out_ref.dtype).reshape(blocks, ROWS, HEAD)
            )
            levels.append(to_lanes(top * SCALE + jnp.log(total), eye))
        levels = jnp.concatenate(levels, axis=0)
        pieces = list(pieces_of(levels))
        spare = ROWS - 3 * levels.shape[0]
        if spare:
            pieces.append(jnp.zeros((spare, HEAD), jnp.float32))
        out_ref[size] = jnp.concatenate(pieces, axis=0).astype(out_ref.dtype)


def blend_kernel(sources, out_ref):
    eye = diagonal(HEAD)
    blocks = HEAD // ROWS
    kvs = (out_ref.shape[1] - STATS) // ROWS
    lane = iota((HEAD, HEAD), 1)
    for start in range(0, out_ref.shape[0], blocks):
        stats = jnp.zeros((HEAD, HEAD), jnp.float32)
        for kv in range(kvs):
            parts = []
            for refs in sources:
                offset = start
                for ref in refs:
                    size = ref.shape[0] - 1
                    if offset < size:
                        break
                    offset -= size
                groups = size // blocks
                table = ref[size, kv * ROWS:(kv + 1) * ROWS].astype(jnp.float32)
                at = offset // blocks
                level = table[at:at + 1] + table[groups + at:groups + at + 1]
                level = level + table[2 * groups + at:2 * groups + at + 1]
                mean = ref[offset:offset + blocks, kv * ROWS:(kv + 1) * ROWS].reshape(HEAD, HEAD)
                parts.append((level, mean))
            top = parts[0][0]
            for level, _ in parts[1:]:
                top = jnp.maximum(top, level)
            weights = [jnp.exp(level - top) for level, _ in parts]
            total = sum(weights)
            mixed = jnp.zeros((HEAD, HEAD), jnp.float32)
            for weight, (_, mean) in zip(weights, parts):
                mixed = mixed + mean.astype(jnp.float32) * to_column(weight / total, eye)
            out_ref[start:start + blocks, kv * ROWS:(kv + 1) * ROWS] = mixed.astype(
                out_ref.dtype
            ).reshape(blocks, ROWS, HEAD)
            column = to_column(top + jnp.log(total), eye)
            for index, piece in enumerate(pieces_of(column)):
                stats = jnp.where(lane == kv * 3 + index, piece, stats)
        out_ref[start:start + blocks, kvs * ROWS:] = stats.astype(out_ref.dtype).reshape(
            blocks, STATS, HEAD
        )


def tail_kernel(queries_ref, suffix_ref, length_ref, out_ref, max_ref, total_ref):
    requests = queries_ref.shape[0]
    limit = suffix_ref.shape[2]
    length = to_column(
        jnp.broadcast_to(length_ref[...].astype(jnp.float32), (requests, requests)), diagonal(requests)
    ).astype(jnp.int32)
    length = jnp.concatenate([length] * GROUP, axis=0)
    shape = (GROUP * requests, requests * limit)
    row, lane = iota(shape, 0), iota(shape, 1)
    shown = (lane // limit == row % requests) & (lane % limit < length)
    for kv in range(out_ref.shape[0]):
        query = jnp.concatenate(
            [
                queries_ref[:, h * HEAD:(h + 1) * HEAD]
                for h in range(kv * GROUP, (kv + 1) * GROUP)
            ],
            axis=0,
        )
        key = suffix_ref[:, 0, :, kv * HEAD:(kv + 1) * HEAD].reshape(requests * limit, HEAD)
        value = suffix_ref[:, 1, :, kv * HEAD:(kv + 1) * HEAD].reshape(requests * limit, HEAD)
        scores = lax.dot_general(
            query, key, (((1,), (1,)), ((), ())), preferred_element_type=jnp.float32
        ) * SCALE
        scores = jnp.where(shown, scores, -1e30)
        top = jnp.max(scores, axis=1, keepdims=True)
        weights = jnp.where(shown, jnp.exp(scores - top), 0.0)
        total = jnp.sum(weights, axis=1, keepdims=True)
        out_ref[kv] = jnp.dot(weights.astype(jnp.bfloat16), value, preferred_element_type=jnp.float32)
        max_ref[kv] = jnp.broadcast_to(top, max_ref.shape[1:])
        total_ref[kv] = jnp.broadcast_to(total, total_ref.shape[1:])


def merge_kernel(owners_ref, back_ref, tail_ref, max_ref, total_ref, out_ref):
    requests = owners_ref.shape[0]
    owners, halves, kvs = back_ref.shape[0], back_ref.shape[1], tail_ref.shape[0]
    _, slot = slots_of(owners_ref[...])
    slot = jnp.concatenate([slot] * GROUP, axis=0).astype(jnp.int32)
    row = iota((GROUP * requests, 1), 0)
    lane = iota((1, owners * ROWS), 1)
    pick = (slot * GROUP + row // requests) == lane
    pick = jnp.where(pick, 1.0, 0.0).astype(jnp.bfloat16)

    def picked(half, at):
        part = back_ref[:, half, at * ROWS:(at + 1) * ROWS].reshape(owners * ROWS, HEAD)
        return jnp.dot(pick, part, preferred_element_type=jnp.float32)

    stats = [picked(half, kvs) for half in range(halves)]
    for kv in range(kvs):
        levels = [
            stat[:, 3 * kv:3 * kv + 1] + stat[:, 3 * kv + 1:3 * kv + 2] + stat[:, 3 * kv + 2:3 * kv + 3]
            for stat in stats
        ]
        overall = max_ref[kv]
        for level in levels:
            overall = jnp.maximum(overall, level)
        tail_weight = jnp.exp(max_ref[kv] - overall)
        numerator = tail_ref[kv] * tail_weight
        denominator = total_ref[kv] * tail_weight
        for half, level in enumerate(levels):
            weight = jnp.exp(level - overall)
            numerator = numerator + picked(half, kv) * weight
            denominator = denominator + weight
        result = (numerator / denominator).astype(out_ref.dtype)
        for group in range(GROUP):
            head = kv * GROUP + group
            out_ref[:, head * HEAD:(head + 1) * HEAD] = result[group * requests:(group + 1) * requests]


def params():
    return pltpu.CompilerParams(vmem_limit_bytes=VMEM_LIMIT)


def place(owners, queries, owner_count):
    shape = (owner_count, Z_HALVES, SLOTS * queries.shape[1] // HEAD, HEAD)
    return pl.pallas_call(
        place_kernel,
        out_shape=jax.ShapeDtypeStruct(shape, queries.dtype),
        compiler_params=params(),
        name="place",
    )(owners, queries)


def attend(chunks, prefix_kv):
    tokens = prefix_kv.shape[2]
    kvs = prefix_kv.shape[3] // HEAD
    rows = sum(chunk.shape[0] * chunk.shape[1] for chunk in chunks)
    return pl.pallas_call(
        functools.partial(attend_kernel, len(chunks)),
        grid=(kvs,),
        in_specs=[
            pl.BlockSpec((1, 1, tokens, HEAD), lambda k: (0, 0, 0, k)),
            pl.BlockSpec((1, 1, tokens, HEAD), lambda k: (0, 1, 0, k)),
        ]
        + [pl.BlockSpec((chunk.shape[0], ROWS, HEAD), lambda k: (0, k, 0)) for chunk in chunks],
        out_specs=[
            pl.BlockSpec((chunk.shape[0] + 1, ROWS, HEAD), lambda k: (0, k, 0)) for chunk in chunks
        ],
        out_shape=[
            jax.ShapeDtypeStruct((chunk.shape[0] + 1,) + chunk.shape[1:], chunk.dtype)
            for chunk in chunks
        ],
        compiler_params=params(),
        cost_estimate=pl.CostEstimate(
            flops=8 * rows * tokens * HEAD, bytes_accessed=rows * HEAD * 4, transcendentals=rows * tokens
        ),
        name="attend",
    )(prefix_kv, prefix_kv, *chunks)


def blend(sources):
    flat = [part for parts in sources for part in parts]
    sizes = [len(parts) for parts in sources]

    def kernel(*refs):
        grouped, at = [], 0
        for size in sizes:
            grouped.append(refs[at:at + size])
            at += size
        blend_kernel(grouped, refs[-1])

    blocks = sum(part.shape[0] - 1 for part in sources[0])
    rows = flat[0].shape[1]
    return pl.pallas_call(
        kernel,
        out_shape=jax.ShapeDtypeStruct((blocks, rows + STATS, HEAD), flat[0].dtype),
        compiler_params=params(),
        name="blend",
    )(*flat)


def tail_attend(queries, suffix_kv, suffix_len):
    kvs = queries.shape[1] // (HEAD * GROUP)
    shape = jax.ShapeDtypeStruct((kvs, GROUP * queries.shape[0], HEAD), jnp.float32)
    return pl.pallas_call(
        tail_kernel,
        out_shape=[shape, shape, shape],
        compiler_params=params(),
        name="tail",
    )(queries, suffix_kv, suffix_len)


def merge(owners, back, tail, top, total, shape, dtype):
    return pl.pallas_call(
        merge_kernel,
        out_shape=jax.ShapeDtypeStruct(shape, dtype),
        compiler_params=params(),
        name="merge",
    )(owners, back, tail, top, total)


def shift(array, by):
    size = lax.axis_size("y")
    return lax.ppermute(array, "y", [(i, (i + by) % size) for i in range(size)])


def per_device(queries, prefix_kv, suffix_kv, prefix_map, suffix_len):
    owner_count = lax.axis_size("prefix")
    ring = lax.axis_size("y")
    plane = ("prefix", "zh")
    buckets = place(prefix_map, queries, owner_count)
    buckets = buckets.reshape((owner_count * Z_HALVES,) + buckets.shape[2:])
    mine = lax.all_to_all(buckets, plane, split_axis=0, concat_axis=0, tiled=True)
    half = mine.shape[0] // 2
    from_left, from_right = mine, mine
    sources = []
    steps = ring // 2
    for step in range(1, steps + 1):
        if step < steps:
            next_left, next_right = shift(from_left, 1), shift(from_right, -1)
        else:
            next_left, next_right = shift(from_left[:half], 1), shift(from_right[half:], -1)
        if step == 1:
            sources.append(attend([mine], prefix_kv))
        from_left, from_right = next_left, next_right
        to_left, to_right = attend([from_left, from_right], prefix_kv)
        if step < steps:
            sources.append([shift(to_left, -step)])
            sources.append([shift(to_right, step)])
        else:
            sources.append([shift(to_left, -step), shift(to_right, step)])
    tail, tail_max, tail_total = tail_attend(queries, suffix_kv, suffix_len)
    blended = blend(sources)
    back = lax.all_to_all(blended, plane, split_axis=0, concat_axis=0, tiled=True)
    back = back.reshape((owner_count, Z_HALVES) + back.shape[1:])
    attended = merge(prefix_map, back, tail, tail_max, tail_total, queries.shape, queries.dtype)
    return lax.all_to_all(attended, "tp", split_axis=0, concat_axis=1, tiled=True)


def solution(mesh):
    prefixes, decs, tps = mesh.devices.shape
    fine = Mesh(
        mesh.devices.reshape(prefixes, Z_HALVES, decs // Z_HALVES, tps), ("prefix", "zh", "y", "tp")
    )
    owner = ("prefix", "zh", "y")
    return jax.shard_map(
        per_device,
        mesh=fine,
        in_specs=(
            P(owner, "tp"),
            P("prefix", None, ("zh", "y"), "tp"),
            P(owner, None, None, "tp"),
            P(owner, None),
            P(owner, None),
        ),
        out_specs=P(owner + ("tp",), None),
        check_vma=False,
    )
```

profile of v0, /device:TPU:81, one launch (start us, length us, event | category | flops | bytes accessed | tf_op | source)
XLA Modules:
  0.0 151.9 jit_solution(6231369843774036152)
XLA Ops:
  0.0 0.7 copy.7.owners_ref
  0.7 0.8 copy-done.1
  1.6 0.4 place.1
  2.0 23.9 %all_to_all.29.refs_0_ = bf16[32,32,128]{2,1,0:T(8,128)(2,1)S(1)} all-to-all(bf16[32,32,128]{2,1,0:T(8,128)(2,1)S(1)} %bitcast.7), channel_id=1, replica_groups=mesh['prefix'=16,'zh'=2,'y'=8,'tp'=2] {'prefix','zh'}, dimensions={0} | all-to-all | bytes 524288 | tf_op jit(solution)/shard_map/all_to_all | solution.py:314
  25.9 3.2 %collective-permute-start = (bf16[32,32,128]{2,1,0:T(8,128)(2,1)S(1)}, bf16[32,32,128]{2,1,0:T(8,128)(2,1)S(1)}, u32[]{:S(2)}, u32[]{:S(2)}) collective-permute-start(bf16[32,32,128]{2,1,0:T(8,128)(2,1)S(1)} %all_to_all.29.refs_0_), channel_id=1, source_target_pairs={{0,2},{2,4},{4,6},{6,8},{8,10},{10,12},{12,14},{14,0},{1,3},{3,5},... | collective-permute-start | bytes 786440 | tf_op jit(solution)/shard_map/ppermute | solution.py:305
  29.1 2.1 %collective-permute-start.1 = (bf16[32,32,128]{2,1,0:T(8,128)(2,1)S(1)}, bf16[32,32,128]{2,1,0:T(8,128)(2,1)S(1)}, u32[]{:S(2)}, u32[]{:S(2)}) collective-permute-start(bf16[32,32,128]{2,1,0:T(8,128)(2,1)S(1)} %all_to_all.29.refs_0_), channel_id=1, source_target_pairs={{0,14},{2,0},{4,2},{6,4},{8,6},{10,8},{12,10},{14,12},{1,15},{3,1}... | collective-permute-start | bytes 786440 | tf_op jit(solution)/shard_map/ppermute | solution.py:305
  31.2 2.6 %collective-permute-done.refs_0_ = bf16[32,32,128]{2,1,0:T(8,128)(2,1)S(1)} collective-permute-done((bf16[32,32,128]{2,1,0:T(8,128)(2,1)S(1)}, bf16[32,32,128]{2,1,0:T(8,128)(2,1)S(1)}, u32[]{:S(2)}, u32[]{:S(2)}) %collective-permute-start) | collective-permute-done | bytes 262176 | tf_op jit(solution)/shard_map/ppermute | solution.py:305
  33.8 3.5 %collective-permute-start.4 = (bf16[32,32,128]{2,1,0:T(8,128)(2,1)S(1)}, bf16[32,32,128]{2,1,0:T(8,128)(2,1)S(1)}, u32[]{:S(2)}, u32[]{:S(2)}) collective-permute-start(bf16[32,32,128]{2,1,0:T(8,128)(2,1)S(1)} %collective-permute-done.refs_0_), channel_id=1, source_target_pairs={{0,2},{2,4},{4,6},{6,8},{8,10},{10,12},{12,14},{14,0},{1,3},{3,5},... | collective-permute-start | bytes 786440 | tf_op jit(solution)/shard_map/ppermute | solution.py:305
  37.3 0.8 collective-permute-done.1.refs_1_
  38.1 1.9 %collective-permute-start.5 = (bf16[32,32,128]{2,1,0:T(8,128)(2,1)S(1)}, bf16[32,32,128]{2,1,0:T(8,128)(2,1)S(1)}, u32[]{:S(2)}, u32[]{:S(2)}) collective-permute-start(bf16[32,32,128]{2,1,0:T(8,128)(2,1)S(1)} %collective-permute-done.1.refs_1_), channel_id=1, source_target_pairs={{0,14},{2,0},{4,2},{6,4},{8,6},{10,8},{12,10},{14,12},{1,15},{3,1}... | collective-permute-start | bytes 786440 | tf_op jit(solution)/shard_map/ppermute | solution.py:305
  40.0 0.9 collective-permute-done.4.refs_0_
  40.9 5.0 %collective-permute-start.8 = (bf16[32,32,128]{2,1,0:T(8,128)(2,1)S(1)}, bf16[32,32,128]{2,1,0:T(8,128)(2,1)S(1)}, u32[]{:S(2)}, u32[]{:S(2)}) collective-permute-start(bf16[32,32,128]{2,1,0:T(8,128)(2,1)S(1)} %collective-permute-done.4.refs_0_), channel_id=1, source_target_pairs={{0,2},{2,4},{4,6},{6,8},{8,10},{10,12},{12,14},{14,0},{1,3},{3,5},... | collective-permute-start | bytes 786440 | tf_op jit(solution)/shard_map/ppermute | solution.py:305
  45.9 0.5 collective-permute-done.5.refs_1_
  46.4 1.9 %collective-permute-start.9 = (bf16[32,32,128]{2,1,0:T(8,128)(2,1)S(1)}, bf16[32,32,128]{2,1,0:T(8,128)(2,1)S(1)}, u32[]{:S(2)}, u32[]{:S(2)}) collective-permute-start(bf16[32,32,128]{2,1,0:T(8,128)(2,1)S(1)} %collective-permute-done.5.refs_1_), channel_id=1, source_target_pairs={{0,14},{2,0},{4,2},{6,4},{8,6},{10,8},{12,10},{14,12},{1,15},{3,1}... | collective-permute-start | bytes 786440 | tf_op jit(solution)/shard_map/ppermute | solution.py:305
  48.3 0.0 copy-start.4
  48.3 1.2 copy-done.4
  49.6 3.5 %attend.6 = (bf16[33,32,128]{2,1,0:T(8,128)(2,1)S(1)}, bf16[33,32,128]{2,1,0:T(8,128)(2,1)S(1)}) custom-call(bf16[1,2,1024,256]{3,2,1,0:T(8,128)(2,1)S(1)} %copy-done.4, bf16[1,2,1024,256]{3,2,1,0:T(8,128)(2,1)S(1)} %copy-done.4, bf16[32,32,128]{2,1,0:T(8,128)(2,1)S(1)} %collective-permute-done.refs_0_, bf16[32,32,128]{2,1,0:T(8,128)(2,1)S(1)} %collective-permute-done.1.refs_1_), custom_call_target="tpu_custom_call" | custom-call | flops 2147483648 | bytes 1048576 | tf_op jit(solution)/shard_map/attend/pallas_call | solution.py:239
  53.1 1.9 %collective-permute-start.2 = (bf16[33,32,128]{2,1,0:T(8,128)(2,1)S(1)}, bf16[33,32,128]{2,1,0:T(8,128)(2,1)S(1)}, u32[]{:S(2)}, u32[]{:S(2)}) collective-permute-start(bf16[33,32,128]{2,1,0:T(8,128)(2,1)S(1)} %get-tuple-element.16), channel_id=1, source_target_pairs={{0,14},{2,0},{4,2},{6,4},{8,6},{10,8},{12,10},{14,12},{1,15},{3,1}... | collective-permute-start | bytes 811016 | tf_op jit(solution)/shard_map/ppermute | solution.py:305
  55.0 4.6 %collective-permute-start.3 = (bf16[33,32,128]{2,1,0:T(8,128)(2,1)S(1)}, bf16[33,32,128]{2,1,0:T(8,128)(2,1)S(1)}, u32[]{:S(2)}, u32[]{:S(2)}) collective-permute-start(bf16[33,32,128]{2,1,0:T(8,128)(2,1)S(1)} %get-tuple-element.17), channel_id=1, source_target_pairs={{0,2},{2,4},{4,6},{6,8},{8,10},{10,12},{12,14},{14,0},{1,3},{3,5},... | collective-permute-start | bytes 811016 | tf_op jit(solution)/shard_map/ppermute | solution.py:305
  59.6 3.5 %attend.7 = (bf16[33,32,128]{2,1,0:T(8,128)(2,1)S(1)}, bf16[33,32,128]{2,1,0:T(8,128)(2,1)S(1)}) custom-call(bf16[1,2,1024,256]{3,2,1,0:T(8,128)(2,1)S(1)} %copy-done.4, bf16[1,2,1024,256]{3,2,1,0:T(8,128)(2,1)S(1)} %copy-done.4, bf16[32,32,128]{2,1,0:T(8,128)(2,1)S(1)} %collective-permute-done.4.refs_0_, bf16[32,32,128]{2,1,0:T(8,128)(2,1)S(1)} %collective-permute-done.5.refs_1_), custom_call_target="tpu_custom_call" | custom-call | flops 2147483648 | bytes 1048576 | tf_op jit(solution)/shard_map/attend/pallas_call | solution.py:239
  63.1 3.1 %collective-permute-start.6 = (bf16[33,32,128]{2,1,0:T(8,128)(2,1)S(1)}, bf16[33,32,128]{2,1,0:T(8,128)(2,1)S(1)}, u32[]{:S(2)}, u32[]{:S(2)}) collective-permute-start(bf16[33,32,128]{2,1,0:T(8,128)(2,1)S(1)} %get-tuple-element.18), channel_id=1, source_target_pairs={{0,12},{2,14},{4,0},{6,2},{8,4},{10,6},{12,8},{14,10},{1,13},{3,15... | collective-permute-start | bytes 811016 | tf_op jit(solution)/shard_map/ppermute | solution.py:305
  66.2 0.0 collective-permute-done.8.refs_0_
  66.3 3.4 %collective-permute-start.12 = (bf16[16,32,128]{2,1,0:T(8,128)(2,1)S(1)}, bf16[16,32,128]{2,1,0:T(8,128)(2,1)S(1)}, u32[]{:S(2)}, u32[]{:S(2)}) collective-permute-start(bf16[16,32,128]{2,1,0:T(8,128)(2,1)S(1)} %slice.8), channel_id=1, source_target_pairs={{0,2},{2,4},{4,6},{6,8},{8,10},{10,12},{12,14},{14,0},{1,3},{3,5},... | collective-permute-start | bytes 393224 | tf_op jit(solution)/shard_map/ppermute | solution.py:305
  69.7 0.0 collective-permute-done.9.refs_1_
  69.7 1.9 %collective-permute-start.13 = (bf16[16,32,128]{2,1,0:T(8,128)(2,1)S(1)}, bf16[16,32,128]{2,1,0:T(8,128)(2,1)S(1)}, u32[]{:S(2)}, u32[]{:S(2)}) collective-permute-start(bf16[16,32,128]{2,1,0:T(8,128)(2,1)S(1)} %slice.9), channel_id=1, source_target_pairs={{0,14},{2,0},{4,2},{6,4},{8,6},{10,8},{12,10},{14,12},{1,15},{3,1}... | collective-permute-start | bytes 393224 | tf_op jit(solution)/shard_map/ppermute | solution.py:305
  71.6 3.5 %attend.8 = (bf16[33,32,128]{2,1,0:T(8,128)(2,1)S(1)}, bf16[33,32,128]{2,1,0:T(8,128)(2,1)S(1)}) custom-call(bf16[1,2,1024,256]{3,2,1,0:T(8,128)(2,1)S(1)} %copy-done.4, bf16[1,2,1024,256]{3,2,1,0:T(8,128)(2,1)S(1)} %copy-done.4, bf16[32,32,128]{2,1,0:T(8,128)(2,1)S(1)} %collective-permute-done.8.refs_0_, bf16[32,32,128]{2,1,0:T(8,128)(2,1)S(1)} %collective-permute-done.9.refs_1_), custom_call_target="tpu_custom_call" | custom-call | flops 2147483648 | bytes 1048576 | tf_op jit(solution)/shard_map/attend/pallas_call | solution.py:239
  75.1 0.0 collective-permute-done.2.refs_1_
  75.2 5.7 %collective-permute-start.7 = (bf16[33,32,128]{2,1,0:T(8,128)(2,1)S(1)}, bf16[33,32,128]{2,1,0:T(8,128)(2,1)S(1)}, u32[]{:S(2)}, u32[]{:S(2)}) collective-permute-start(bf16[33,32,128]{2,1,0:T(8,128)(2,1)S(1)} %get-tuple-element.19), channel_id=1, source_target_pairs={{0,4},{2,6},{4,8},{6,10},{8,12},{10,14},{12,0},{14,2},{1,5},{3,7},... | collective-permute-start | bytes 811016 | tf_op jit(solution)/shard_map/ppermute | solution.py:305
  80.9 2.6 %collective-permute-start.10 = (bf16[33,32,128]{2,1,0:T(8,128)(2,1)S(1)}, bf16[33,32,128]{2,1,0:T(8,128)(2,1)S(1)}, u32[]{:S(2)}, u32[]{:S(2)}) collective-permute-start(bf16[33,32,128]{2,1,0:T(8,128)(2,1)S(1)} %get-tuple-element.20), channel_id=1, source_target_pairs={{0,10},{2,12},{4,14},{6,0},{8,2},{10,4},{12,6},{14,8},{1,11},{3,13... | collective-permute-start | bytes 811016 | tf_op jit(solution)/shard_map/ppermute | solution.py:305
  83.5 5.7 %collective-permute-start.11 = (bf16[33,32,128]{2,1,0:T(8,128)(2,1)S(1)}, bf16[33,32,128]{2,1,0:T(8,128)(2,1)S(1)}, u32[]{:S(2)}, u32[]{:S(2)}) collective-permute-start(bf16[33,32,128]{2,1,0:T(8,128)(2,1)S(1)} %get-tuple-element.21), channel_id=1, source_target_pairs={{0,6},{2,8},{4,10},{6,12},{8,14},{10,0},{12,2},{14,4},{1,7},{3,9},... | collective-permute-start | bytes 811016 | tf_op jit(solution)/shard_map/ppermute | solution.py:305
  89.2 2.4 %attend.9 = (bf16[17,32,128]{2,1,0:T(8,128)(2,1)S(1)}, bf16[17,32,128]{2,1,0:T(8,128)(2,1)S(1)}) custom-call(bf16[1,2,1024,256]{3,2,1,0:T(8,128)(2,1)S(1)} %copy-done.4, bf16[1,2,1024,256]{3,2,1,0:T(8,128)(2,1)S(1)} %copy-done.4, bf16[16,32,128]{2,1,0:T(8,128)(2,1)S(1)} %collective-permute-done.12.refs_0_, ...), custom_call_target="tpu_custom_call" | custom-call | flops 1073741824 | bytes 524288 | tf_op jit(solution)/shard_map/attend/pallas_call | solution.py:239
  91.6 0.0 collective-permute-done.3.refs_2_
  91.6 3.7 %collective-permute-start.14 = (bf16[17,32,128]{2,1,0:T(8,128)(2,1)S(1)}, bf16[17,32,128]{2,1,0:T(8,128)(2,1)S(1)}, u32[]{:S(2)}, u32[]{:S(2)}) collective-permute-start(bf16[17,32,128]{2,1,0:T(8,128)(2,1)S(1)} %get-tuple-element.22), channel_id=1, source_target_pairs={{0,8},{2,10},{4,12},{6,14},{8,0},{10,2},{12,4},{14,6},{1,9},{3,11}... | collective-permute-start | bytes 417800 | tf_op jit(solution)/shard_map/ppermute | solution.py:305
  95.3 0.0 collective-permute-done.6.refs_3_
  95.3 5.5 %collective-permute-start.15 = (bf16[17,32,128]{2,1,0:T(8,128)(2,1)S(1)}, bf16[17,32,128]{2,1,0:T(8,128)(2,1)S(1)}, u32[]{:S(2)}, u32[]{:S(2)}) collective-permute-start(bf16[17,32,128]{2,1,0:T(8,128)(2,1)S(1)} %get-tuple-element.23), channel_id=1, source_target_pairs={{0,8},{2,10},{4,12},{6,14},{8,0},{10,2},{12,4},{14,6},{1,9},{3,11}... | collective-permute-start | bytes 417800 | tf_op jit(solution)/shard_map/ppermute | solution.py:305
  100.8 2.3 %attend.5.refs_0_ = bf16[33,32,128]{2,1,0:T(8,128)(2,1)S(1)} custom-call(bf16[1,2,1024,256]{3,2,1,0:T(8,128)(2,1)S(1)} %copy-done.4, bf16[1,2,1024,256]{3,2,1,0:T(8,128)(2,1)S(1)} %copy-done.4, bf16[32,32,128]{2,1,0:T(8,128)(2,1)S(1)} %all_to_all.29.refs_0_), custom_call_target="tpu_custom_call" | custom-call | flops 1073741824 | bytes 524288 | tf_op jit(solution)/shard_map/attend/pallas_call | solution.py:239
  103.2 0.0 copy-start
  103.2 15.2 %collective-permute-done.14.refs_7_ = bf16[17,32,128]{2,1,0:T(8,128)(2,1)S(1)} collective-permute-done((bf16[17,32,128]{2,1,0:T(8,128)(2,1)S(1)}, bf16[17,32,128]{2,1,0:T(8,128)(2,1)S(1)}, u32[]{:S(2)}, u32[]{:S(2)}) %collective-permute-start.14) | collective-permute-done | bytes 139296 | tf_op jit(solution)/shard_map/ppermute | solution.py:305
  118.4 4.6 %collective-permute-done.15.refs_8_ = bf16[17,32,128]{2,1,0:T(8,128)(2,1)S(1)} collective-permute-done((bf16[17,32,128]{2,1,0:T(8,128)(2,1)S(1)}, bf16[17,32,128]{2,1,0:T(8,128)(2,1)S(1)}, u32[]{:S(2)}, u32[]{:S(2)}) %collective-permute-start.15) | collective-permute-done | bytes 139296 | tf_op jit(solution)/shard_map/ppermute | solution.py:305
  123.0 0.0 collective-permute-done.10.refs_5_
  123.0 0.0 collective-permute-done.11.refs_6_
  123.0 2.1 %blend.1 = bf16[32,48,128]{2,1,0:T(8,128)(2,1)} custom-call(bf16[33,32,128]{2,1,0:T(8,128)(2,1)S(1)} %attend.5.refs_0_, bf16[33,32,128]{2,1,0:T(8,128)(2,1)S(1)} %collective-permute-done.2.refs_1_, bf16[33,32,128]{2,1,0:T(8,128)(2,1)S(1)} %collective-permute-done.3.refs_2_, bf16[33,32,128]{2,1,0:T(8,128)(2,1)S(1)} %collective-permute-done.6.refs_3_, ...), custom_call_target="tpu_custom_call" | custom-call | tf_op jit(solution)/shard_map/blend/pallas_call | solution.py:275
  125.0 5.5 %all-to-all-start.1 = ((bf16[32,48,128]{2,1,0:T(8,128)(2,1)}), bf16[32,48,128]{2,1,0:T(8,128)(2,1)S(1)}, u32[]{:S(2)}, u32[]{:S(2)}) async-start(bf16[32,48,128]{2,1,0:T(8,128)(2,1)} %blend.1), calls=%async_computation.1 | async-start | bytes 786432 | tf_op jit(solution)/shard_map/all_to_all | solution.py:335
  130.6 0.8 tail.1
  131.5 13.0 %all-to-all-done.1 = bf16[32,48,128]{2,1,0:T(8,128)(2,1)S(1)} async-done(((bf16[32,48,128]{2,1,0:T(8,128)(2,1)}), bf16[32,48,128]{2,1,0:T(8,128)(2,1)S(1)}, u32[]{:S(2)}, u32[]{:S(2)}) %all-to-all-start.1) | async-done | bytes 393248 | tf_op jit(solution)/shard_map/all_to_all | solution.py:335
  144.5 0.6 merge.1
  145.1 6.2 %all_to_all.30 = bf16[2,8,2048]{2,1,0:T(8,128)(2,1)S(1)} all-to-all(bf16[2,8,2048]{2,1,0:T(8,128)(2,1)S(1)} %bitcast.8), channel_id=1, replica_groups=mesh['prefix'=16,'zh'=2,'y'=8,'tp'=2] {'tp'}, dimensions={0} | all-to-all | bytes 131072 | tf_op jit(solution)/shard_map/all_to_all | solution.py:338
  151.3 0.6 copy.9
  (11 shorter events, 0.0 us)
Async XLA Ops:
  0.7 0.8 copy-start.1
  25.9 7.9 %collective-permute-start = (bf16[32,32,128]{2,1,0:T(8,128)(2,1)S(1)}, bf16[32,32,128]{2,1,0:T(8,128)(2,1)S(1)}, u32[]{:S(2)}, u32[]{:S(2)}) collective-permute-start(bf16[32,32,128]{2,1,0:T(8,128)(2,1)S(1)} %all_to_all.29.refs_0_), channel_id=1, source_target_pairs={{0,2},{2,4},{4,6},{6,8},{8,10},{10,12},{12,14},{14,0},{1,3},{3,5},... | collective-permute-start | bytes 786440 | tf_op jit(solution)/shard_map/ppermute | solution.py:305
  29.1 9.0 %collective-permute-start.1 = (bf16[32,32,128]{2,1,0:T(8,128)(2,1)S(1)}, bf16[32,32,128]{2,1,0:T(8,128)(2,1)S(1)}, u32[]{:S(2)}, u32[]{:S(2)}) collective-permute-start(bf16[32,32,128]{2,1,0:T(8,128)(2,1)S(1)} %all_to_all.29.refs_0_), channel_id=1, source_target_pairs={{0,14},{2,0},{4,2},{6,4},{8,6},{10,8},{12,10},{14,12},{1,15},{3,1}... | collective-permute-start | bytes 786440 | tf_op jit(solution)/shard_map/ppermute | solution.py:305
  33.8 7.1 %collective-permute-start.4 = (bf16[32,32,128]{2,1,0:T(8,128)(2,1)S(1)}, bf16[32,32,128]{2,1,0:T(8,128)(2,1)S(1)}, u32[]{:S(2)}, u32[]{:S(2)}) collective-permute-start(bf16[32,32,128]{2,1,0:T(8,128)(2,1)S(1)} %collective-permute-done.refs_0_), channel_id=1, source_target_pairs={{0,2},{2,4},{4,6},{6,8},{8,10},{10,12},{12,14},{14,0},{1,3},{3,5},... | collective-permute-start | bytes 786440 | tf_op jit(solution)/shard_map/ppermute | solution.py:305
  38.1 8.3 %collective-permute-start.5 = (bf16[32,32,128]{2,1,0:T(8,128)(2,1)S(1)}, bf16[32,32,128]{2,1,0:T(8,128)(2,1)S(1)}, u32[]{:S(2)}, u32[]{:S(2)}) collective-permute-start(bf16[32,32,128]{2,1,0:T(8,128)(2,1)S(1)} %collective-permute-done.1.refs_1_), channel_id=1, source_target_pairs={{0,14},{2,0},{4,2},{6,4},{8,6},{10,8},{12,10},{14,12},{1,15},{3,1}... | collective-permute-start | bytes 786440 | tf_op jit(solution)/shard_map/ppermute | solution.py:305
  40.9 25.3 %collective-permute-start.8 = (bf16[32,32,128]{2,1,0:T(8,128)(2,1)S(1)}, bf16[32,32,128]{2,1,0:T(8,128)(2,1)S(1)}, u32[]{:S(2)}, u32[]{:S(2)}) collective-permute-start(bf16[32,32,128]{2,1,0:T(8,128)(2,1)S(1)} %collective-permute-done.4.refs_0_), channel_id=1, source_target_pairs={{0,2},{2,4},{4,6},{6,8},{8,10},{10,12},{12,14},{14,0},{1,3},{3,5},... | collective-permute-start | bytes 786440 | tf_op jit(solution)/shard_map/ppermute | solution.py:305
  46.4 23.2 %collective-permute-start.9 = (bf16[32,32,128]{2,1,0:T(8,128)(2,1)S(1)}, bf16[32,32,128]{2,1,0:T(8,128)(2,1)S(1)}, u32[]{:S(2)}, u32[]{:S(2)}) collective-permute-start(bf16[32,32,128]{2,1,0:T(8,128)(2,1)S(1)} %collective-permute-done.5.refs_1_), channel_id=1, source_target_pairs={{0,14},{2,0},{4,2},{6,4},{8,6},{10,8},{12,10},{14,12},{1,15},{3,1}... | collective-permute-start | bytes 786440 | tf_op jit(solution)/shard_map/ppermute | solution.py:305
  48.3 1.2 copy-start.4
  53.1 22.1 %collective-permute-start.2 = (bf16[33,32,128]{2,1,0:T(8,128)(2,1)S(1)}, bf16[33,32,128]{2,1,0:T(8,128)(2,1)S(1)}, u32[]{:S(2)}, u32[]{:S(2)}) collective-permute-start(bf16[33,32,128]{2,1,0:T(8,128)(2,1)S(1)} %get-tuple-element.16), channel_id=1, source_target_pairs={{0,14},{2,0},{4,2},{6,4},{8,6},{10,8},{12,10},{14,12},{1,15},{3,1}... | collective-permute-start | bytes 811016 | tf_op jit(solution)/shard_map/ppermute | solution.py:305
  55.0 36.6 %collective-permute-start.3 = (bf16[33,32,128]{2,1,0:T(8,128)(2,1)S(1)}, bf16[33,32,128]{2,1,0:T(8,128)(2,1)S(1)}, u32[]{:S(2)}, u32[]{:S(2)}) collective-permute-start(bf16[33,32,128]{2,1,0:T(8,128)(2,1)S(1)} %get-tuple-element.17), channel_id=1, source_target_pairs={{0,2},{2,4},{4,6},{6,8},{8,10},{10,12},{12,14},{14,0},{1,3},{3,5},... | collective-permute-start | bytes 811016 | tf_op jit(solution)/shard_map/ppermute | solution.py:305
  63.1 32.2 %collective-permute-start.6 = (bf16[33,32,128]{2,1,0:T(8,128)(2,1)S(1)}, bf16[33,32,128]{2,1,0:T(8,128)(2,1)S(1)}, u32[]{:S(2)}, u32[]{:S(2)}) collective-permute-start(bf16[33,32,128]{2,1,0:T(8,128)(2,1)S(1)} %get-tuple-element.18), channel_id=1, source_target_pairs={{0,12},{2,14},{4,0},{6,2},{8,4},{10,6},{12,8},{14,10},{1,13},{3,15... | collective-permute-start | bytes 811016 | tf_op jit(solution)/shard_map/ppermute | solution.py:305
  66.3 14.6 %collective-permute-start.12 = (bf16[16,32,128]{2,1,0:T(8,128)(2,1)S(1)}, bf16[16,32,128]{2,1,0:T(8,128)(2,1)S(1)}, u32[]{:S(2)}, u32[]{:S(2)}) collective-permute-start(bf16[16,32,128]{2,1,0:T(8,128)(2,1)S(1)} %slice.8), channel_id=1, source_target_pairs={{0,2},{2,4},{4,6},{6,8},{8,10},{10,12},{12,14},{14,0},{1,3},{3,5},... | collective-permute-start | bytes 393224 | tf_op jit(solution)/shard_map/ppermute | solution.py:305
  69.7 13.8 %collective-permute-start.13 = (bf16[16,32,128]{2,1,0:T(8,128)(2,1)S(1)}, bf16[16,32,128]{2,1,0:T(8,128)(2,1)S(1)}, u32[]{:S(2)}, u32[]{:S(2)}) collective-permute-start(bf16[16,32,128]{2,1,0:T(8,128)(2,1)S(1)} %slice.9), channel_id=1, source_target_pairs={{0,14},{2,0},{4,2},{6,4},{8,6},{10,8},{12,10},{14,12},{1,15},{3,1}... | collective-permute-start | bytes 393224 | tf_op jit(solution)/shard_map/ppermute | solution.py:305
  75.2 28.0 %collective-permute-start.7 = (bf16[33,32,128]{2,1,0:T(8,128)(2,1)S(1)}, bf16[33,32,128]{2,1,0:T(8,128)(2,1)S(1)}, u32[]{:S(2)}, u32[]{:S(2)}) collective-permute-start(bf16[33,32,128]{2,1,0:T(8,128)(2,1)S(1)} %get-tuple-element.19), channel_id=1, source_target_pairs={{0,4},{2,6},{4,8},{6,10},{8,12},{10,14},{12,0},{14,2},{1,5},{3,7},... | collective-permute-start | bytes 811016 | tf_op jit(solution)/shard_map/ppermute | solution.py:305
  80.9 42.0 %collective-permute-start.10 = (bf16[33,32,128]{2,1,0:T(8,128)(2,1)S(1)}, bf16[33,32,128]{2,1,0:T(8,128)(2,1)S(1)}, u32[]{:S(2)}, u32[]{:S(2)}) collective-permute-start(bf16[33,32,128]{2,1,0:T(8,128)(2,1)S(1)} %get-tuple-element.20), channel_id=1, source_target_pairs={{0,10},{2,12},{4,14},{6,0},{8,2},{10,4},{12,6},{14,8},{1,11},{3,13... | collective-permute-start | bytes 811016 | tf_op jit(solution)/shard_map/ppermute | solution.py:305
  83.5 39.5 %collective-permute-start.11 = (bf16[33,32,128]{2,1,0:T(8,128)(2,1)S(1)}, bf16[33,32,128]{2,1,0:T(8,128)(2,1)S(1)}, u32[]{:S(2)}, u32[]{:S(2)}) collective-permute-start(bf16[33,32,128]{2,1,0:T(8,128)(2,1)S(1)} %get-tuple-element.21), channel_id=1, source_target_pairs={{0,6},{2,8},{4,10},{6,12},{8,14},{10,0},{12,2},{14,4},{1,7},{3,9},... | collective-permute-start | bytes 811016 | tf_op jit(solution)/shard_map/ppermute | solution.py:305
  91.6 26.7 %collective-permute-start.14 = (bf16[17,32,128]{2,1,0:T(8,128)(2,1)S(1)}, bf16[17,32,128]{2,1,0:T(8,128)(2,1)S(1)}, u32[]{:S(2)}, u32[]{:S(2)}) collective-permute-start(bf16[17,32,128]{2,1,0:T(8,128)(2,1)S(1)} %get-tuple-element.22), channel_id=1, source_target_pairs={{0,8},{2,10},{4,12},{6,14},{8,0},{10,2},{12,4},{14,6},{1,9},{3,11}... | collective-permute-start | bytes 417800 | tf_op jit(solution)/shard_map/ppermute | solution.py:305
  95.3 27.6 %collective-permute-start.15 = (bf16[17,32,128]{2,1,0:T(8,128)(2,1)S(1)}, bf16[17,32,128]{2,1,0:T(8,128)(2,1)S(1)}, u32[]{:S(2)}, u32[]{:S(2)}) collective-permute-start(bf16[17,32,128]{2,1,0:T(8,128)(2,1)S(1)} %get-tuple-element.23), channel_id=1, source_target_pairs={{0,8},{2,10},{4,12},{6,14},{8,0},{10,2},{12,4},{14,6},{1,9},{3,11}... | collective-permute-start | bytes 417800 | tf_op jit(solution)/shard_map/ppermute | solution.py:305
  103.2 27.4 %copy-start = (bf16[16,2,64,256]{3,2,1,0:T(8,128)(2,1)S(1)}, bf16[16,2,64,256]{3,2,1,0:T(8,128)(2,1)}, u32[]{:S(2)}) copy-start(bf16[16,2,64,256]{3,2,1,0:T(8,128)(2,1)} %suffix_ref.1) | copy-start | bytes 3145732
  125.0 5.6 %copy-start.2 = (bf16[16,2048]{1,0:T(8,128)(2,1)S(1)}, bf16[16,2048]{1,0:T(8,128)(2,1)}, u32[]{:S(2)}) copy-start(bf16[16,2048]{1,0:T(8,128)(2,1)} %queries_ref.3) | copy-start | bytes 196612
  125.0 5.6 %copy-start.3 = (s32[1,16]{1,0:T(1,128)S(1)}, s32[1,16]{1,0:T(1,128)}, u32[]{:S(2)}) copy-start(s32[1,16]{1,0:T(1,128)} %length_ref.1) | copy-start | bytes 196
  125.0 19.4 %all-to-all-start.1 = ((bf16[32,48,128]{2,1,0:T(8,128)(2,1)}), bf16[32,48,128]{2,1,0:T(8,128)(2,1)S(1)}, u32[]{:S(2)}, u32[]{:S(2)}) async-start(bf16[32,48,128]{2,1,0:T(8,128)(2,1)} %blend.1), calls=%async_computation.1 | async-start | bytes 786432 | tf_op jit(solution)/shard_map/all_to_all | solution.py:335
where the time goes:
time: 153 us; the launch traced here: 152 us
  starting transfers between devices  61.2 us (40%)
  waiting for transfers between devices  37.6 us (25%)
  blocking collectives  30.1 us (20%)
  Pallas kernels  19.2 us (13%)
  local copies, waits for them, and re-layouts  3.45 us (2%)
    ppermute x16, starting transfers between devices, shift(): return lax.ppermute(array, 'y', [(i, (i + by) % size) for i in range(size)])  55.7 us
    ppermute x16, waiting for transfers between devices, shift(): return lax.ppermute(array, 'y', [(i, (i + by) % size) for i in range(size)])  24.6 us
    all_to_all x1, blocking collectives, per_device(): lax.all_to_all(buckets, plane, split_axis=0, concat_axis=0, tiled=True)  23.9 us
    pallas_call x5, Pallas kernels, attend(): pl.pallas_call(functools.partial(attend_kernel, len(chunks)), grid=(kvs,)...  15.3 us
    all_to_all x1, waiting for transfers between devices, per_device(): lax.all_to_all(blended, plane, split_axis=0, concat_axis=0, tiled=True)  13 us
    all_to_all x1, blocking collectives, per_device(): lax.all_to_all(attended, 'tp', split_axis=0, concat_axis=1, tiled=True)  6.16 us
    all_to_all x1, starting transfers between devices, per_device(): lax.all_to_all(blended, plane, split_axis=0, concat_axis=0, tiled=True)  5.54 us
    unnamed x12, local copies, waits for them, and re-layouts  3.43 us
  transfers between devices with their start and end apart: 17, of which 7 were waited for; matrix products, arithmetic and copies ran while one was open for 0% of the time, Pallas kernels for 11%

commit v1 on v0

--- a/solution.py
+++ b/solution.py
@@ -77,77 +77,76 @@
         out_ref[:, half] = placed
 
 
-def attend_kernel(count, key_ref, value_ref, *refs):
-    key, value = key_ref[0, 0], value_ref[0, 0]
-    wide = jnp.concatenate([value, jnp.ones_like(value)], axis=1)
+def attend_kernel(key_ref, value_ref, far_key_ref, far_value_ref, query_ref, out_ref):
+    keys = (key_ref[0, 0], far_key_ref[0, 0])
+    values = (value_ref[0, 0], far_value_ref[0, 0])
+    wides = [jnp.concatenate([value, jnp.ones_like(value)], axis=1) for value in values]
     eye = diagonal(HEAD)
     blocks = HEAD // ROWS
-    for query_ref, out_ref in zip(refs[:count], refs[count:]):
-        size = query_ref.shape[0]
-        levels = []
-        for start in range(0, size, blocks):
-            scores = lax.dot_general(
-                query_ref[start:start + blocks].reshape(HEAD, HEAD),
-                key,
-                (((1,), (1,)), ((), ())),
-                preferred_element_type=jnp.float32,
+    size = query_ref.shape[0]
+    levels = []
+    for start in range(0, size, blocks):
+        query = query_ref[start:start + blocks].reshape(HEAD, HEAD)
+        scores = [
+            lax.dot_general(query, key, (((1,), (1,)), ((), ())), preferred_element_type=jnp.float32)
+            for key in keys
+        ]
+        top = jnp.max(jnp.maximum(scores[0], scores[1]), axis=1, keepdims=True)
+        result = jnp.zeros((HEAD, 2 * HEAD), jnp.float32)
+        for score, wide in zip(scores, wides):
+            weights = jnp.exp2((score - top) * (SCALE * LOG2E))
+            result = result + jnp.dot(
+                weights.astype(jnp.bfloat16), wide, preferred_element_type=jnp.float32
             )
-            top = jnp.max(scores, axis=1, keepdims=True)
-            weights = jnp.exp2((scores - top) * (SCALE * LOG2E))
-            result = jnp.dot(weights.astype(jnp.bfloat16), wide, preferred_element_type=jnp.float32)
-            total = result[:, HEAD:]
-            out_ref[start:start + blocks] = (
-                (result[:, :HEAD] / total).astype(out_ref.dtype).reshape(blocks, ROWS, HEAD)
-            )
-            levels.append(to_lanes(top * SCALE + jnp.log(total), eye))
-        levels = jnp.concatenate(levels, axis=0)
-        pieces = list(pieces_of(levels))
-        spare = ROWS - 3 * levels.shape[0]
-        if spare:
-            pieces.append(jnp.zeros((spare, HEAD), jnp.float32))
-        out_ref[size] = jnp.concatenate(pieces, axis=0).astype(out_ref.dtype)
-
-
-def blend_kernel(sources, out_ref):
+        total = result[:, HEAD:]
+        out_ref[start:start + blocks] = (
+            (result[:, :HEAD] / total).astype(out_ref.dtype).reshape(blocks, ROWS, HEAD)
+        )
+        levels.append(to_lanes(top * SCALE + jnp.log(total), eye))
+    levels = jnp.concatenate(levels, axis=0)
+    pieces = list(pieces_of(levels))
+    spare = ROWS - 3 * levels.shape[0]
+    if spare:
+        pieces.append(jnp.zeros((spare, HEAD), jnp.float32))
+    out_ref[size] = jnp.concatenate(pieces, axis=0).astype(out_ref.dtype)
+
+
+def blend_kernel(*refs):
+    sources, outs = refs[:-2], refs[-2:]
+    size, rows = sources[0].shape[0] - 1, sources[0].shape[1]
     eye = diagonal(HEAD)
     blocks = HEAD // ROWS
-    kvs = (out_ref.shape[1] - STATS) // ROWS
+    groups, kvs = size // blocks, rows // ROWS
     lane = iota((HEAD, HEAD), 1)
-    for start in range(0, out_ref.shape[0], blocks):
+    tables = [ref[size].astype(jnp.float32) for ref in sources]
+    for group in range(groups):
+        out_ref = outs[group * 2 // groups]
+        here = slice(group * blocks, (group + 1) * blocks)
+        start = group % (groups // 2) * blocks
+        there = slice(start, start + blocks)
         stats = jnp.zeros((HEAD, HEAD), jnp.float32)
         for kv in range(kvs):
-            parts = []
-            for refs in sources:
-                offset = start
-                for ref in refs:
-                    size = ref.shape[0] - 1
-                    if offset < size:
-                        break
-                    offset -= size
-                groups = size // blocks
-                table = ref[size, kv * ROWS:(kv + 1) * ROWS].astype(jnp.float32)
-                at = offset // blocks
-                level = table[at:at + 1] + table[groups + at:groups + at + 1]
-                level = level + table[2 * groups + at:2 * groups + at + 1]
-                mean = ref[offset:offset + blocks, kv * ROWS:(kv + 1) * ROWS].reshape(HEAD, HEAD)
-                parts.append((level, mean))
-            top = parts[0][0]
-            for level, _ in parts[1:]:
-                top = jnp.maximum(top, level)
-            weights = [jnp.exp(level - top) for level, _ in parts]
+            at = kv * ROWS + group
+            levels = [
+                table[at:at + 1]
+                + table[at + groups:at + groups + 1]
+                + table[at + 2 * groups:at + 2 * groups + 1]
+                for table in tables
+            ]
+            top = functools.reduce(jnp.maximum, levels)
+            weights = [jnp.exp(level - top) for level in levels]
             total = sum(weights)
             mixed = jnp.zeros((HEAD, HEAD), jnp.float32)
-            for weight, (_, mean) in zip(weights, parts):
-                mixed = mixed + mean.astype(jnp.float32) * to_column(weight / total, eye)
-            out_ref[start:start + blocks, kv * ROWS:(kv + 1) * ROWS] = mixed.astype(
-                out_ref.dtype
-            ).reshape(blocks, ROWS, HEAD)
+            for weight, ref in zip(weights, sources):
+                mean = ref[here, kv * ROWS:(kv + 1) * ROWS].reshape(HEAD, HEAD).astype(jnp.float32)
+                mixed = mixed + mean * to_column(weight / total, eye)
+            out_ref[there, kv * ROWS:(kv + 1) * ROWS] = mixed.astype(out_ref.dtype).reshape(
+                blocks, ROWS, HEAD
+            )
             column = to_column(top + jnp.log(total), eye)
             for index, piece in enumerate(pieces_of(column)):
                 stats = jnp.where(lane == kv * 3 + index, piece, stats)
-        out_ref[start:start + blocks, kvs * ROWS:] = stats.astype(out_ref.dtype).reshape(
-            blocks, STATS, HEAD
-        )
+        out_ref[there, rows:] = stats.astype(out_ref.dtype).reshape(blocks, STATS, HEAD)
 
 
 def tail_kernel(queries_ref, suffix_ref, length_ref, out_ref, max_ref, total_ref):
@@ -232,52 +231,36 @@
     )(owners, queries)
 
 
-def attend(chunks, prefix_kv):
-    tokens = prefix_kv.shape[2]
-    kvs = prefix_kv.shape[3] // HEAD
-    rows = sum(chunk.shape[0] * chunk.shape[1] for chunk in chunks)
-    return pl.pallas_call(
-        functools.partial(attend_kernel, len(chunks)),
+def attend(query, prefix_kv, far_kv):
+    tokens, kvs = prefix_kv.shape[2], prefix_kv.shape[3] // HEAD
+    size, rows, width = query.shape
+    key = pl.BlockSpec((1, 1, tokens, HEAD), lambda k: (0, 0, 0, k))
+    value = pl.BlockSpec((1, 1, tokens, HEAD), lambda k: (0, 1, 0, k))
+    return pl.pallas_call(
+        attend_kernel,
         grid=(kvs,),
-        in_specs=[
-            pl.BlockSpec((1, 1, tokens, HEAD), lambda k: (0, 0, 0, k)),
-            pl.BlockSpec((1, 1, tokens, HEAD), lambda k: (0, 1, 0, k)),
-        ]
-        + [pl.BlockSpec((chunk.shape[0], ROWS, HEAD), lambda k: (0, k, 0)) for chunk in chunks],
-        out_specs=[
-            pl.BlockSpec((chunk.shape[0] + 1, ROWS, HEAD), lambda k: (0, k, 0)) for chunk in chunks
-        ],
-        out_shape=[
-            jax.ShapeDtypeStruct((chunk.shape[0] + 1,) + chunk.shape[1:], chunk.dtype)
-            for chunk in chunks
-        ],
+        in_specs=[key, value, key, value, pl.BlockSpec((size, ROWS, width), lambda k: (0, k, 0))],
+        out_specs=pl.BlockSpec((size + 1, ROWS, width), lambda k: (0, k, 0)),
+        out_shape=jax.ShapeDtypeStruct((size + 1, rows, width), query.dtype),
         compiler_params=params(),
         cost_estimate=pl.CostEstimate(
-            flops=8 * rows * tokens * HEAD, bytes_accessed=rows * HEAD * 4, transcendentals=rows * tokens
+            flops=12 * size * rows * tokens * HEAD,
+            bytes_accessed=size * rows * HEAD * 4,
+            transcendentals=2 * size * rows * tokens,
         ),
         name="attend",
-    )(prefix_kv, prefix_kv, *chunks)
+    )(prefix_kv, prefix_kv, far_kv, far_kv, query)
 
 
 def blend(sources):
-    flat = [part for parts in sources for part in parts]
-    sizes = [len(parts) for parts in sources]
-
-    def kernel(*refs):
-        grouped, at = [], 0
-        for size in sizes:
-            grouped.append(refs[at:at + size])
-            at += size
-        blend_kernel(grouped, refs[-1])
-
-    blocks = sum(part.shape[0] - 1 for part in sources[0])
-    rows = flat[0].shape[1]
-    return pl.pallas_call(
-        kernel,
-        out_shape=jax.ShapeDtypeStruct((blocks, rows + STATS, HEAD), flat[0].dtype),
+    size, rows, width = sources[0].shape
+    shape = jax.ShapeDtypeStruct(((size - 1) // 2, rows + STATS, width), sources[0].dtype)
+    return pl.pallas_call(
+        blend_kernel,
+        out_shape=[shape, shape],
         compiler_params=params(),
         name="blend",
-    )(*flat)
+    )(*sources)
 
 
 def tail_attend(queries, suffix_kv, suffix_len):
@@ -300,41 +283,57 @@
     )(owners, back, tail, top, total)
 
 
-def shift(array, by):
-    size = lax.axis_size("y")
-    return lax.ppermute(array, "y", [(i, (i + by) % size) for i in range(size)])
+def send(array, step):
+    ring, cores = lax.axis_size("y"), lax.axis_size("tp")
+    pairs = []
+    for at in range(ring):
+        for core in range(cores):
+            to = (at + (step if core == 0 else -step)) % ring
+            pairs.append((at * cores + core, to * cores + core))
+    return lax.ppermute(array, ("y", "tp"), pairs)
+
+
+def swap(array):
+    ring, cores = lax.axis_size("y"), lax.axis_size("tp")
+    pairs = []
+    for at in range(ring):
+        for core in range(cores):
+            to = (at + (1 if at % 2 == core % 2 else -1)) % ring
+            pairs.append((at * cores + core, to * cores + core))
+    return lax.ppermute(array, ("y", "tp"), pairs)
 
 
 def per_device(queries, prefix_kv, suffix_kv, prefix_map, suffix_len):
     owner_count = lax.axis_size("prefix")
     ring = lax.axis_size("y")
     plane = ("prefix", "zh")
+    odd = lax.axis_index("y") % 2
+    far_kv = swap(prefix_kv)
     buckets = place(prefix_map, queries, owner_count)
     buckets = buckets.reshape((owner_count * Z_HALVES,) + buckets.shape[2:])
     mine = lax.all_to_all(buckets, plane, split_axis=0, concat_axis=0, tiled=True)
+    mine, far_kv = lax.optimization_barrier((mine, far_kv))
     half = mine.shape[0] // 2
-    from_left, from_right = mine, mine
+    kept = lax.dynamic_slice_in_dim(mine, odd * half, half, 0)
+    given = swap(lax.dynamic_slice_in_dim(mine, (1 - odd) * half, half, 0))
+    chunk = jnp.concatenate([kept, given], axis=0)
     sources = []
-    steps = ring // 2
-    for step in range(1, steps + 1):
-        if step < steps:
-            next_left, next_right = shift(from_left, 1), shift(from_right, -1)
-        else:
-            next_left, next_right = shift(from_left[:half], 1), shift(from_right[half:], -1)
-        if step == 1:
-            sources.append(attend([mine], prefix_kv))
-        from_left, from_right = next_left, next_right
-        to_left, to_right = attend([from_left, from_right], prefix_kv)
-        if step < steps:
-            sources.append([shift(to_left, -step)])
-            sources.append([shift(to_right, step)])
-        else:
-            sources.append([shift(to_left, -step), shift(to_right, step)])
-    tail, tail_max, tail_total = tail_attend(queries, suffix_kv, suffix_len)
-    blended = blend(sources)
+    for step in range(ring // 2):
+        following = send(chunk, 2) if step < ring // 2 - 1 else None
+        partial = attend(chunk, prefix_kv, far_kv)
+        sources.append(send(partial, -2 * step) if step else partial)
+        if step < ring // 2 - 1:
+            chunk, _ = lax.optimization_barrier((following, partial))
+    tails = tail_attend(queries, suffix_kv, suffix_len)
+    kept, given = blend(sources)
+    given, tails = lax.optimization_barrier((given, tails))
+    given = swap(given)
+    blended = jnp.where(
+        odd == 0, jnp.concatenate([kept, given], axis=0), jnp.concatenate([given, kept], axis=0)
+    )
     back = lax.all_to_all(blended, plane, split_axis=0, concat_axis=0, tiled=True)
     back = back.reshape((owner_count, Z_HALVES) + back.shape[1:])
-    attended = merge(prefix_map, back, tail, tail_max, tail_total, queries.shape, queries.dtype)
+    attended = merge(prefix_map, back, *tails, queries.shape, queries.dtype)
     return lax.all_to_all(attended, "tp", split_axis=0, concat_axis=1, tiled=True)
 
 

time: 153 us -> 140 us (0.915)
  the two profiles are of different devices: /device:TPU:81 before, /device:TPU:1 now
where the time goes in v1:
time: 140 us
  starting transfers between devices  44.4 us (32%)
  waiting for transfers between devices  42.4 us (30%)
  blocking collectives  31 us (22%)
  Pallas kernels  19.4 us (14%)
  local copies, waits for them, and re-layouts  2.24 us (2%)
    ppermute x6, starting transfers between devices, send(): return lax.ppermute(array, ('y', 'tp'), pairs)  21.8 us
    ppermute x6, waiting for transfers between devices, send(): return lax.ppermute(array, ('y', 'tp'), pairs)  20.2 us
    all_to_all x1, blocking collectives, per_device(): lax.all_to_all(blended, plane, split_axis=0, concat_axis=0, tiled=True)  17.9 us
    pallas_call x4, Pallas kernels, attend(): pl.pallas_call(attend_kernel, grid=(kvs,), in_specs=[key, value, key, val...  16.1 us
    all_to_all x1, blocking collectives, per_device(): lax.all_to_all(attended, 'tp', split_axis=0, concat_axis=1, tiled=True)  13.1 us
    all_to_all x1, starting transfers between devices, per_device(): lax.all_to_all(buckets, plane, split_axis=0, concat_axis=0, tiled=True)  12.9 us
    all_to_all x1, waiting for transfers between devices, per_device(): lax.all_to_all(buckets, plane, split_axis=0, concat_axis=0, tiled=True)  11.5 us
    ppermute x3, waiting for transfers between devices, swap(): return lax.ppermute(array, ('y', 'tp'), pairs)  10.7 us
  transfers between devices with their start and end apart: 10, of which 7 were waited for; matrix products, arithmetic and copies ran while one was open for 1% of the time, Pallas kernels for 13%

profile of v1, /device:TPU:1, one launch (start us, length us, event | category | flops | bytes accessed | tf_op | source)
XLA Modules:
  0.0 139.8 jit_solution(12540923868745256294)
XLA Ops:
  0.0 5.9 %collective-permute-start = (bf16[1,2,1024,256]{3,2,1,0:T(8,128)(2,1)}, bf16[1,2,1024,256]{3,2,1,0:T(8,128)(2,1)S(1)}, u32[]{:S(2)}, u32[]{:S(2)}) collective-permute-start(bf16[1,2,1024,256]{3,2,1,0:T(8,128)(2,1)} %value_ref.7), channel_id=1, source_target_pairs={{0,2},{1,15},{2,0},{3,5},{4,6},{5,3},{6,4},{7,9},{8,10},{9,7},{10,... | collective-permute-start | bytes 3145736 | tf_op jit(solution)/shard_map/ppermute | solution.py:303
  5.9 0.7 copy.7.owners_ref
  6.7 0.0 copy-start.1
  6.7 0.8 copy-done.1
  7.5 0.0 copy-start.4
  7.5 1.1 place.1
  8.6 12.9 %all-to-all-start = ((bf16[32,32,128]{2,1,0:T(8,128)(2,1)}), bf16[32,32,128]{2,1,0:T(8,128)(2,1)S(1)}, u32[]{:S(2)}, u32[]{:S(2)}) async-start(bf16[32,32,128]{2,1,0:T(8,128)(2,1)} %bitcast), calls=%async_computation | async-start | bytes 524288 | tf_op jit(solution)/shard_map/all_to_all | solution.py:314
  21.5 11.5 %all-to-all-done = bf16[32,32,128]{2,1,0:T(8,128)(2,1)S(1)} async-done(((bf16[32,32,128]{2,1,0:T(8,128)(2,1)}), bf16[32,32,128]{2,1,0:T(8,128)(2,1)S(1)}, u32[]{:S(2)}, u32[]{:S(2)}) %all-to-all-start) | async-done | bytes 262176 | tf_op jit(solution)/shard_map/all_to_all | solution.py:314
  33.1 0.0 collective-permute-done.far_key_ref.far_value_ref
  33.1 1.9 %collective-permute-start.1 = (bf16[16,32,128]{2,1,0:T(8,128)(2,1)S(1)}, bf16[16,32,128]{2,1,0:T(8,128)(2,1)S(1)}, u32[]{:S(2)}, u32[]{:S(2)}) collective-permute-start(bf16[16,32,128]{2,1,0:T(8,128)(2,1)S(1)} %get-tuple-element.34), channel_id=1, source_target_pairs={{0,2},{1,15},{2,0},{3,5},{4,6},{5,3},{6,4},{7,9},{8,10},{9,7},{10,... | collective-permute-start | bytes 393224 | tf_op jit(solution)/shard_map/ppermute | solution.py:303
  35.0 5.0 %collective-permute-done.1 = bf16[16,32,128]{2,1,0:T(8,128)(2,1)S(1)} collective-permute-done((bf16[16,32,128]{2,1,0:T(8,128)(2,1)S(1)}, bf16[16,32,128]{2,1,0:T(8,128)(2,1)S(1)}, u32[]{:S(2)}, u32[]{:S(2)}) %collective-permute-start.1) | collective-permute-done | bytes 131104 | tf_op jit(solution)/shard_map/ppermute | solution.py:303
  40.0 1.9 %collective-permute-start.2 = (bf16[32,32,128]{2,1,0:T(8,128)(2,1)S(1)}, bf16[32,32,128]{2,1,0:T(8,128)(2,1)S(1)}, u32[]{:S(2)}, u32[]{:S(2)}) collective-permute-start(bf16[32,32,128]{2,1,0:T(8,128)(2,1)S(1)} %pad_maximum_fusion.query_ref), channel_id=1, source_target_pairs={{0,4},{1,13},{2,6},{3,15},{4,8},{5,1},{6,10},{7,3},{8,12},{9,5},{1... | collective-permute-start | bytes 786440 | tf_op jit(solution)/shard_map/ppermute | solution.py:293
  42.0 0.0 copy-done.4
  42.0 4.0 %attend.4.refs_0_ = bf16[33,32,128]{2,1,0:T(8,128)(2,1)S(1)} custom-call(bf16[1,2,1024,256]{3,2,1,0:T(8,128)(2,1)S(1)} %copy-done.4, bf16[1,2,1024,256]{3,2,1,0:T(8,128)(2,1)S(1)} %copy-done.4, bf16[1,2,1024,256]{3,2,1,0:T(8,128)(2,1)S(1)} %collective-permute-done.far_key_ref.far_value_ref, ...), custom_call_target="tpu_custom_call" | custom-call | flops 1610612736 | bytes 524288 | tf_op jit(solution)/shard_map/attend/pallas_call | solution.py:239
  46.0 2.5 %collective-permute-done.2.query_ref = bf16[32,32,128]{2,1,0:T(8,128)(2,1)S(1)} collective-permute-done((bf16[32,32,128]{2,1,0:T(8,128)(2,1)S(1)}, bf16[32,32,128]{2,1,0:T(8,128)(2,1)S(1)}, u32[]{:S(2)}, u32[]{:S(2)}) %collective-permute-start.2) | collective-permute-done | bytes 262176 | tf_op jit(solution)/shard_map/ppermute | solution.py:293
  48.5 3.9 %collective-permute-start.4 = (bf16[32,32,128]{2,1,0:T(8,128)(2,1)S(1)}, bf16[32,32,128]{2,1,0:T(8,128)(2,1)S(1)}, u32[]{:S(2)}, u32[]{:S(2)}) collective-permute-start(bf16[32,32,128]{2,1,0:T(8,128)(2,1)S(1)} %collective-permute-done.2.query_ref), channel_id=1, source_target_pairs={{0,4},{1,13},{2,6},{3,15},{4,8},{5,1},{6,10},{7,3},{8,12},{9,5},{1... | collective-permute-start | bytes 786440 | tf_op jit(solution)/shard_map/ppermute | solution.py:293
  52.4 4.0 %attend.5 = bf16[33,32,128]{2,1,0:T(8,128)(2,1)S(1)} custom-call(bf16[1,2,1024,256]{3,2,1,0:T(8,128)(2,1)S(1)} %copy-done.4, bf16[1,2,1024,256]{3,2,1,0:T(8,128)(2,1)S(1)} %copy-done.4, bf16[1,2,1024,256]{3,2,1,0:T(8,128)(2,1)S(1)} %collective-permute-done.far_key_ref.far_value_ref, ...), custom_call_target="tpu_custom_call" | custom-call | flops 1610612736 | bytes 524288 | tf_op jit(solution)/shard_map/attend/pallas_call | solution.py:239
  56.4 0.1 collective-permute-done.4.query_ref
  56.5 5.2 %collective-permute-start.6 = (bf16[32,32,128]{2,1,0:T(8,128)(2,1)S(1)}, bf16[32,32,128]{2,1,0:T(8,128)(2,1)S(1)}, u32[]{:S(2)}, u32[]{:S(2)}) collective-permute-start(bf16[32,32,128]{2,1,0:T(8,128)(2,1)S(1)} %collective-permute-done.4.query_ref), channel_id=1, source_target_pairs={{0,4},{1,13},{2,6},{3,15},{4,8},{5,1},{6,10},{7,3},{8,12},{9,5},{1... | collective-permute-start | bytes 786440 | tf_op jit(solution)/shard_map/ppermute | solution.py:293
  61.7 1.9 %collective-permute-start.3 = (bf16[33,32,128]{2,1,0:T(8,128)(2,1)S(1)}, bf16[33,32,128]{2,1,0:T(8,128)(2,1)S(1)}, u32[]{:S(2)}, u32[]{:S(2)}) collective-permute-start(bf16[33,32,128]{2,1,0:T(8,128)(2,1)S(1)} %attend.5), channel_id=1, source_target_pairs={{0,12},{1,5},{2,14},{3,7},{4,0},{5,9},{6,2},{7,11},{8,4},{9,13},{1... | collective-permute-start | bytes 811016 | tf_op jit(solution)/shard_map/ppermute | solution.py:293
  63.7 4.0 %attend.6 = bf16[33,32,128]{2,1,0:T(8,128)(2,1)S(1)} custom-call(bf16[1,2,1024,256]{3,2,1,0:T(8,128)(2,1)S(1)} %copy-done.4, bf16[1,2,1024,256]{3,2,1,0:T(8,128)(2,1)S(1)} %copy-done.4, bf16[1,2,1024,256]{3,2,1,0:T(8,128)(2,1)S(1)} %collective-permute-done.far_key_ref.far_value_ref, ...), custom_call_target="tpu_custom_call" | custom-call | flops 1610612736 | bytes 524288 | tf_op jit(solution)/shard_map/attend/pallas_call | solution.py:239
  67.7 0.0 copy-start
  67.7 0.0 copy-start.2
  67.7 0.0 copy-start.3
  67.7 4.7 %collective-permute-start.5 = (bf16[33,32,128]{2,1,0:T(8,128)(2,1)S(1)}, bf16[33,32,128]{2,1,0:T(8,128)(2,1)S(1)}, u32[]{:S(2)}, u32[]{:S(2)}) collective-permute-start(bf16[33,32,128]{2,1,0:T(8,128)(2,1)S(1)} %attend.6), channel_id=1, source_target_pairs={{0,8},{1,9},{2,10},{3,11},{4,12},{5,13},{6,14},{7,15},{8,0},{9,1},... | collective-permute-start | bytes 811016 | tf_op jit(solution)/shard_map/ppermute | solution.py:293
  72.4 0.0 collective-permute-done.6.query_ref
  72.5 4.0 %attend.7 = bf16[33,32,128]{2,1,0:T(8,128)(2,1)S(1)} custom-call(bf16[1,2,1024,256]{3,2,1,0:T(8,128)(2,1)S(1)} %copy-done.4, bf16[1,2,1024,256]{3,2,1,0:T(8,128)(2,1)S(1)} %copy-done.4, bf16[1,2,1024,256]{3,2,1,0:T(8,128)(2,1)S(1)} %collective-permute-done.far_key_ref.far_value_ref, ...), custom_call_target="tpu_custom_call" | custom-call | flops 1610612736 | bytes 524288 | tf_op jit(solution)/shard_map/attend/pallas_call | solution.py:239
  76.5 4.1 %collective-permute-start.7 = (bf16[33,32,128]{2,1,0:T(8,128)(2,1)S(1)}, bf16[33,32,128]{2,1,0:T(8,128)(2,1)S(1)}, u32[]{:S(2)}, u32[]{:S(2)}) collective-permute-start(bf16[33,32,128]{2,1,0:T(8,128)(2,1)S(1)} %attend.7), channel_id=1, source_target_pairs={{0,4},{1,13},{2,6},{3,15},{4,8},{5,1},{6,10},{7,3},{8,12},{9,5},{1... | collective-permute-start | bytes 811016 | tf_op jit(solution)/shard_map/ppermute | solution.py:293
  80.5 0.0 copy-done
  80.6 0.0 copy-done.2
  80.6 0.0 copy-done.3
  80.6 0.8 tail.1
  81.4 0.0 collective-permute-done.3.refs_1_
  81.4 4.3 %collective-permute-done.5.refs_2_ = bf16[33,32,128]{2,1,0:T(8,128)(2,1)S(1)} collective-permute-done((bf16[33,32,128]{2,1,0:T(8,128)(2,1)S(1)}, bf16[33,32,128]{2,1,0:T(8,128)(2,1)S(1)}, u32[]{:S(2)}, u32[]{:S(2)}) %collective-permute-start.5) | collective-permute-done | bytes 270368 | tf_op jit(solution)/shard_map/ppermute | solution.py:293
  85.7 13.4 %collective-permute-done.7.refs_3_ = bf16[33,32,128]{2,1,0:T(8,128)(2,1)S(1)} collective-permute-done((bf16[33,32,128]{2,1,0:T(8,128)(2,1)S(1)}, bf16[33,32,128]{2,1,0:T(8,128)(2,1)S(1)}, u32[]{:S(2)}, u32[]{:S(2)}) %collective-permute-start.7) | collective-permute-done | bytes 270368 | tf_op jit(solution)/shard_map/ppermute | solution.py:293
  99.1 0.8 blend.1
  99.9 1.9 %collective-permute-start.8 = (bf16[16,48,128]{2,1,0:T(8,128)(2,1)S(1)}, bf16[16,48,128]{2,1,0:T(8,128)(2,1)S(1)}, u32[]{:S(2)}, u32[]{:S(2)}) collective-permute-start(bf16[16,48,128]{2,1,0:T(8,128)(2,1)S(1)} %get-tuple-element.29), channel_id=1, source_target_pairs={{0,2},{1,15},{2,0},{3,5},{4,6},{5,3},{6,4},{7,9},{8,10},{9,7},{10,... | collective-permute-start | bytes 589832 | tf_op jit(solution)/shard_map/ppermute | solution.py:303
  101.9 5.7 %collective-permute-done.8 = bf16[16,48,128]{2,1,0:T(8,128)(2,1)S(1)} collective-permute-done((bf16[16,48,128]{2,1,0:T(8,128)(2,1)S(1)}, bf16[16,48,128]{2,1,0:T(8,128)(2,1)S(1)}, u32[]{:S(2)}, u32[]{:S(2)}) %collective-permute-start.8) | collective-permute-done | bytes 196640 | tf_op jit(solution)/shard_map/ppermute | solution.py:303
  107.6 17.9 %all_to_all.29 = bf16[32,48,128]{2,1,0:T(8,128)(2,1)S(1)} all-to-all(bf16[32,48,128]{2,1,0:T(8,128)(2,1)S(1)} %maximum_select_fusion), channel_id=1, replica_groups=mesh['prefix'=16,'zh'=2,'y'=8,'tp'=2] {'prefix','zh'}, dimensions={0} | all-to-all | bytes 786432 | tf_op jit(solution)/shard_map/all_to_all | solution.py:334
  125.5 0.6 merge.1
  126.1 13.1 %all_to_all.30 = bf16[2,8,2048]{2,1,0:T(8,128)(2,1)S(1)} all-to-all(bf16[2,8,2048]{2,1,0:T(8,128)(2,1)S(1)} %bitcast.7), channel_id=1, replica_groups=mesh['prefix'=16,'zh'=2,'y'=8,'tp'=2] {'tp'}, dimensions={0} | all-to-all | bytes 131072 | tf_op jit(solution)/shard_map/all_to_all | solution.py:337
  139.2 0.6 copy.9
  (3 shorter events, 0.1 us)
Async XLA Ops:
  0.0 33.1 %collective-permute-start = (bf16[1,2,1024,256]{3,2,1,0:T(8,128)(2,1)}, bf16[1,2,1024,256]{3,2,1,0:T(8,128)(2,1)S(1)}, u32[]{:S(2)}, u32[]{:S(2)}) collective-permute-start(bf16[1,2,1024,256]{3,2,1,0:T(8,128)(2,1)} %value_ref.7), channel_id=1, source_target_pairs={{0,2},{1,15},{2,0},{3,5},{4,6},{5,3},{6,4},{7,9},{8,10},{9,7},{10,... | collective-permute-start | bytes 3145736 | tf_op jit(solution)/shard_map/ppermute | solution.py:303
  6.7 0.8 copy-start.1
  7.5 34.5 %copy-start.4 = (bf16[1,2,1024,256]{3,2,1,0:T(8,128)(2,1)S(1)}, bf16[1,2,1024,256]{3,2,1,0:T(8,128)(2,1)}, u32[]{:S(2)}) copy-start(bf16[1,2,1024,256]{3,2,1,0:T(8,128)(2,1)} %value_ref.7) | copy-start | bytes 3145732
  8.6 24.4 %all-to-all-start = ((bf16[32,32,128]{2,1,0:T(8,128)(2,1)}), bf16[32,32,128]{2,1,0:T(8,128)(2,1)S(1)}, u32[]{:S(2)}, u32[]{:S(2)}) async-start(bf16[32,32,128]{2,1,0:T(8,128)(2,1)} %bitcast), calls=%async_computation | async-start | bytes 524288 | tf_op jit(solution)/shard_map/all_to_all | solution.py:314
  33.1 6.9 %collective-permute-start.1 = (bf16[16,32,128]{2,1,0:T(8,128)(2,1)S(1)}, bf16[16,32,128]{2,1,0:T(8,128)(2,1)S(1)}, u32[]{:S(2)}, u32[]{:S(2)}) collective-permute-start(bf16[16,32,128]{2,1,0:T(8,128)(2,1)S(1)} %get-tuple-element.34), channel_id=1, source_target_pairs={{0,2},{1,15},{2,0},{3,5},{4,6},{5,3},{6,4},{7,9},{8,10},{9,7},{10,... | collective-permute-start | bytes 393224 | tf_op jit(solution)/shard_map/ppermute | solution.py:303
  40.0 8.4 %collective-permute-start.2 = (bf16[32,32,128]{2,1,0:T(8,128)(2,1)S(1)}, bf16[32,32,128]{2,1,0:T(8,128)(2,1)S(1)}, u32[]{:S(2)}, u32[]{:S(2)}) collective-permute-start(bf16[32,32,128]{2,1,0:T(8,128)(2,1)S(1)} %pad_maximum_fusion.query_ref), channel_id=1, source_target_pairs={{0,4},{1,13},{2,6},{3,15},{4,8},{5,1},{6,10},{7,3},{8,12},{9,5},{1... | collective-permute-start | bytes 786440 | tf_op jit(solution)/shard_map/ppermute | solution.py:293
  48.5 8.0 %collective-permute-start.4 = (bf16[32,32,128]{2,1,0:T(8,128)(2,1)S(1)}, bf16[32,32,128]{2,1,0:T(8,128)(2,1)S(1)}, u32[]{:S(2)}, u32[]{:S(2)}) collective-permute-start(bf16[32,32,128]{2,1,0:T(8,128)(2,1)S(1)} %collective-permute-done.2.query_ref), channel_id=1, source_target_pairs={{0,4},{1,13},{2,6},{3,15},{4,8},{5,1},{6,10},{7,3},{8,12},{9,5},{1... | collective-permute-start | bytes 786440 | tf_op jit(solution)/shard_map/ppermute | solution.py:293
  56.5 16.0 %collective-permute-start.6 = (bf16[32,32,128]{2,1,0:T(8,128)(2,1)S(1)}, bf16[32,32,128]{2,1,0:T(8,128)(2,1)S(1)}, u32[]{:S(2)}, u32[]{:S(2)}) collective-permute-start(bf16[32,32,128]{2,1,0:T(8,128)(2,1)S(1)} %collective-permute-done.4.query_ref), channel_id=1, source_target_pairs={{0,4},{1,13},{2,6},{3,15},{4,8},{5,1},{6,10},{7,3},{8,12},{9,5},{1... | collective-permute-start | bytes 786440 | tf_op jit(solution)/shard_map/ppermute | solution.py:293
  61.7 19.7 %collective-permute-start.3 = (bf16[33,32,128]{2,1,0:T(8,128)(2,1)S(1)}, bf16[33,32,128]{2,1,0:T(8,128)(2,1)S(1)}, u32[]{:S(2)}, u32[]{:S(2)}) collective-permute-start(bf16[33,32,128]{2,1,0:T(8,128)(2,1)S(1)} %attend.5), channel_id=1, source_target_pairs={{0,12},{1,5},{2,14},{3,7},{4,0},{5,9},{6,2},{7,11},{8,4},{9,13},{1... | collective-permute-start | bytes 811016 | tf_op jit(solution)/shard_map/ppermute | solution.py:293
  67.7 12.9 %copy-start = (bf16[16,2,64,256]{3,2,1,0:T(8,128)(2,1)S(1)}, bf16[16,2,64,256]{3,2,1,0:T(8,128)(2,1)}, u32[]{:S(2)}) copy-start(bf16[16,2,64,256]{3,2,1,0:T(8,128)(2,1)} %suffix_ref.1) | copy-start | bytes 3145732
  67.7 12.9 %copy-start.2 = (bf16[16,2048]{1,0:T(8,128)(2,1)S(1)}, bf16[16,2048]{1,0:T(8,128)(2,1)}, u32[]{:S(2)}) copy-start(bf16[16,2048]{1,0:T(8,128)(2,1)} %queries_ref.3) | copy-start | bytes 196612
  67.7 12.9 %copy-start.3 = (s32[1,16]{1,0:T(1,128)S(1)}, s32[1,16]{1,0:T(1,128)}, u32[]{:S(2)}) copy-start(s32[1,16]{1,0:T(1,128)} %length_ref.1) | copy-start | bytes 196
  67.7 18.0 %collective-permute-start.5 = (bf16[33,32,128]{2,1,0:T(8,128)(2,1)S(1)}, bf16[33,32,128]{2,1,0:T(8,128)(2,1)S(1)}, u32[]{:S(2)}, u32[]{:S(2)}) collective-permute-start(bf16[33,32,128]{2,1,0:T(8,128)(2,1)S(1)} %attend.6), channel_id=1, source_target_pairs={{0,8},{1,9},{2,10},{3,11},{4,12},{5,13},{6,14},{7,15},{8,0},{9,1},... | collective-permute-start | bytes 811016 | tf_op jit(solution)/shard_map/ppermute | solution.py:293
  76.5 22.6 %collective-permute-start.7 = (bf16[33,32,128]{2,1,0:T(8,128)(2,1)S(1)}, bf16[33,32,128]{2,1,0:T(8,128)(2,1)S(1)}, u32[]{:S(2)}, u32[]{:S(2)}) collective-permute-start(bf16[33,32,128]{2,1,0:T(8,128)(2,1)S(1)} %attend.7), channel_id=1, source_target_pairs={{0,4},{1,13},{2,6},{3,15},{4,8},{5,1},{6,10},{7,3},{8,12},{9,5},{1... | collective-permute-start | bytes 811016 | tf_op jit(solution)/shard_map/ppermute | solution.py:293
  99.9 7.6 %collective-permute-start.8 = (bf16[16,48,128]{2,1,0:T(8,128)(2,1)S(1)}, bf16[16,48,128]{2,1,0:T(8,128)(2,1)S(1)}, u32[]{:S(2)}, u32[]{:S(2)}) collective-permute-start(bf16[16,48,128]{2,1,0:T(8,128)(2,1)S(1)} %get-tuple-element.29), channel_id=1, source_target_pairs={{0,2},{1,15},{2,0},{3,5},{4,6},{5,3},{6,4},{7,9},{8,10},{9,7},{10,... | collective-permute-start | bytes 589832 | tf_op jit(solution)/shard_map/ppermute | solution.py:303

commit v2 on v1

--- a/solution.py
+++ b/solution.py
@@ -16,6 +16,7 @@
 LOG2E = math.log2(math.e)
 STATS = 16
 Z_HALVES = 2
+CLASSES = 4
 VMEM_LIMIT = 48 * 1024 * 1024
 
 
@@ -77,76 +78,91 @@
         out_ref[:, half] = placed
 
 
-def attend_kernel(key_ref, value_ref, far_key_ref, far_value_ref, query_ref, out_ref):
-    keys = (key_ref[0, 0], far_key_ref[0, 0])
-    values = (value_ref[0, 0], far_value_ref[0, 0])
-    wides = [jnp.concatenate([value, jnp.ones_like(value)], axis=1) for value in values]
+def fan_kernel(mine_ref, out_ref):
+    size = mine_ref.shape[0] // 2
+    for target in range(out_ref.shape[0]):
+        kv, half = target // 2 % 2, target % 2
+        out_ref[target] = mine_ref[half * size:(half + 1) * size, kv * ROWS:(kv + 1) * ROWS]
+
+
+def attend_kernel(*refs):
+    held, query_ref, out_ref = refs[:-2], refs[-2], refs[-1]
+    keys = [ref[0] for ref in held]
+    wides = [jnp.concatenate([ref[1], jnp.ones_like(ref[1])], axis=1) for ref in held]
     eye = diagonal(HEAD)
     blocks = HEAD // ROWS
-    size = query_ref.shape[0]
-    levels = []
-    for start in range(0, size, blocks):
+    targets, size = out_ref.shape[0], out_ref.shape[1] - 1
+
+    def scores_of(start):
         query = query_ref[start:start + blocks].reshape(HEAD, HEAD)
-        scores = [
+        return [
             lax.dot_general(query, key, (((1,), (1,)), ((), ())), preferred_element_type=jnp.float32)
             for key in keys
         ]
-        top = jnp.max(jnp.maximum(scores[0], scores[1]), axis=1, keepdims=True)
-        result = jnp.zeros((HEAD, 2 * HEAD), jnp.float32)
-        for score, wide in zip(scores, wides):
-            weights = jnp.exp2((score - top) * (SCALE * LOG2E))
-            result = result + jnp.dot(
-                weights.astype(jnp.bfloat16), wide, preferred_element_type=jnp.float32
+
+    ahead = scores_of(0)
+    for target in range(targets):
+        levels = []
+        for start in range(0, size, blocks):
+            scores = ahead
+            following = target * size + start + blocks
+            if following < targets * size:
+                ahead = scores_of(following)
+            top = jnp.max(functools.reduce(jnp.maximum, scores), axis=1, keepdims=True)
+            result = jnp.zeros((HEAD, 2 * HEAD), jnp.float32)
+            for score, wide in zip(scores, wides):
+                weights = jnp.exp2((score - top) * (SCALE * LOG2E))
+                result = result + jnp.dot(
+                    weights.astype(jnp.bfloat16), wide, preferred_element_type=jnp.float32
+                )
+            total = result[:, HEAD:]
+            out_ref[target, start:start + blocks] = (
+                (result[:, :HEAD] / total).astype(out_ref.dtype).reshape(blocks, ROWS, HEAD)
             )
-        total = result[:, HEAD:]
-        out_ref[start:start + blocks] = (
-            (result[:, :HEAD] / total).astype(out_ref.dtype).reshape(blocks, ROWS, HEAD)
-        )
-        levels.append(to_lanes(top * SCALE + jnp.log(total), eye))
-    levels = jnp.concatenate(levels, axis=0)
-    pieces = list(pieces_of(levels))
-    spare = ROWS - 3 * levels.shape[0]
-    if spare:
-        pieces.append(jnp.zeros((spare, HEAD), jnp.float32))
-    out_ref[size] = jnp.concatenate(pieces, axis=0).astype(out_ref.dtype)
-
-
-def blend_kernel(*refs):
-    sources, outs = refs[:-2], refs[-2:]
-    size, rows = sources[0].shape[0] - 1, sources[0].shape[1]
+            levels.append(to_lanes(top * SCALE + jnp.log(total), eye))
+        levels = jnp.concatenate(levels, axis=0)
+        pieces = list(pieces_of(levels))
+        spare = ROWS - 3 * levels.shape[0]
+        if spare:
+            pieces.append(jnp.zeros((spare, HEAD), jnp.float32))
+        out_ref[target, size] = jnp.concatenate(pieces, axis=0).astype(out_ref.dtype)
+
+
+def blend_kernel(back_ref, out_ref):
+    ring, size = back_ref.shape[0], back_ref.shape[1] - 1
+    kvs = (out_ref.shape[1] - STATS) // ROWS
     eye = diagonal(HEAD)
     blocks = HEAD // ROWS
-    groups, kvs = size // blocks, rows // ROWS
+    groups = size // blocks
     lane = iota((HEAD, HEAD), 1)
-    tables = [ref[size].astype(jnp.float32) for ref in sources]
-    for group in range(groups):
-        out_ref = outs[group * 2 // groups]
-        here = slice(group * blocks, (group + 1) * blocks)
-        start = group % (groups // 2) * blocks
-        there = slice(start, start + blocks)
-        stats = jnp.zeros((HEAD, HEAD), jnp.float32)
-        for kv in range(kvs):
-            at = kv * ROWS + group
-            levels = [
-                table[at:at + 1]
-                + table[at + groups:at + groups + 1]
-                + table[at + 2 * groups:at + 2 * groups + 1]
-                for table in tables
-            ]
-            top = functools.reduce(jnp.maximum, levels)
-            weights = [jnp.exp(level - top) for level in levels]
-            total = sum(weights)
-            mixed = jnp.zeros((HEAD, HEAD), jnp.float32)
-            for weight, ref in zip(weights, sources):
-                mean = ref[here, kv * ROWS:(kv + 1) * ROWS].reshape(HEAD, HEAD).astype(jnp.float32)
-                mixed = mixed + mean * to_column(weight / total, eye)
-            out_ref[there, kv * ROWS:(kv + 1) * ROWS] = mixed.astype(out_ref.dtype).reshape(
-                blocks, ROWS, HEAD
-            )
-            column = to_column(top + jnp.log(total), eye)
-            for index, piece in enumerate(pieces_of(column)):
-                stats = jnp.where(lane == kv * 3 + index, piece, stats)
-        out_ref[there, rows:] = stats.astype(out_ref.dtype).reshape(blocks, STATS, HEAD)
+    table = back_ref[:, size].astype(jnp.float32)
+    for half in range(2):
+        for group in range(groups):
+            here = slice(group * blocks, (group + 1) * blocks)
+            there = slice(half * size + group * blocks, half * size + (group + 1) * blocks)
+            stats = jnp.zeros((HEAD, HEAD), jnp.float32)
+            for kv in range(kvs):
+                members = range(2 * kv + half, ring, CLASSES)
+                levels = [
+                    table[source, group:group + 1]
+                    + table[source, groups + group:groups + group + 1]
+                    + table[source, 2 * groups + group:2 * groups + group + 1]
+                    for source in members
+                ]
+                top = functools.reduce(jnp.maximum, levels)
+                weights = [jnp.exp(level - top) for level in levels]
+                total = sum(weights)
+                mixed = jnp.zeros((HEAD, HEAD), jnp.float32)
+                for weight, source in zip(weights, members):
+                    mean = back_ref[source, here].reshape(HEAD, HEAD).astype(jnp.float32)
+                    mixed = mixed + mean * to_column(weight / total, eye)
+                out_ref[there, kv * ROWS:(kv + 1) * ROWS] = mixed.astype(out_ref.dtype).reshape(
+                    blocks, ROWS, HEAD
+                )
+                column = to_column(top + jnp.log(total), eye)
+                for index, piece in enumerate(pieces_of(column)):
+                    stats = jnp.where(lane == kv * 3 + index, piece, stats)
+            out_ref[there, kvs * ROWS:] = stats.astype(out_ref.dtype).reshape(blocks, STATS, HEAD)
 
 
 def tail_kernel(queries_ref, suffix_ref, length_ref, out_ref, max_ref, total_ref):
@@ -231,36 +247,46 @@
     )(owners, queries)
 
 
-def attend(query, prefix_kv, far_kv):
-    tokens, kvs = prefix_kv.shape[2], prefix_kv.shape[3] // HEAD
-    size, rows, width = query.shape
-    key = pl.BlockSpec((1, 1, tokens, HEAD), lambda k: (0, 0, 0, k))
-    value = pl.BlockSpec((1, 1, tokens, HEAD), lambda k: (0, 1, 0, k))
+def fan(mine, ring):
+    shape = (ring, mine.shape[0] // 2, ROWS, HEAD)
+    return pl.pallas_call(
+        fan_kernel,
+        out_shape=jax.ShapeDtypeStruct(shape, mine.dtype),
+        compiler_params=params(),
+        name="fan",
+    )(mine)
+
+
+def attend(query, held):
+    tokens = sum(part.shape[1] for part in held)
+    ring, size, rows, width = query.shape
+    step = 2
+    whole = pl.BlockSpec(held[0].shape, lambda i: (0, 0, 0))
     return pl.pallas_call(
         attend_kernel,
-        grid=(kvs,),
-        in_specs=[key, value, key, value, pl.BlockSpec((size, ROWS, width), lambda k: (0, k, 0))],
-        out_specs=pl.BlockSpec((size + 1, ROWS, width), lambda k: (0, k, 0)),
-        out_shape=jax.ShapeDtypeStruct((size + 1, rows, width), query.dtype),
+        grid=(ring // step,),
+        in_specs=[whole] * len(held)
+        + [pl.BlockSpec((step * size, rows, width), lambda i: (i, 0, 0))],
+        out_specs=pl.BlockSpec((step, size + 1, rows, width), lambda i: (i, 0, 0, 0)),
+        out_shape=jax.ShapeDtypeStruct((ring, size + 1, rows, width), query.dtype),
         compiler_params=params(),
         cost_estimate=pl.CostEstimate(
-            flops=12 * size * rows * tokens * HEAD,
-            bytes_accessed=size * rows * HEAD * 4,
-            transcendentals=2 * size * rows * tokens,
+            flops=6 * ring * size * rows * tokens * HEAD,
+            bytes_accessed=ring * size * rows * HEAD * 4,
+            transcendentals=ring * size * rows * tokens,
         ),
         name="attend",
-    )(prefix_kv, prefix_kv, far_kv, far_kv, query)
-
-
-def blend(sources):
-    size, rows, width = sources[0].shape
-    shape = jax.ShapeDtypeStruct(((size - 1) // 2, rows + STATS, width), sources[0].dtype)
+    )(*held, query.reshape(ring * size, rows, width))
+
+
+def blend(back, kvs):
+    _, size, rows, width = back.shape
     return pl.pallas_call(
         blend_kernel,
-        out_shape=[shape, shape],
+        out_shape=jax.ShapeDtypeStruct((2 * (size - 1), kvs * rows + STATS, width), back.dtype),
         compiler_params=params(),
         name="blend",
-    )(*sources)
+    )(back)
 
 
 def tail_attend(queries, suffix_kv, suffix_len):
@@ -283,22 +309,14 @@
     )(owners, back, tail, top, total)
 
 
-def send(array, step):
+def share(array, flip):
     ring, cores = lax.axis_size("y"), lax.axis_size("tp")
     pairs = []
     for at in range(ring):
         for core in range(cores):
-            to = (at + (step if core == 0 else -step)) % ring
-            pairs.append((at * cores + core, to * cores + core))
-    return lax.ppermute(array, ("y", "tp"), pairs)
-
-
-def swap(array):
-    ring, cores = lax.axis_size("y"), lax.axis_size("tp")
-    pairs = []
-    for at in range(ring):
-        for core in range(cores):
-            to = (at + (1 if at % 2 == core % 2 else -1)) % ring
+            first = at - (at - 2 * core) % CLASSES
+            spots = [(first + i) % ring for i in range(CLASSES)]
+            to = next(spot for spot in spots if spot % CLASSES == (at % CLASSES) ^ flip)
             pairs.append((at * cores + core, to * cores + core))
     return lax.ppermute(array, ("y", "tp"), pairs)
 
@@ -307,30 +325,21 @@
     owner_count = lax.axis_size("prefix")
     ring = lax.axis_size("y")
     plane = ("prefix", "zh")
-    odd = lax.axis_index("y") % 2
-    far_kv = swap(prefix_kv)
+    kvs = queries.shape[1] // (HEAD * GROUP)
+    kv = lax.axis_index("y") // 2 % 2
+    own = lax.dynamic_slice_in_dim(prefix_kv[0], kv * HEAD, HEAD, 2)
+    other = lax.dynamic_slice_in_dim(prefix_kv[0], (1 - kv) * HEAD, HEAD, 2)
+    shared = [share(own, 1), share(other, 2), share(other, 3)]
     buckets = place(prefix_map, queries, owner_count)
     buckets = buckets.reshape((owner_count * Z_HALVES,) + buckets.shape[2:])
     mine = lax.all_to_all(buckets, plane, split_axis=0, concat_axis=0, tiled=True)
-    mine, far_kv = lax.optimization_barrier((mine, far_kv))
-    half = mine.shape[0] // 2
-    kept = lax.dynamic_slice_in_dim(mine, odd * half, half, 0)
-    given = swap(lax.dynamic_slice_in_dim(mine, (1 - odd) * half, half, 0))
-    chunk = jnp.concatenate([kept, given], axis=0)
-    sources = []
-    for step in range(ring // 2):
-        following = send(chunk, 2) if step < ring // 2 - 1 else None
-        partial = attend(chunk, prefix_kv, far_kv)
-        sources.append(send(partial, -2 * step) if step else partial)
-        if step < ring // 2 - 1:
-            chunk, _ = lax.optimization_barrier((following, partial))
+    sent = fan(mine, ring)
+    sent, shared = lax.optimization_barrier((sent, shared))
+    query = lax.all_to_all(sent, "y", split_axis=0, concat_axis=0, tiled=True)
+    partial = attend(query, [own] + shared)
+    back = lax.all_to_all(partial, "y", split_axis=0, concat_axis=0, tiled=True)
     tails = tail_attend(queries, suffix_kv, suffix_len)
-    kept, given = blend(sources)
-    given, tails = lax.optimization_barrier((given, tails))
-    given = swap(given)
-    blended = jnp.where(
-        odd == 0, jnp.concatenate([kept, given], axis=0), jnp.concatenate([given, kept], axis=0)
-    )
+    blended = blend(back, kvs)
     back = lax.all_to_all(blended, plane, split_axis=0, concat_axis=0, tiled=True)
     back = back.reshape((owner_count, Z_HALVES) + back.shape[1:])
     attended = merge(prefix_map, back, *tails, queries.shape, queries.dtype)

time: 140 us -> 127 us (0.907)
  blocking collectives: 31 us -> 76.2 us
  waiting for transfers between devices: 42.4 us -> 9.96 us
  starting transfers between devices: 44.4 us -> 24 us
  Pallas kernels: 19.4 us -> 14.3 us
    all_to_all x1 -> x3, blocking collectives: 17.9 us -> 67.4 us  [the longest x1 26.5 us: per_device(): query = lax.all_to_all(sent, 'y', split_axis=0, concat_axis=0, tiled=True)]
    ppermute x9 -> x3, waiting for transfers between devices: 30.9 us -> 0.01 us  [share(): return lax.ppermute(array, ('y', 'tp'), pairs)]
    ppermute x9 -> x3, starting transfers between devices: 31.5 us -> 10.9 us  [share(): return lax.ppermute(array, ('y', 'tp'), pairs)]
    pallas_call x5 -> x3, Pallas kernels: 16.9 us -> 12.4 us  [the longest x1 11.1 us: attend(): pl.pallas_call(attend_kernel, grid=(ring // step,), in_specs=[whole] * le...]
    all_to_all x1, blocking collectives: 13.1 us -> 8.8 us  [per_device(): lax.all_to_all(attended, 'tp', split_axis=0, concat_axis=1, tiled=True)]
    all_to_all x1, waiting for transfers between devices: 11.5 us -> 9.95 us  [per_device(): lax.all_to_all(blended, plane, split_axis=0, concat_axis=0, tiled=True)]
    unnamed x12 -> x10, local copies, waits for them, and re-layouts: 2.22 us -> 0.73 us
  transfers between devices with their start and end apart: 10 -> 4, of which waited for: 7 -> 1; matrix products, arithmetic and copies ran while one was open for 1% -> 0% of each run, Pallas kernels for 13% -> 1%
where the time goes in v2:
time: 127 us
  blocking collectives  76.2 us (60%)
  starting transfers between devices  24 us (19%)
  Pallas kernels  14.3 us (11%)
  waiting for transfers between devices  9.96 us (8%)
  local copies, waits for them, and re-layouts  2.03 us (2%)
    all_to_all x1, blocking collectives, per_device(): query = lax.all_to_all(sent, 'y', split_axis=0, concat_axis=0, tiled=True)  26.5 us
    all_to_all x1, blocking collectives, per_device(): lax.all_to_all(buckets, plane, split_axis=0, concat_axis=0, tiled=True)  22.8 us
    all_to_all x1, blocking collectives, per_device(): back = lax.all_to_all(partial, 'y', split_axis=0, concat_axis=0, tiled=True)  18.1 us
    all_to_all x1, starting transfers between devices, per_device(): lax.all_to_all(blended, plane, split_axis=0, concat_axis=0, tiled=True)  13.1 us
    pallas_call x1, Pallas kernels, attend(): pl.pallas_call(attend_kernel, grid=(ring // step,), in_specs=[whole] * le...  11.1 us
    ppermute x3, starting transfers between devices, share(): return lax.ppermute(array, ('y', 'tp'), pairs)  10.9 us
    all_to_all x1, waiting for transfers between devices, per_device(): lax.all_to_all(blended, plane, split_axis=0, concat_axis=0, tiled=True)  9.95 us
    all_to_all x1, blocking collectives, per_device(): lax.all_to_all(attended, 'tp', split_axis=0, concat_axis=1, tiled=True)  8.8 us
  transfers between devices with their start and end apart: 4, of which 1 were waited for; matrix products, arithmetic and copies ran while one was open for 0% of the time, Pallas kernels for 1%

profile of v2, /device:TPU:1, one launch (start us, length us, event | category | flops | bytes accessed | tf_op | source)
XLA Modules:
  0.0 126.5 jit_solution(12424504461002933061)
XLA Ops:
  0.0 0.0 copy-start.1
  0.0 1.3 %dynamic-slice_bitcast_fusion = (bf16[2,1024,128]{2,1,0:T(8,128)(2,1)S(1)}, bf16[2,1024,128]{2,1,0:T(8,128)(2,1)S(1)}) fusion(bf16[1,2,1024,256]{3,2,1,0:T(8,128)(2,1)} %param.6, s32[]{:T(128)S(6)} %select_n.20, s32[]{:T(128)S(6)} %select_n.19), kind=kLoop, calls=%fused_computation | loop fusion | bytes 2097160 | tf_op jit(solution)/shard_map/dynamic_slice | solution.py:331
  1.3 0.0 copy-start.3
  1.3 4.0 %collective-permute-start = (bf16[2,1024,128]{2,1,0:T(8,128)(2,1)S(1)}, bf16[2,1024,128]{2,1,0:T(8,128)(2,1)S(1)}, u32[]{:S(2)}, u32[]{:S(2)}) collective-permute-start(bf16[2,1024,128]{2,1,0:T(8,128)(2,1)S(1)} %get-tuple-element.20.refs_0_), channel_id=1, source_target_pairs={{0,2},{1,3},{2,0},{3,1},{4,6},{5,7},{6,4},{7,5},{8,10},{9,11},{10,... | collective-permute-start | bytes 1572872 | tf_op jit(solution)/shard_map/ppermute | solution.py:321
  5.4 5.0 %collective-permute-start.1 = (bf16[2,1024,128]{2,1,0:T(8,128)(2,1)S(1)}, bf16[2,1024,128]{2,1,0:T(8,128)(2,1)S(1)}, u32[]{:S(2)}, u32[]{:S(2)}) collective-permute-start(bf16[2,1024,128]{2,1,0:T(8,128)(2,1)S(1)} %get-tuple-element.19), channel_id=1, source_target_pairs={{0,4},{1,13},{2,6},{3,15},{4,0},{5,9},{6,2},{7,11},{8,12},{9,5},{1... | collective-permute-start | bytes 1572872 | tf_op jit(solution)/shard_map/ppermute | solution.py:321
  10.4 1.9 %collective-permute-start.2 = (bf16[2,1024,128]{2,1,0:T(8,128)(2,1)S(1)}, bf16[2,1024,128]{2,1,0:T(8,128)(2,1)S(1)}, u32[]{:S(2)}, u32[]{:S(2)}) collective-permute-start(bf16[2,1024,128]{2,1,0:T(8,128)(2,1)S(1)} %get-tuple-element.19), channel_id=1, source_target_pairs={{0,6},{1,15},{2,4},{3,13},{4,2},{5,11},{6,0},{7,9},{8,14},{9,7},{1... | collective-permute-start | bytes 1572872 | tf_op jit(solution)/shard_map/ppermute | solution.py:321
  12.3 0.0 copy-done.3
  12.3 0.1 copy.7.owners_ref
  12.4 0.0 copy-done.1
  12.4 0.4 place.1
  12.8 22.8 %all_to_all.39.mine_ref = bf16[32,32,128]{2,1,0:T(8,128)(2,1)S(1)} all-to-all(bf16[32,32,128]{2,1,0:T(8,128)(2,1)S(1)} %bitcast.12), channel_id=1, replica_groups=mesh['prefix'=16,'zh'=2,'y'=8,'tp'=2] {'prefix','zh'}, dimensions={0} | all-to-all | bytes 524288 | tf_op jit(solution)/shard_map/all_to_all | solution.py:335
  35.6 0.1 fan.1
  35.7 0.0 collective-permute-done.refs_1_
  35.7 0.0 collective-permute-done.1.refs_2_
  35.7 0.0 collective-permute-done.2.refs_3_
  35.7 26.5 %all_to_all.40 = bf16[8,16,16,128]{3,2,1,0:T(8,128)(2,1)S(1)} all-to-all(bf16[8,16,16,128]{3,2,1,0:T(8,128)(2,1)S(1)} %fan.1), channel_id=1, replica_groups=mesh['prefix'=16,'zh'=2,'y'=8,'tp'=2] {'y'}, dimensions={0} | all-to-all | bytes 1048576 | tf_op jit(solution)/shard_map/all_to_all | solution.py:338
  62.2 11.1 %attend.1 = bf16[8,17,16,128]{3,2,1,0:T(8,128)(2,1)S(1)} custom-call(bf16[2,1024,128]{2,1,0:T(8,128)(2,1)S(1)} %get-tuple-element.20.refs_0_, bf16[2,1024,128]{2,1,0:T(8,128)(2,1)S(1)} %collective-permute-done.refs_1_, bf16[2,1024,128]{2,1,0:T(8,128)(2,1)S(1)} %collective-permute-done.1.refs_2_, bf16[2,1024,128]{2,1,0:T(8,128)(2,1)S(1)} %collective-permute-done.2.refs_3_, ...), custom_call_target="tpu_custom_call" | custom-call | flops 6442450944 | bytes 1048576 | tf_op jit(solution)/shard_map/attend/pallas_call | solution.py:265
  73.3 18.1 %all_to_all.41.back_ref = bf16[8,17,16,128]{3,2,1,0:T(8,128)(2,1)S(1)} all-to-all(bf16[8,17,16,128]{3,2,1,0:T(8,128)(2,1)S(1)} %attend.1), channel_id=1, replica_groups=mesh['prefix'=16,'zh'=2,'y'=8,'tp'=2] {'y'}, dimensions={0} | all-to-all | bytes 1114112 | tf_op jit(solution)/shard_map/all_to_all | solution.py:340
  91.4 0.0 copy-start
  91.4 1.3 blend.1
  92.6 0.0 copy-start.2
  92.6 13.1 %all-to-all-start.3 = ((bf16[32,48,128]{2,1,0:T(8,128)(2,1)}), bf16[32,48,128]{2,1,0:T(8,128)(2,1)S(1)}, u32[]{:S(2)}, u32[]{:S(2)}) async-start(bf16[32,48,128]{2,1,0:T(8,128)(2,1)} %blend.1), calls=%async_computation.3 | async-start | bytes 786432 | tf_op jit(solution)/shard_map/all_to_all | solution.py:343
  105.7 0.0 copy-done
  105.7 0.0 copy-done.2
  105.7 0.8 tail.1
  106.5 9.9 %all-to-all-done.3 = bf16[32,48,128]{2,1,0:T(8,128)(2,1)S(1)} async-done(((bf16[32,48,128]{2,1,0:T(8,128)(2,1)}), bf16[32,48,128]{2,1,0:T(8,128)(2,1)S(1)}, u32[]{:S(2)}, u32[]{:S(2)}) %all-to-all-start.3) | async-done | bytes 393248 | tf_op jit(solution)/shard_map/all_to_all | solution.py:343
  116.5 0.6 merge.1
  117.1 8.8 %all_to_all.42 = bf16[2,8,2048]{2,1,0:T(8,128)(2,1)S(1)} all-to-all(bf16[2,8,2048]{2,1,0:T(8,128)(2,1)S(1)} %bitcast.14), channel_id=1, replica_groups=mesh['prefix'=16,'zh'=2,'y'=8,'tp'=2] {'tp'}, dimensions={0} | all-to-all | bytes 131072 | tf_op jit(solution)/shard_map/all_to_all | solution.py:346
  125.9 0.6 copy.9
Async XLA Ops:
  0.0 12.4 %copy-start.1 = (bf16[16,2048]{1,0:T(8,128)(2,1)S(1)}, bf16[16,2048]{1,0:T(8,128)(2,1)}, u32[]{:S(2)}) copy-start(bf16[16,2048]{1,0:T(8,128)(2,1)} %queries_ref.3) | copy-start | bytes 196612
  1.3 11.0 %copy-start.3 = (s32[16,1]{0,1:T(1,128)S(1)}, s32[16,1]{0,1:T(1,128)}, u32[]{:S(2)}) copy-start(s32[16,1]{0,1:T(1,128)} %param.8) | copy-start | bytes 196
  1.3 34.4 %collective-permute-start = (bf16[2,1024,128]{2,1,0:T(8,128)(2,1)S(1)}, bf16[2,1024,128]{2,1,0:T(8,128)(2,1)S(1)}, u32[]{:S(2)}, u32[]{:S(2)}) collective-permute-start(bf16[2,1024,128]{2,1,0:T(8,128)(2,1)S(1)} %get-tuple-element.20.refs_0_), channel_id=1, source_target_pairs={{0,2},{1,3},{2,0},{3,1},{4,6},{5,7},{6,4},{7,5},{8,10},{9,11},{10,... | collective-permute-start | bytes 1572872 | tf_op jit(solution)/shard_map/ppermute | solution.py:321
  5.4 30.3 %collective-permute-start.1 = (bf16[2,1024,128]{2,1,0:T(8,128)(2,1)S(1)}, bf16[2,1024,128]{2,1,0:T(8,128)(2,1)S(1)}, u32[]{:S(2)}, u32[]{:S(2)}) collective-permute-start(bf16[2,1024,128]{2,1,0:T(8,128)(2,1)S(1)} %get-tuple-element.19), channel_id=1, source_target_pairs={{0,4},{1,13},{2,6},{3,15},{4,0},{5,9},{6,2},{7,11},{8,12},{9,5},{1... | collective-permute-start | bytes 1572872 | tf_op jit(solution)/shard_map/ppermute | solution.py:321
  10.4 25.3 %collective-permute-start.2 = (bf16[2,1024,128]{2,1,0:T(8,128)(2,1)S(1)}, bf16[2,1024,128]{2,1,0:T(8,128)(2,1)S(1)}, u32[]{:S(2)}, u32[]{:S(2)}) collective-permute-start(bf16[2,1024,128]{2,1,0:T(8,128)(2,1)S(1)} %get-tuple-element.19), channel_id=1, source_target_pairs={{0,6},{1,15},{2,4},{3,13},{4,2},{5,11},{6,0},{7,9},{8,14},{9,7},{1... | collective-permute-start | bytes 1572872 | tf_op jit(solution)/shard_map/ppermute | solution.py:321
  91.4 14.3 %copy-start = (bf16[16,2,64,256]{3,2,1,0:T(8,128)(2,1)S(1)}, bf16[16,2,64,256]{3,2,1,0:T(8,128)(2,1)}, u32[]{:S(2)}) copy-start(bf16[16,2,64,256]{3,2,1,0:T(8,128)(2,1)} %suffix_ref.1) | copy-start | bytes 3145732
  92.6 13.1 %copy-start.2 = (s32[1,16]{1,0:T(1,128)S(1)}, s32[1,16]{1,0:T(1,128)}, u32[]{:S(2)}) copy-start(s32[1,16]{1,0:T(1,128)} %length_ref.1) | copy-start | bytes 196
  92.6 23.9 %all-to-all-start.3 = ((bf16[32,48,128]{2,1,0:T(8,128)(2,1)}), bf16[32,48,128]{2,1,0:T(8,128)(2,1)S(1)}, u32[]{:S(2)}, u32[]{:S(2)}) async-start(bf16[32,48,128]{2,1,0:T(8,128)(2,1)} %blend.1), calls=%async_computation.3 | async-start | bytes 786432 | tf_op jit(solution)/shard_map/all_to_all | solution.py:343

commit v3 on v2

--- a/solution.py
+++ b/solution.py
@@ -81,7 +81,7 @@
 def fan_kernel(mine_ref, out_ref):
     size = mine_ref.shape[0] // 2
     for target in range(out_ref.shape[0]):
-        kv, half = target // 2 % 2, target % 2
+        kv, half = target % 2, target // 2 % 2
         out_ref[target] = mine_ref[half * size:(half + 1) * size, kv * ROWS:(kv + 1) * ROWS]
 
 
@@ -90,11 +90,12 @@
     keys = [ref[0] for ref in held]
     wides = [jnp.concatenate([ref[1], jnp.ones_like(ref[1])], axis=1) for ref in held]
     eye = diagonal(HEAD)
-    blocks = HEAD // ROWS
     targets, size = out_ref.shape[0], out_ref.shape[1] - 1
 
-    def scores_of(start):
-        query = query_ref[start:start + blocks].reshape(HEAD, HEAD)
+    rows = size * ROWS
+
+    def scores_of(target):
+        query = query_ref[target * size:(target + 1) * size].reshape(rows, HEAD)
         return [
             lax.dot_general(query, key, (((1,), (1,)), ((), ())), preferred_element_type=jnp.float32)
             for key in keys
@@ -102,25 +103,24 @@
 
     ahead = scores_of(0)
     for target in range(targets):
-        levels = []
-        for start in range(0, size, blocks):
-            scores = ahead
-            following = target * size + start + blocks
-            if following < targets * size:
-                ahead = scores_of(following)
-            top = jnp.max(functools.reduce(jnp.maximum, scores), axis=1, keepdims=True)
-            result = jnp.zeros((HEAD, 2 * HEAD), jnp.float32)
-            for score, wide in zip(scores, wides):
-                weights = jnp.exp2((score - top) * (SCALE * LOG2E))
-                result = result + jnp.dot(
-                    weights.astype(jnp.bfloat16), wide, preferred_element_type=jnp.float32
-                )
-            total = result[:, HEAD:]
-            out_ref[target, start:start + blocks] = (
-                (result[:, :HEAD] / total).astype(out_ref.dtype).reshape(blocks, ROWS, HEAD)
+        scores = ahead
+        if target + 1 < targets:
+            ahead = scores_of(target + 1)
+        top = jnp.max(functools.reduce(jnp.maximum, scores), axis=1, keepdims=True)
+        result = jnp.zeros((rows, 2 * HEAD), jnp.float32)
+        for score, wide in zip(scores, wides):
+            weights = jnp.exp2((score - top) * (SCALE * LOG2E))
+            result = result + jnp.dot(
+                weights.astype(jnp.bfloat16), wide, preferred_element_type=jnp.float32
             )
-            levels.append(to_lanes(top * SCALE + jnp.log(total), eye))
-        levels = jnp.concatenate(levels, axis=0)
+        total = result[:, HEAD:]
+        out_ref[target, :size] = (
+            (result[:, :HEAD] / total).astype(out_ref.dtype).reshape(size, ROWS, HEAD)
+        )
+        level = top * SCALE + jnp.log(total)
+        levels = jnp.concatenate(
+            [to_lanes(level[at:at + HEAD], eye) for at in range(0, rows, HEAD)], axis=0
+        )
         pieces = list(pieces_of(levels))
         spare = ROWS - 3 * levels.shape[0]
         if spare:
@@ -142,7 +142,7 @@
             there = slice(half * size + group * blocks, half * size + (group + 1) * blocks)
             stats = jnp.zeros((HEAD, HEAD), jnp.float32)
             for kv in range(kvs):
-                members = range(2 * kv + half, ring, CLASSES)
+                members = range(kv + 2 * half, ring, CLASSES)
                 levels = [
                     table[source, group:group + 1]
                     + table[source, groups + group:groups + group + 1]
@@ -260,7 +260,7 @@
 def attend(query, held):
     tokens = sum(part.shape[1] for part in held)
     ring, size, rows, width = query.shape
-    step = 2
+    step = 4
     whole = pl.BlockSpec(held[0].shape, lambda i: (0, 0, 0))
     return pl.pallas_call(
         attend_kernel,
@@ -309,14 +309,12 @@
     )(owners, back, tail, top, total)
 
 
-def share(array, flip):
+def send(array, step):
     ring, cores = lax.axis_size("y"), lax.axis_size("tp")
     pairs = []
     for at in range(ring):
         for core in range(cores):
-            first = at - (at - 2 * core) % CLASSES
-            spots = [(first + i) % ring for i in range(CLASSES)]
-            to = next(spot for spot in spots if spot % CLASSES == (at % CLASSES) ^ flip)
+            to = (at + (step if core == 0 else -step)) % ring
             pairs.append((at * cores + core, to * cores + core))
     return lax.ppermute(array, ("y", "tp"), pairs)
 
@@ -326,17 +324,17 @@
     ring = lax.axis_size("y")
     plane = ("prefix", "zh")
     kvs = queries.shape[1] // (HEAD * GROUP)
-    kv = lax.axis_index("y") // 2 % 2
+    kv = lax.axis_index("y") % 2
     own = lax.dynamic_slice_in_dim(prefix_kv[0], kv * HEAD, HEAD, 2)
     other = lax.dynamic_slice_in_dim(prefix_kv[0], (1 - kv) * HEAD, HEAD, 2)
-    shared = [share(own, 1), share(other, 2), share(other, 3)]
+    shared = [send(other, 1), send(other, -1), send(own, -2)]
     buckets = place(prefix_map, queries, owner_count)
     buckets = buckets.reshape((owner_count * Z_HALVES,) + buckets.shape[2:])
     mine = lax.all_to_all(buckets, plane, split_axis=0, concat_axis=0, tiled=True)
     sent = fan(mine, ring)
-    sent, shared = lax.optimization_barrier((sent, shared))
     query = lax.all_to_all(sent, "y", split_axis=0, concat_axis=0, tiled=True)
     partial = attend(query, [own] + shared)
+    partial, queries = lax.optimization_barrier((partial, queries))
     back = lax.all_to_all(partial, "y", split_axis=0, concat_axis=0, tiled=True)
     tails = tail_attend(queries, suffix_kv, suffix_len)
     blended = blend(back, kvs)

time: 127 us -> 130 us (1.024)
  waiting for transfers between devices: 9.96 us -> 36.6 us
  blocking collectives: 76.2 us -> 53.4 us
  starting transfers between devices: 24 us -> 22.5 us
    ppermute x3, waiting for transfers between devices: 0.01 us -> 26.6 us  [send(): return lax.ppermute(array, ('y', 'tp'), pairs)]
    all_to_all x1 -> x0, blocking collectives: 26.5 us -> none  [per_device(): query = lax.all_to_all(sent, 'y', split_axis=0, concat_axis=0, tiled=True)]
    all_to_all x1, starting transfers between devices: 13.1 us -> 6.18 us  [per_device(): lax.all_to_all(blended, plane, split_axis=0, concat_axis=0, tiled=True)]
    all_to_all x0 -> x1, starting transfers between devices: none -> 6.82 us  [per_device(): query = lax.all_to_all(sent, 'y', split_axis=0, concat_axis=0, tiled=True)]
    all_to_all x1, blocking collectives: 18.1 us -> 21.5 us  [per_device(): back = lax.all_to_all(partial, 'y', split_axis=0, concat_axis=0, tiled=True)]
    unnamed x10 -> x12, local copies, waits for them, and re-layouts: 0.73 us -> 2.21 us
    ppermute x3, starting transfers between devices: 10.9 us -> 9.54 us  [send(): return lax.ppermute(array, ('y', 'tp'), pairs)]
  transfers between devices with their start and end apart: 4 -> 5, of which waited for: 1 -> 3; matrix products, arithmetic and copies ran while one was open for 0% -> 0% of each run, Pallas kernels for 1% -> 1%
where the time goes in v3:
time: 130 us; the launch traced here: 129 us
  blocking collectives  53.4 us (41%)
  waiting for transfers between devices  36.6 us (28%)
  starting transfers between devices  22.5 us (17%)
  Pallas kernels  14.1 us (11%)
  local copies, waits for them, and re-layouts  2.4 us (2%)
    ppermute x3, waiting for transfers between devices, send(): return lax.ppermute(array, ('y', 'tp'), pairs)  26.6 us
    all_to_all x1, blocking collectives, per_device(): lax.all_to_all(buckets, plane, split_axis=0, concat_axis=0, tiled=True)  23.6 us
    all_to_all x1, blocking collectives, per_device(): back = lax.all_to_all(partial, 'y', split_axis=0, concat_axis=0, tiled=True)  21.5 us
    pallas_call x1, Pallas kernels, attend(): pl.pallas_call(attend_kernel, grid=(ring // step,), in_specs=[whole] * le...  10.1 us
    all_to_all x1, waiting for transfers between devices, per_device(): lax.all_to_all(blended, plane, split_axis=0, concat_axis=0, tiled=True)  10 us
    ppermute x3, starting transfers between devices, send(): return lax.ppermute(array, ('y', 'tp'), pairs)  9.54 us
    all_to_all x1, blocking collectives, per_device(): lax.all_to_all(attended, 'tp', split_axis=0, concat_axis=1, tiled=True)  8.26 us
    all_to_all x1, starting transfers between devices, per_device(): query = lax.all_to_all(sent, 'y', split_axis=0, concat_axis=0, tiled=True)  6.82 us
  transfers between devices with their start and end apart: 5, of which 3 were waited for; matrix products, arithmetic and copies ran while one was open for 0% of the time, Pallas kernels for 1%

profile of v3, /device:TPU:1, one launch (start us, length us, event | category | flops | bytes accessed | tf_op | source)
XLA Modules:
  0.0 129.1 jit_solution(6117392706973216989)
XLA Ops:
  0.0 0.7 copy.7.owners_ref
  0.7 0.0 copy-start.1
  0.7 0.8 copy-done.1
  1.6 0.4 place.1
  2.0 23.6 %all_to_all.39.mine_ref = bf16[32,32,128]{2,1,0:T(8,128)(2,1)S(1)} all-to-all(bf16[32,32,128]{2,1,0:T(8,128)(2,1)S(1)} %bitcast.12), channel_id=1, replica_groups=mesh['prefix'=16,'zh'=2,'y'=8,'tp'=2] {'prefix','zh'}, dimensions={0} | all-to-all | bytes 524288 | tf_op jit(solution)/shard_map/all_to_all | solution.py:333
  25.6 0.0 copy-start.4
  25.6 0.9 fan.1
  26.5 6.8 %all-to-all-start.1 = ((bf16[8,16,16,128]{3,2,1,0:T(8,128)(2,1)}), bf16[8,16,16,128]{3,2,1,0:T(8,128)(2,1)S(1)}, u32[]{:S(2)}, u32[]{:S(2)}) async-start(bf16[8,16,16,128]{3,2,1,0:T(8,128)(2,1)} %fan.1), calls=%async_computation.1 | async-start | bytes 1048576 | tf_op jit(solution)/shard_map/all_to_all | solution.py:335
  33.3 0.0 copy-done.4
  33.3 0.2 dynamic-slice_bitcast_fusion
  33.5 3.4 %collective-permute-start.1 = (bf16[2,1024,128]{2,1,0:T(8,128)(2,1)S(1)}, bf16[2,1024,128]{2,1,0:T(8,128)(2,1)S(1)}, u32[]{:S(2)}, u32[]{:S(2)}) collective-permute-start(bf16[2,1024,128]{2,1,0:T(8,128)(2,1)S(1)} %get-tuple-element.15), channel_id=1, source_target_pairs={{0,14},{1,3},{2,0},{3,5},{4,2},{5,7},{6,4},{7,9},{8,6},{9,11},{10,... | collective-permute-start | bytes 1572872 | tf_op jit(solution)/shard_map/ppermute | solution.py:319
  36.9 3.1 %collective-permute-start = (bf16[2,1024,128]{2,1,0:T(8,128)(2,1)S(1)}, bf16[2,1024,128]{2,1,0:T(8,128)(2,1)S(1)}, u32[]{:S(2)}, u32[]{:S(2)}) collective-permute-start(bf16[2,1024,128]{2,1,0:T(8,128)(2,1)S(1)} %get-tuple-element.15), channel_id=1, source_target_pairs={{0,2},{1,15},{2,4},{3,1},{4,6},{5,3},{6,8},{7,5},{8,10},{9,7},{10,... | collective-permute-start | bytes 1572872 | tf_op jit(solution)/shard_map/ppermute | solution.py:319
  40.0 3.0 %collective-permute-start.2 = (bf16[2,1024,128]{2,1,0:T(8,128)(2,1)S(1)}, bf16[2,1024,128]{2,1,0:T(8,128)(2,1)S(1)}, u32[]{:S(2)}, u32[]{:S(2)}) collective-permute-start(bf16[2,1024,128]{2,1,0:T(8,128)(2,1)S(1)} %get-tuple-element.16.refs_0_), channel_id=1, source_target_pairs={{0,12},{1,5},{2,14},{3,7},{4,0},{5,9},{6,2},{7,11},{8,4},{9,13},{1... | collective-permute-start | bytes 1572872 | tf_op jit(solution)/shard_map/ppermute | solution.py:319
  43.1 15.0 %collective-permute-done.1.refs_2_ = bf16[2,1024,128]{2,1,0:T(8,128)(2,1)S(1)} collective-permute-done((bf16[2,1024,128]{2,1,0:T(8,128)(2,1)S(1)}, bf16[2,1024,128]{2,1,0:T(8,128)(2,1)S(1)}, u32[]{:S(2)}, u32[]{:S(2)}) %collective-permute-start.1) | collective-permute-done | bytes 524320 | tf_op jit(solution)/shard_map/ppermute | solution.py:319
  58.1 0.0 collective-permute-done.refs_1_
  58.1 11.5 %collective-permute-done.2.refs_3_ = bf16[2,1024,128]{2,1,0:T(8,128)(2,1)S(1)} collective-permute-done((bf16[2,1024,128]{2,1,0:T(8,128)(2,1)S(1)}, bf16[2,1024,128]{2,1,0:T(8,128)(2,1)S(1)}, u32[]{:S(2)}, u32[]{:S(2)}) %collective-permute-start.2) | collective-permute-done | bytes 524320 | tf_op jit(solution)/shard_map/ppermute | solution.py:319
  69.6 0.0 all-to-all-done.1
  69.6 10.1 %attend.1 = bf16[8,17,16,128]{3,2,1,0:T(8,128)(2,1)S(1)} custom-call(bf16[2,1024,128]{2,1,0:T(8,128)(2,1)S(1)} %get-tuple-element.16.refs_0_, bf16[2,1024,128]{2,1,0:T(8,128)(2,1)S(1)} %collective-permute-done.refs_1_, bf16[2,1024,128]{2,1,0:T(8,128)(2,1)S(1)} %collective-permute-done.1.refs_2_, bf16[2,1024,128]{2,1,0:T(8,128)(2,1)S(1)} %collective-permute-done.2.refs_3_, ...), custom_call_target="tpu_custom_call" | custom-call | flops 6442450944 | bytes 1048576 | tf_op jit(solution)/shard_map/attend/pallas_call | solution.py:265
  79.8 21.5 %all_to_all.40.back_ref = bf16[8,17,16,128]{3,2,1,0:T(8,128)(2,1)S(1)} all-to-all(bf16[8,17,16,128]{3,2,1,0:T(8,128)(2,1)S(1)} %attend.1), channel_id=1, replica_groups=mesh['prefix'=16,'zh'=2,'y'=8,'tp'=2] {'y'}, dimensions={0} | all-to-all | bytes 1114112 | tf_op jit(solution)/shard_map/all_to_all | solution.py:338
  101.3 0.0 copy-start
  101.3 1.2 blend.1
  102.6 0.0 copy-start.2
  102.6 0.0 copy-start.3
  102.6 6.2 %all-to-all-start.3 = ((bf16[32,48,128]{2,1,0:T(8,128)(2,1)}), bf16[32,48,128]{2,1,0:T(8,128)(2,1)S(1)}, u32[]{:S(2)}, u32[]{:S(2)}) async-start(bf16[32,48,128]{2,1,0:T(8,128)(2,1)} %blend.1), calls=%async_computation.3 | async-start | bytes 786432 | tf_op jit(solution)/shard_map/all_to_all | solution.py:341
  108.7 0.0 copy-done
  108.8 0.0 copy-done.2
  108.8 0.0 copy-done.3
  108.8 0.8 tail.1
  109.6 10.0 %all-to-all-done.3 = bf16[32,48,128]{2,1,0:T(8,128)(2,1)S(1)} async-done(((bf16[32,48,128]{2,1,0:T(8,128)(2,1)}), bf16[32,48,128]{2,1,0:T(8,128)(2,1)S(1)}, u32[]{:S(2)}, u32[]{:S(2)}) %all-to-all-start.3) | async-done | bytes 393248 | tf_op jit(solution)/shard_map/all_to_all | solution.py:341
  119.6 0.6 merge.1
  120.2 8.3 %all_to_all.41 = bf16[2,8,2048]{2,1,0:T(8,128)(2,1)S(1)} all-to-all(bf16[2,8,2048]{2,1,0:T(8,128)(2,1)S(1)} %bitcast.14), channel_id=1, replica_groups=mesh['prefix'=16,'zh'=2,'y'=8,'tp'=2] {'tp'}, dimensions={0} | all-to-all | bytes 131072 | tf_op jit(solution)/shard_map/all_to_all | solution.py:344
  128.5 0.6 copy.9
Async XLA Ops:
  0.7 0.8 copy-start.1
  25.6 7.7 %copy-start.4 = (bf16[1,2,1024,256]{3,2,1,0:T(8,128)(2,1)S(1)}, bf16[1,2,1024,256]{3,2,1,0:T(8,128)(2,1)}, u32[]{:S(2)}) copy-start(bf16[1,2,1024,256]{3,2,1,0:T(8,128)(2,1)} %param.6) | copy-start | bytes 3145732
  26.5 43.1 %all-to-all-start.1 = ((bf16[8,16,16,128]{3,2,1,0:T(8,128)(2,1)}), bf16[8,16,16,128]{3,2,1,0:T(8,128)(2,1)S(1)}, u32[]{:S(2)}, u32[]{:S(2)}) async-start(bf16[8,16,16,128]{3,2,1,0:T(8,128)(2,1)} %fan.1), calls=%async_computation.1 | async-start | bytes 1048576 | tf_op jit(solution)/shard_map/all_to_all | solution.py:335
  33.5 24.6 %collective-permute-start.1 = (bf16[2,1024,128]{2,1,0:T(8,128)(2,1)S(1)}, bf16[2,1024,128]{2,1,0:T(8,128)(2,1)S(1)}, u32[]{:S(2)}, u32[]{:S(2)}) collective-permute-start(bf16[2,1024,128]{2,1,0:T(8,128)(2,1)S(1)} %get-tuple-element.15), channel_id=1, source_target_pairs={{0,14},{1,3},{2,0},{3,5},{4,2},{5,7},{6,4},{7,9},{8,6},{9,11},{10,... | collective-permute-start | bytes 1572872 | tf_op jit(solution)/shard_map/ppermute | solution.py:319
  36.9 21.2 %collective-permute-start = (bf16[2,1024,128]{2,1,0:T(8,128)(2,1)S(1)}, bf16[2,1024,128]{2,1,0:T(8,128)(2,1)S(1)}, u32[]{:S(2)}, u32[]{:S(2)}) collective-permute-start(bf16[2,1024,128]{2,1,0:T(8,128)(2,1)S(1)} %get-tuple-element.15), channel_id=1, source_target_pairs={{0,2},{1,15},{2,4},{3,1},{4,6},{5,3},{6,8},{7,5},{8,10},{9,7},{10,... | collective-permute-start | bytes 1572872 | tf_op jit(solution)/shard_map/ppermute | solution.py:319
  40.0 29.6 %collective-permute-start.2 = (bf16[2,1024,128]{2,1,0:T(8,128)(2,1)S(1)}, bf16[2,1024,128]{2,1,0:T(8,128)(2,1)S(1)}, u32[]{:S(2)}, u32[]{:S(2)}) collective-permute-start(bf16[2,1024,128]{2,1,0:T(8,128)(2,1)S(1)} %get-tuple-element.16.refs_0_), channel_id=1, source_target_pairs={{0,12},{1,5},{2,14},{3,7},{4,0},{5,9},{6,2},{7,11},{8,4},{9,13},{1... | collective-permute-start | bytes 1572872 | tf_op jit(solution)/shard_map/ppermute | solution.py:319
  101.3 7.4 %copy-start = (bf16[16,2,64,256]{3,2,1,0:T(8,128)(2,1)S(1)}, bf16[16,2,64,256]{3,2,1,0:T(8,128)(2,1)}, u32[]{:S(2)}) copy-start(bf16[16,2,64,256]{3,2,1,0:T(8,128)(2,1)} %suffix_ref.1) | copy-start | bytes 3145732
  102.6 6.2 %copy-start.2 = (bf16[16,2048]{1,0:T(8,128)(2,1)S(1)}, bf16[16,2048]{1,0:T(8,128)(2,1)}, u32[]{:S(2)}) copy-start(bf16[16,2048]{1,0:T(8,128)(2,1)} %queries_ref.2) | copy-start | bytes 196612
  102.6 6.2 %copy-start.3 = (s32[1,16]{1,0:T(1,128)S(1)}, s32[1,16]{1,0:T(1,128)}, u32[]{:S(2)}) copy-start(s32[1,16]{1,0:T(1,128)} %length_ref.1) | copy-start | bytes 196
  102.6 17.1 %all-to-all-start.3 = ((bf16[32,48,128]{2,1,0:T(8,128)(2,1)}), bf16[32,48,128]{2,1,0:T(8,128)(2,1)S(1)}, u32[]{:S(2)}, u32[]{:S(2)}) async-start(bf16[32,48,128]{2,1,0:T(8,128)(2,1)} %blend.1), calls=%async_computation.3 | async-start | bytes 786432 | tf_op jit(solution)/shard_map/all_to_all | solution.py:341

commit v4 on v3

--- a/solution.py
+++ b/solution.py
@@ -261,7 +261,7 @@
     tokens = sum(part.shape[1] for part in held)
     ring, size, rows, width = query.shape
     step = 4
-    whole = pl.BlockSpec(held[0].shape, lambda i: (0, 0, 0))
+    whole = pl.BlockSpec(memory_space=pltpu.VMEM)
     return pl.pallas_call(
         attend_kernel,
         grid=(ring // step,),
@@ -332,6 +332,7 @@
     buckets = buckets.reshape((owner_count * Z_HALVES,) + buckets.shape[2:])
     mine = lax.all_to_all(buckets, plane, split_axis=0, concat_axis=0, tiled=True)
     sent = fan(mine, ring)
+    sent, shared = lax.optimization_barrier((sent, shared))
     query = lax.all_to_all(sent, "y", split_axis=0, concat_axis=0, tiled=True)
     partial = attend(query, [own] + shared)
     partial, queries = lax.optimization_barrier((partial, queries))

time: 130 us -> 116 us (0.89)
  waiting for transfers between devices: 36.6 us -> 9.95 us
  blocking collectives: 53.4 us -> 72.3 us
  starting transfers between devices: 22.5 us -> 18 us
    ppermute x3, waiting for transfers between devices: 26.6 us -> 0.01 us  [send(): return lax.ppermute(array, ('y', 'tp'), pairs)]
    all_to_all x0 -> x1, blocking collectives: none -> 22.6 us  [per_device(): query = lax.all_to_all(sent, 'y', split_axis=0, concat_axis=0, tiled=True)]
    all_to_all x1 -> x0, starting transfers between devices: 6.82 us -> none  [per_device(): query = lax.all_to_all(sent, 'y', split_axis=0, concat_axis=0, tiled=True)]
    all_to_all x1, blocking collectives: 21.5 us -> 18.3 us  [per_device(): back = lax.all_to_all(partial, 'y', split_axis=0, concat_axis=0, tiled=True)]
    unnamed x12 -> x10, local copies, waits for them, and re-layouts: 2.21 us -> 0.73 us
    all_to_all x1, starting transfers between devices: 6.18 us -> 7.63 us  [per_device(): lax.all_to_all(blended, plane, split_axis=0, concat_axis=0, tiled=True)]
  transfers between devices with their start and end apart: 5 -> 4, of which waited for: 3 -> 1; matrix products, arithmetic and copies ran while one was open for 0% -> 0% of each run, Pallas kernels for 1% -> 1%
where the time goes in v4:
time: 116 us
  blocking collectives  72.3 us (62%)
  starting transfers between devices  18 us (16%)
  Pallas kernels  13.3 us (11%)
  waiting for transfers between devices  9.95 us (9%)
  local copies, waits for them, and re-layouts  2.03 us (2%)
    all_to_all x1, blocking collectives, per_device(): query = lax.all_to_all(sent, 'y', split_axis=0, concat_axis=0, tiled=True)  22.6 us
    all_to_all x1, blocking collectives, per_device(): lax.all_to_all(buckets, plane, split_axis=0, concat_axis=0, tiled=True)  22.6 us
    all_to_all x1, blocking collectives, per_device(): back = lax.all_to_all(partial, 'y', split_axis=0, concat_axis=0, tiled=True)  18.3 us
    ppermute x3, starting transfers between devices, send(): return lax.ppermute(array, ('y', 'tp'), pairs)  10.3 us
    pallas_call x1, Pallas kernels, attend(): pl.pallas_call(attend_kernel, grid=(ring // step,), in_specs=[whole] * le...  10.1 us
    all_to_all x1, waiting for transfers between devices, per_device(): lax.all_to_all(blended, plane, split_axis=0, concat_axis=0, tiled=True)  9.95 us
    all_to_all x1, blocking collectives, per_device(): lax.all_to_all(attended, 'tp', split_axis=0, concat_axis=1, tiled=True)  8.82 us
    all_to_all x1, starting transfers between devices, per_device(): lax.all_to_all(blended, plane, split_axis=0, concat_axis=0, tiled=True)  7.63 us
  transfers between devices with their start and end apart: 4, of which 1 were waited for; matrix products, arithmetic and copies ran while one was open for 0% of the time, Pallas kernels for 1%

profile of v4, /device:TPU:1, one launch (start us, length us, event | category | flops | bytes accessed | tf_op | source)
XLA Modules:
  0.0 115.7 jit_solution(5848147551863959063)
XLA Ops:
  0.0 0.0 copy-start.1
  0.0 1.3 %dynamic-slice_bitcast_fusion = (bf16[2,1024,128]{2,1,0:T(8,128)(2,1)S(1)}, bf16[2,1024,128]{2,1,0:T(8,128)(2,1)S(1)}) fusion(bf16[1,2,1024,256]{3,2,1,0:T(8,128)(2,1)} %param.6, s32[]{:T(128)S(6)} %select_n.15, s32[]{:T(128)S(6)} %select_n.14), kind=kLoop, calls=%fused_computation | loop fusion | bytes 2097160 | tf_op jit(solution)/shard_map/dynamic_slice | solution.py:329
  1.3 0.0 copy-start.3
  1.3 4.0 %collective-permute-start.1 = (bf16[2,1024,128]{2,1,0:T(8,128)(2,1)S(1)}, bf16[2,1024,128]{2,1,0:T(8,128)(2,1)S(1)}, u32[]{:S(2)}, u32[]{:S(2)}) collective-permute-start(bf16[2,1024,128]{2,1,0:T(8,128)(2,1)S(1)} %get-tuple-element.23), channel_id=1, source_target_pairs={{0,14},{1,3},{2,0},{3,5},{4,2},{5,7},{6,4},{7,9},{8,6},{9,11},{10,... | collective-permute-start | bytes 1572872 | tf_op jit(solution)/shard_map/ppermute | solution.py:319
  5.4 3.8 %collective-permute-start = (bf16[2,1024,128]{2,1,0:T(8,128)(2,1)S(1)}, bf16[2,1024,128]{2,1,0:T(8,128)(2,1)S(1)}, u32[]{:S(2)}, u32[]{:S(2)}) collective-permute-start(bf16[2,1024,128]{2,1,0:T(8,128)(2,1)S(1)} %get-tuple-element.23), channel_id=1, source_target_pairs={{0,2},{1,15},{2,4},{3,1},{4,6},{5,3},{6,8},{7,5},{8,10},{9,7},{10,... | collective-permute-start | bytes 1572872 | tf_op jit(solution)/shard_map/ppermute | solution.py:319
  9.2 2.5 %collective-permute-start.2 = (bf16[2,1024,128]{2,1,0:T(8,128)(2,1)S(1)}, bf16[2,1024,128]{2,1,0:T(8,128)(2,1)S(1)}, u32[]{:S(2)}, u32[]{:S(2)}) collective-permute-start(bf16[2,1024,128]{2,1,0:T(8,128)(2,1)S(1)} %get-tuple-element.24.refs_0_), channel_id=1, source_target_pairs={{0,12},{1,5},{2,14},{3,7},{4,0},{5,9},{6,2},{7,11},{8,4},{9,13},{1... | collective-permute-start | bytes 1572872 | tf_op jit(solution)/shard_map/ppermute | solution.py:319
  11.7 0.0 copy-done.3
  11.7 0.1 copy.7.owners_ref
  11.8 0.0 copy-done.1
  11.8 0.4 place.1
  12.2 22.6 %all_to_all.39.mine_ref = bf16[32,32,128]{2,1,0:T(8,128)(2,1)S(1)} all-to-all(bf16[32,32,128]{2,1,0:T(8,128)(2,1)S(1)} %bitcast.12), channel_id=1, replica_groups=mesh['prefix'=16,'zh'=2,'y'=8,'tp'=2] {'prefix','zh'}, dimensions={0} | all-to-all | bytes 524288 | tf_op jit(solution)/shard_map/all_to_all | solution.py:333
  34.8 0.1 fan.1
  34.8 0.0 collective-permute-done.1.refs_2_
  34.8 0.0 collective-permute-done.refs_1_
  34.8 0.0 collective-permute-done.2.refs_3_
  34.9 22.6 %all_to_all.40 = bf16[8,16,16,128]{3,2,1,0:T(8,128)(2,1)S(1)} all-to-all(bf16[8,16,16,128]{3,2,1,0:T(8,128)(2,1)S(1)} %fan.1), channel_id=1, replica_groups=mesh['prefix'=16,'zh'=2,'y'=8,'tp'=2] {'y'}, dimensions={0} | all-to-all | bytes 1048576 | tf_op jit(solution)/shard_map/all_to_all | solution.py:336
  57.5 10.1 %attend.1 = bf16[8,17,16,128]{3,2,1,0:T(8,128)(2,1)S(1)} custom-call(bf16[2,1024,128]{2,1,0:T(8,128)(2,1)S(1)} %get-tuple-element.24.refs_0_, bf16[2,1024,128]{2,1,0:T(8,128)(2,1)S(1)} %collective-permute-done.refs_1_, bf16[2,1024,128]{2,1,0:T(8,128)(2,1)S(1)} %collective-permute-done.1.refs_2_, bf16[2,1024,128]{2,1,0:T(8,128)(2,1)S(1)} %collective-permute-done.2.refs_3_, ...), custom_call_target="tpu_custom_call" | custom-call | flops 6442450944 | bytes 1048576 | tf_op jit(solution)/shard_map/attend/pallas_call | solution.py:265
  67.6 18.3 %all_to_all.41.back_ref = bf16[8,17,16,128]{3,2,1,0:T(8,128)(2,1)S(1)} all-to-all(bf16[8,17,16,128]{3,2,1,0:T(8,128)(2,1)S(1)} %attend.1), channel_id=1, replica_groups=mesh['prefix'=16,'zh'=2,'y'=8,'tp'=2] {'y'}, dimensions={0} | all-to-all | bytes 1114112 | tf_op jit(solution)/shard_map/all_to_all | solution.py:339
  85.9 0.0 copy-start
  85.9 1.3 %blend.1 = bf16[32,48,128]{2,1,0:T(8,128)(2,1)} custom-call(bf16[8,17,16,128]{3,2,1,0:T(8,128)(2,1)S(1)} %all_to_all.41.back_ref), custom_call_target="tpu_custom_call" | custom-call | tf_op jit(solution)/shard_map/blend/pallas_call | solution.py:284
  87.2 0.0 copy-start.2
  87.2 7.6 %all-to-all-start.3 = ((bf16[32,48,128]{2,1,0:T(8,128)(2,1)}), bf16[32,48,128]{2,1,0:T(8,128)(2,1)S(1)}, u32[]{:S(2)}, u32[]{:S(2)}) async-start(bf16[32,48,128]{2,1,0:T(8,128)(2,1)} %blend.1), calls=%async_computation.3 | async-start | bytes 786432 | tf_op jit(solution)/shard_map/all_to_all | solution.py:342
  94.8 0.0 copy-done
  94.8 0.0 copy-done.2
  94.8 0.8 tail.1
  95.7 9.9 %all-to-all-done.3 = bf16[32,48,128]{2,1,0:T(8,128)(2,1)S(1)} async-done(((bf16[32,48,128]{2,1,0:T(8,128)(2,1)}), bf16[32,48,128]{2,1,0:T(8,128)(2,1)S(1)}, u32[]{:S(2)}, u32[]{:S(2)}) %all-to-all-start.3) | async-done | bytes 393248 | tf_op jit(solution)/shard_map/all_to_all | solution.py:342
  105.6 0.6 merge.1
  106.2 8.8 %all_to_all.42 = bf16[2,8,2048]{2,1,0:T(8,128)(2,1)S(1)} all-to-all(bf16[2,8,2048]{2,1,0:T(8,128)(2,1)S(1)} %bitcast.14), channel_id=1, replica_groups=mesh['prefix'=16,'zh'=2,'y'=8,'tp'=2] {'tp'}, dimensions={0} | all-to-all | bytes 131072 | tf_op jit(solution)/shard_map/all_to_all | solution.py:345
  115.1 0.6 copy.9
Async XLA Ops:
  0.0 11.8 %copy-start.1 = (bf16[16,2048]{1,0:T(8,128)(2,1)S(1)}, bf16[16,2048]{1,0:T(8,128)(2,1)}, u32[]{:S(2)}) copy-start(bf16[16,2048]{1,0:T(8,128)(2,1)} %queries_ref.2) | copy-start | bytes 196612
  1.3 10.4 %copy-start.3 = (s32[16,1]{0,1:T(1,128)S(1)}, s32[16,1]{0,1:T(1,128)}, u32[]{:S(2)}) copy-start(s32[16,1]{0,1:T(1,128)} %param.8) | copy-start | bytes 196
  1.3 33.5 %collective-permute-start.1 = (bf16[2,1024,128]{2,1,0:T(8,128)(2,1)S(1)}, bf16[2,1024,128]{2,1,0:T(8,128)(2,1)S(1)}, u32[]{:S(2)}, u32[]{:S(2)}) collective-permute-start(bf16[2,1024,128]{2,1,0:T(8,128)(2,1)S(1)} %get-tuple-element.23), channel_id=1, source_target_pairs={{0,14},{1,3},{2,0},{3,5},{4,2},{5,7},{6,4},{7,9},{8,6},{9,11},{10,... | collective-permute-start | bytes 1572872 | tf_op jit(solution)/shard_map/ppermute | solution.py:319
  5.4 29.5 %collective-permute-start = (bf16[2,1024,128]{2,1,0:T(8,128)(2,1)S(1)}, bf16[2,1024,128]{2,1,0:T(8,128)(2,1)S(1)}, u32[]{:S(2)}, u32[]{:S(2)}) collective-permute-start(bf16[2,1024,128]{2,1,0:T(8,128)(2,1)S(1)} %get-tuple-element.23), channel_id=1, source_target_pairs={{0,2},{1,15},{2,4},{3,1},{4,6},{5,3},{6,8},{7,5},{8,10},{9,7},{10,... | collective-permute-start | bytes 1572872 | tf_op jit(solution)/shard_map/ppermute | solution.py:319
  9.2 25.7 %collective-permute-start.2 = (bf16[2,1024,128]{2,1,0:T(8,128)(2,1)S(1)}, bf16[2,1024,128]{2,1,0:T(8,128)(2,1)S(1)}, u32[]{:S(2)}, u32[]{:S(2)}) collective-permute-start(bf16[2,1024,128]{2,1,0:T(8,128)(2,1)S(1)} %get-tuple-element.24.refs_0_), channel_id=1, source_target_pairs={{0,12},{1,5},{2,14},{3,7},{4,0},{5,9},{6,2},{7,11},{8,4},{9,13},{1... | collective-permute-start | bytes 1572872 | tf_op jit(solution)/shard_map/ppermute | solution.py:319
  85.9 8.9 %copy-start = (bf16[16,2,64,256]{3,2,1,0:T(8,128)(2,1)S(1)}, bf16[16,2,64,256]{3,2,1,0:T(8,128)(2,1)}, u32[]{:S(2)}) copy-start(bf16[16,2,64,256]{3,2,1,0:T(8,128)(2,1)} %suffix_ref.1) | copy-start | bytes 3145732
  87.2 7.6 %copy-start.2 = (s32[1,16]{1,0:T(1,128)S(1)}, s32[1,16]{1,0:T(1,128)}, u32[]{:S(2)}) copy-start(s32[1,16]{1,0:T(1,128)} %length_ref.1) | copy-start | bytes 196
  87.2 18.4 %all-to-all-start.3 = ((bf16[32,48,128]{2,1,0:T(8,128)(2,1)}), bf16[32,48,128]{2,1,0:T(8,128)(2,1)S(1)}, u32[]{:S(2)}, u32[]{:S(2)}) async-start(bf16[32,48,128]{2,1,0:T(8,128)(2,1)} %blend.1), calls=%async_computation.3 | async-start | bytes 786432 | tf_op jit(solution)/shard_map/all_to_all | solution.py:342

commit v5 on v4

--- a/solution.py
+++ b/solution.py
@@ -85,33 +85,30 @@
         out_ref[target] = mine_ref[half * size:(half + 1) * size, kv * ROWS:(kv + 1) * ROWS]
 
 
-def attend_kernel(*refs):
-    held, query_ref, out_ref = refs[:-2], refs[-2], refs[-1]
-    keys = [ref[0] for ref in held]
-    wides = [jnp.concatenate([ref[1], jnp.ones_like(ref[1])], axis=1) for ref in held]
+def attend_kernel(count, *refs):
+    held, query_ref, out_ref = refs[:count], refs[count], refs[count + 1]
+    first_ref, second_ref, wide_ref = refs[count + 2:]
     eye = diagonal(HEAD)
     targets, size = out_ref.shape[0], out_ref.shape[1] - 1
-
     rows = size * ROWS
-
-    def scores_of(target):
-        query = query_ref[target * size:(target + 1) * size].reshape(rows, HEAD)
-        return [
-            lax.dot_general(query, key, (((1,), (1,)), ((), ())), preferred_element_type=jnp.float32)
-            for key in keys
-        ]
-
-    ahead = scores_of(0)
-    for target in range(targets):
-        scores = ahead
-        if target + 1 < targets:
-            ahead = scores_of(target + 1)
+    for index, ref in enumerate(held):
+        wide_ref[index] = jnp.concatenate([ref[1], jnp.ones_like(ref[1])], axis=1)
+
+    def score(slot_ref, target):
+        query = query_ref[pl.ds(target * size, size)].reshape(rows, HEAD)
+        for index, ref in enumerate(held):
+            slot_ref[index] = lax.dot_general(
+                query, ref[0], (((1,), (1,)), ((), ())), preferred_element_type=jnp.float32
+            )
+
+    def finish(slot_ref, target):
+        scores = [slot_ref[index] for index in range(count)]
         top = jnp.max(functools.reduce(jnp.maximum, scores), axis=1, keepdims=True)
         result = jnp.zeros((rows, 2 * HEAD), jnp.float32)
-        for score, wide in zip(scores, wides):
-            weights = jnp.exp2((score - top) * (SCALE * LOG2E))
+        for index in range(count):
+            weights = jnp.exp2((slot_ref[index] - top) * (SCALE * LOG2E))
             result = result + jnp.dot(
-                weights.astype(jnp.bfloat16), wide, preferred_element_type=jnp.float32
+                weights.astype(jnp.bfloat16), wide_ref[index], preferred_element_type=jnp.float32
             )
         total = result[:, HEAD:]
         out_ref[target, :size] = (
@@ -127,20 +124,29 @@
             pieces.append(jnp.zeros((spare, HEAD), jnp.float32))
         out_ref[target, size] = jnp.concatenate(pieces, axis=0).astype(out_ref.dtype)
 
+    score(first_ref, 0)
+
+    def pair(index, carry):
+        target = 2 * index
+        score(second_ref, target + 1)
+        finish(first_ref, target)
+        score(first_ref, jnp.minimum(target + 2, targets - 1))
+        finish(second_ref, target + 1)
+        return carry
+
+    lax.fori_loop(0, targets // 2, pair, 0)
+
 
 def blend_kernel(back_ref, out_ref):
     ring, size = back_ref.shape[0], back_ref.shape[1] - 1
     kvs = (out_ref.shape[1] - STATS) // ROWS
-    eye = diagonal(HEAD)
     blocks = HEAD // ROWS
     groups = size // blocks
     lane = iota((HEAD, HEAD), 1)
     table = back_ref[:, size].astype(jnp.float32)
+    lanes, places = [], []
     for half in range(2):
         for group in range(groups):
-            here = slice(group * blocks, (group + 1) * blocks)
-            there = slice(half * size + group * blocks, half * size + (group + 1) * blocks)
-            stats = jnp.zeros((HEAD, HEAD), jnp.float32)
             for kv in range(kvs):
                 members = range(kv + 2 * half, ring, CLASSES)
                 levels = [
@@ -152,16 +158,26 @@
                 top = functools.reduce(jnp.maximum, levels)
                 weights = [jnp.exp(level - top) for level in levels]
                 total = sum(weights)
-                mixed = jnp.zeros((HEAD, HEAD), jnp.float32)
-                for weight, source in zip(weights, members):
-                    mean = back_ref[source, here].reshape(HEAD, HEAD).astype(jnp.float32)
-                    mixed = mixed + mean * to_column(weight / total, eye)
-                out_ref[there, kv * ROWS:(kv + 1) * ROWS] = mixed.astype(out_ref.dtype).reshape(
-                    blocks, ROWS, HEAD
-                )
-                column = to_column(top + jnp.log(total), eye)
-                for index, piece in enumerate(pieces_of(column)):
-                    stats = jnp.where(lane == kv * 3 + index, piece, stats)
+                places.append((half, group, kv, members, len(lanes)))
+                lanes += [weight / total for weight in weights] + [top + jnp.log(total)]
+    lanes += [jnp.zeros((1, HEAD), jnp.float32)] * (-len(lanes) % 8)
+    columns = jnp.transpose(jnp.concatenate(lanes, axis=0))
+    stats = None
+    for half, group, kv, members, at in places:
+        here = slice(group * blocks, (group + 1) * blocks)
+        there = slice(half * size + group * blocks, half * size + (group + 1) * blocks)
+        mixed = jnp.zeros((HEAD, HEAD), jnp.float32)
+        for index, source in enumerate(members):
+            mean = back_ref[source, here].reshape(HEAD, HEAD).astype(jnp.float32)
+            mixed = mixed + mean * columns[:, at + index:at + index + 1]
+        out_ref[there, kv * ROWS:(kv + 1) * ROWS] = mixed.astype(out_ref.dtype).reshape(
+            blocks, ROWS, HEAD
+        )
+        stats = jnp.zeros((HEAD, HEAD), jnp.float32) if kv == 0 else stats
+        level = columns[:, at + len(members):at + len(members) + 1]
+        for index, piece in enumerate(pieces_of(level)):
+            stats = jnp.where(lane == kv * 3 + index, piece, stats)
+        if kv == kvs - 1:
             out_ref[there, kvs * ROWS:] = stats.astype(out_ref.dtype).reshape(blocks, STATS, HEAD)
 
 
@@ -258,22 +274,21 @@
 
 
 def attend(query, held):
-    tokens = sum(part.shape[1] for part in held)
+    count, tokens = len(held), held[0].shape[1]
     ring, size, rows, width = query.shape
-    step = 4
-    whole = pl.BlockSpec(memory_space=pltpu.VMEM)
-    return pl.pallas_call(
-        attend_kernel,
-        grid=(ring // step,),
-        in_specs=[whole] * len(held)
-        + [pl.BlockSpec((step * size, rows, width), lambda i: (i, 0, 0))],
-        out_specs=pl.BlockSpec((step, size + 1, rows, width), lambda i: (i, 0, 0, 0)),
+    slot = pltpu.VMEM((count, size * rows, tokens), jnp.float32)
+    total = ring * size * rows
+    return pl.pallas_call(
+        functools.partial(attend_kernel, count),
+        in_specs=[pl.BlockSpec(memory_space=pltpu.VMEM)] * (count + 1),
+        out_specs=pl.BlockSpec(memory_space=pltpu.VMEM),
         out_shape=jax.ShapeDtypeStruct((ring, size + 1, rows, width), query.dtype),
+        scratch_shapes=[slot, slot, pltpu.VMEM((count, tokens, 2 * HEAD), query.dtype)],
         compiler_params=params(),
         cost_estimate=pl.CostEstimate(
-            flops=6 * ring * size * rows * tokens * HEAD,
-            bytes_accessed=ring * size * rows * HEAD * 4,
-            transcendentals=ring * size * rows * tokens,
+            flops=6 * total * count * tokens * HEAD,
+            bytes_accessed=total * HEAD * 4,
+            transcendentals=total * count * tokens,
         ),
         name="attend",
     )(*held, query.reshape(ring * size, rows, width))
@@ -327,7 +342,7 @@
     kv = lax.axis_index("y") % 2
     own = lax.dynamic_slice_in_dim(prefix_kv[0], kv * HEAD, HEAD, 2)
     other = lax.dynamic_slice_in_dim(prefix_kv[0], (1 - kv) * HEAD, HEAD, 2)
-    shared = [send(other, 1), send(other, -1), send(own, -2)]
+    shared = [send(own, -2), send(other, 1), send(other, -1)]
     buckets = place(prefix_map, queries, owner_count)
     buckets = buckets.reshape((owner_count * Z_HALVES,) + buckets.shape[2:])
     mine = lax.all_to_all(buckets, plane, split_axis=0, concat_axis=0, tiled=True)

time: 116 us -> 118 us (1.017)
  Pallas kernels: 13.3 us -> 15 us
    pallas_call x1, Pallas kernels: 10.1 us -> 11.6 us  [attend(): pl.pallas_call(functools.partial(attend_kernel, count), in_specs=[pl.Bloc...]
where the time goes in v5:
time: 118 us; the launch traced here: 117 us
  blocking collectives  72 us (61%)
  starting transfers between devices  18.2 us (15%)
  Pallas kernels  15 us (13%)
  waiting for transfers between devices  9.96 us (8%)
  local copies, waits for them, and re-layouts  2.03 us (2%)
    all_to_all x1, blocking collectives, per_device(): query = lax.all_to_all(sent, 'y', split_axis=0, concat_axis=0, tiled=True)  22.6 us
    all_to_all x1, blocking collectives, per_device(): lax.all_to_all(buckets, plane, split_axis=0, concat_axis=0, tiled=True)  22.6 us
    all_to_all x1, blocking collectives, per_device(): back = lax.all_to_all(partial, 'y', split_axis=0, concat_axis=0, tiled=True)  18 us
    pallas_call x1, Pallas kernels, attend(): pl.pallas_call(functools.partial(attend_kernel, count), in_specs=[pl.Bloc...  11.6 us
    ppermute x3, starting transfers between devices, send(): return lax.ppermute(array, ('y', 'tp'), pairs)  10.3 us
    all_to_all x1, waiting for transfers between devices, per_device(): lax.all_to_all(blended, plane, split_axis=0, concat_axis=0, tiled=True)  9.95 us
    all_to_all x1, blocking collectives, per_device(): lax.all_to_all(attended, 'tp', split_axis=0, concat_axis=1, tiled=True)  8.82 us
    all_to_all x1, starting transfers between devices, per_device(): lax.all_to_all(blended, plane, split_axis=0, concat_axis=0, tiled=True)  7.9 us
  transfers between devices with their start and end apart: 4, of which 1 were waited for; matrix products, arithmetic and copies ran while one was open for 0% of the time, Pallas kernels for 1%

profile of v5, /device:TPU:1, one launch (start us, length us, event | category | flops | bytes accessed | tf_op | source)
XLA Modules:
  0.0 117.3 jit_solution(13370175501378279180)
XLA Ops:
  0.0 0.0 copy-start.1
  0.0 1.3 %dynamic-slice_bitcast_fusion = (bf16[2,1024,128]{2,1,0:T(8,128)(2,1)S(1)}, bf16[2,1024,128]{2,1,0:T(8,128)(2,1)S(1)}) fusion(bf16[1,2,1024,256]{3,2,1,0:T(8,128)(2,1)} %param.6, s32[]{:T(128)S(6)} %select_n.15, s32[]{:T(128)S(6)} %select_n.14), kind=kLoop, calls=%fused_computation | loop fusion | bytes 2097160 | tf_op jit(solution)/shard_map/dynamic_slice | solution.py:344
  1.3 0.0 copy-start.3
  1.3 4.0 %collective-permute-start.2 = (bf16[2,1024,128]{2,1,0:T(8,128)(2,1)S(1)}, bf16[2,1024,128]{2,1,0:T(8,128)(2,1)S(1)}, u32[]{:S(2)}, u32[]{:S(2)}) collective-permute-start(bf16[2,1024,128]{2,1,0:T(8,128)(2,1)S(1)} %get-tuple-element.23), channel_id=1, source_target_pairs={{0,14},{1,3},{2,0},{3,5},{4,2},{5,7},{6,4},{7,9},{8,6},{9,11},{10,... | collective-permute-start | bytes 1572872 | tf_op jit(solution)/shard_map/ppermute | solution.py:334
  5.4 3.8 %collective-permute-start.1 = (bf16[2,1024,128]{2,1,0:T(8,128)(2,1)S(1)}, bf16[2,1024,128]{2,1,0:T(8,128)(2,1)S(1)}, u32[]{:S(2)}, u32[]{:S(2)}) collective-permute-start(bf16[2,1024,128]{2,1,0:T(8,128)(2,1)S(1)} %get-tuple-element.23), channel_id=1, source_target_pairs={{0,2},{1,15},{2,4},{3,1},{4,6},{5,3},{6,8},{7,5},{8,10},{9,7},{10,... | collective-permute-start | bytes 1572872 | tf_op jit(solution)/shard_map/ppermute | solution.py:334
  9.2 2.5 %collective-permute-start = (bf16[2,1024,128]{2,1,0:T(8,128)(2,1)S(1)}, bf16[2,1024,128]{2,1,0:T(8,128)(2,1)S(1)}, u32[]{:S(2)}, u32[]{:S(2)}) collective-permute-start(bf16[2,1024,128]{2,1,0:T(8,128)(2,1)S(1)} %get-tuple-element.24.refs_0_), channel_id=1, source_target_pairs={{0,12},{1,5},{2,14},{3,7},{4,0},{5,9},{6,2},{7,11},{8,4},{9,13},{1... | collective-permute-start | bytes 1572872 | tf_op jit(solution)/shard_map/ppermute | solution.py:334
  11.7 0.0 copy-done.3
  11.7 0.1 copy.7.owners_ref
  11.8 0.0 copy-done.1
  11.8 0.4 place.1
  12.2 22.6 %all_to_all.39.mine_ref = bf16[32,32,128]{2,1,0:T(8,128)(2,1)S(1)} all-to-all(bf16[32,32,128]{2,1,0:T(8,128)(2,1)S(1)} %bitcast.12), channel_id=1, replica_groups=mesh['prefix'=16,'zh'=2,'y'=8,'tp'=2] {'prefix','zh'}, dimensions={0} | all-to-all | bytes 524288 | tf_op jit(solution)/shard_map/all_to_all | solution.py:348
  34.8 0.1 fan.1
  34.8 0.0 collective-permute-done.2.refs_3_
  34.8 0.0 collective-permute-done.1.refs_2_
  34.8 0.0 collective-permute-done.refs_1_
  34.9 22.6 %all_to_all.40 = bf16[8,16,16,128]{3,2,1,0:T(8,128)(2,1)S(1)} all-to-all(bf16[8,16,16,128]{3,2,1,0:T(8,128)(2,1)S(1)} %fan.1), channel_id=1, replica_groups=mesh['prefix'=16,'zh'=2,'y'=8,'tp'=2] {'y'}, dimensions={0} | all-to-all | bytes 1048576 | tf_op jit(solution)/shard_map/all_to_all | solution.py:351
  57.5 11.6 %attend.1 = bf16[8,17,16,128]{3,2,1,0:T(8,128)(2,1)S(1)} custom-call(bf16[2,1024,128]{2,1,0:T(8,128)(2,1)S(1)} %get-tuple-element.24.refs_0_, bf16[2,1024,128]{2,1,0:T(8,128)(2,1)S(1)} %collective-permute-done.refs_1_, bf16[2,1024,128]{2,1,0:T(8,128)(2,1)S(1)} %collective-permute-done.1.refs_2_, bf16[2,1024,128]{2,1,0:T(8,128)(2,1)S(1)} %collective-permute-done.2.refs_3_, ...), custom_call_target="tpu_custom_call" | custom-call | flops 6442450944 | bytes 1048576 | tf_op jit(solution)/shard_map/attend/pallas_call | solution.py:281
  69.0 18.0 %all_to_all.41.back_ref = bf16[8,17,16,128]{3,2,1,0:T(8,128)(2,1)S(1)} all-to-all(bf16[8,17,16,128]{3,2,1,0:T(8,128)(2,1)S(1)} %attend.1), channel_id=1, replica_groups=mesh['prefix'=16,'zh'=2,'y'=8,'tp'=2] {'y'}, dimensions={0} | all-to-all | bytes 1114112 | tf_op jit(solution)/shard_map/all_to_all | solution.py:354
  87.1 0.0 copy-start
  87.1 1.5 %blend.1 = bf16[32,48,128]{2,1,0:T(8,128)(2,1)} custom-call(bf16[8,17,16,128]{3,2,1,0:T(8,128)(2,1)S(1)} %all_to_all.41.back_ref), custom_call_target="tpu_custom_call" | custom-call | tf_op jit(solution)/shard_map/blend/pallas_call | solution.py:299
  88.5 0.0 copy-start.2
  88.5 7.9 %all-to-all-start.3 = ((bf16[32,48,128]{2,1,0:T(8,128)(2,1)}), bf16[32,48,128]{2,1,0:T(8,128)(2,1)S(1)}, u32[]{:S(2)}, u32[]{:S(2)}) async-start(bf16[32,48,128]{2,1,0:T(8,128)(2,1)} %blend.1), calls=%async_computation.3 | async-start | bytes 786432 | tf_op jit(solution)/shard_map/all_to_all | solution.py:357
  96.4 0.0 copy-done
  96.5 0.0 copy-done.2
  96.5 0.8 tail.1
  97.3 9.9 %all-to-all-done.3 = bf16[32,48,128]{2,1,0:T(8,128)(2,1)S(1)} async-done(((bf16[32,48,128]{2,1,0:T(8,128)(2,1)}), bf16[32,48,128]{2,1,0:T(8,128)(2,1)S(1)}, u32[]{:S(2)}, u32[]{:S(2)}) %all-to-all-start.3) | async-done | bytes 393248 | tf_op jit(solution)/shard_map/all_to_all | solution.py:357
  107.2 0.6 merge.1
  107.9 8.8 %all_to_all.42 = bf16[2,8,2048]{2,1,0:T(8,128)(2,1)S(1)} all-to-all(bf16[2,8,2048]{2,1,0:T(8,128)(2,1)S(1)} %bitcast.14), channel_id=1, replica_groups=mesh['prefix'=16,'zh'=2,'y'=8,'tp'=2] {'tp'}, dimensions={0} | all-to-all | bytes 131072 | tf_op jit(solution)/shard_map/all_to_all | solution.py:360
  116.7 0.6 copy.9
Async XLA Ops:
  0.0 11.8 %copy-start.1 = (bf16[16,2048]{1,0:T(8,128)(2,1)S(1)}, bf16[16,2048]{1,0:T(8,128)(2,1)}, u32[]{:S(2)}) copy-start(bf16[16,2048]{1,0:T(8,128)(2,1)} %queries_ref.2) | copy-start | bytes 196612
  1.3 10.4 %copy-start.3 = (s32[16,1]{0,1:T(1,128)S(1)}, s32[16,1]{0,1:T(1,128)}, u32[]{:S(2)}) copy-start(s32[16,1]{0,1:T(1,128)} %param.8) | copy-start | bytes 196
  1.3 33.5 %collective-permute-start.2 = (bf16[2,1024,128]{2,1,0:T(8,128)(2,1)S(1)}, bf16[2,1024,128]{2,1,0:T(8,128)(2,1)S(1)}, u32[]{:S(2)}, u32[]{:S(2)}) collective-permute-start(bf16[2,1024,128]{2,1,0:T(8,128)(2,1)S(1)} %get-tuple-element.23), channel_id=1, source_target_pairs={{0,14},{1,3},{2,0},{3,5},{4,2},{5,7},{6,4},{7,9},{8,6},{9,11},{10,... | collective-permute-start | bytes 1572872 | tf_op jit(solution)/shard_map/ppermute | solution.py:334
  5.4 29.5 %collective-permute-start.1 = (bf16[2,1024,128]{2,1,0:T(8,128)(2,1)S(1)}, bf16[2,1024,128]{2,1,0:T(8,128)(2,1)S(1)}, u32[]{:S(2)}, u32[]{:S(2)}) collective-permute-start(bf16[2,1024,128]{2,1,0:T(8,128)(2,1)S(1)} %get-tuple-element.23), channel_id=1, source_target_pairs={{0,2},{1,15},{2,4},{3,1},{4,6},{5,3},{6,8},{7,5},{8,10},{9,7},{10,... | collective-permute-start | bytes 1572872 | tf_op jit(solution)/shard_map/ppermute | solution.py:334
  9.2 25.7 %collective-permute-start = (bf16[2,1024,128]{2,1,0:T(8,128)(2,1)S(1)}, bf16[2,1024,128]{2,1,0:T(8,128)(2,1)S(1)}, u32[]{:S(2)}, u32[]{:S(2)}) collective-permute-start(bf16[2,1024,128]{2,1,0:T(8,128)(2,1)S(1)} %get-tuple-element.24.refs_0_), channel_id=1, source_target_pairs={{0,12},{1,5},{2,14},{3,7},{4,0},{5,9},{6,2},{7,11},{8,4},{9,13},{1... | collective-permute-start | bytes 1572872 | tf_op jit(solution)/shard_map/ppermute | solution.py:334
  87.1 9.4 %copy-start = (bf16[16,2,64,256]{3,2,1,0:T(8,128)(2,1)S(1)}, bf16[16,2,64,256]{3,2,1,0:T(8,128)(2,1)}, u32[]{:S(2)}) copy-start(bf16[16,2,64,256]{3,2,1,0:T(8,128)(2,1)} %suffix_ref.1) | copy-start | bytes 3145732
  88.5 7.9 %copy-start.2 = (s32[1,16]{1,0:T(1,128)S(1)}, s32[1,16]{1,0:T(1,128)}, u32[]{:S(2)}) copy-start(s32[1,16]{1,0:T(1,128)} %length_ref.1) | copy-start | bytes 196
  88.5 18.7 %all-to-all-start.3 = ((bf16[32,48,128]{2,1,0:T(8,128)(2,1)}), bf16[32,48,128]{2,1,0:T(8,128)(2,1)S(1)}, u32[]{:S(2)}, u32[]{:S(2)}) async-start(bf16[32,48,128]{2,1,0:T(8,128)(2,1)} %blend.1), calls=%async_computation.3 | async-start | bytes 786432 | tf_op jit(solution)/shard_map/all_to_all | solution.py:357

commit v6 on v3

--- a/solution.py
+++ b/solution.py
@@ -260,14 +260,10 @@
 def attend(query, held):
     tokens = sum(part.shape[1] for part in held)
     ring, size, rows, width = query.shape
-    step = 4
-    whole = pl.BlockSpec(held[0].shape, lambda i: (0, 0, 0))
     return pl.pallas_call(
         attend_kernel,
-        grid=(ring // step,),
-        in_specs=[whole] * len(held)
-        + [pl.BlockSpec((step * size, rows, width), lambda i: (i, 0, 0))],
-        out_specs=pl.BlockSpec((step, size + 1, rows, width), lambda i: (i, 0, 0, 0)),
+        in_specs=[pl.BlockSpec(memory_space=pltpu.VMEM)] * (len(held) + 1),
+        out_specs=pl.BlockSpec(memory_space=pltpu.VMEM),
         out_shape=jax.ShapeDtypeStruct((ring, size + 1, rows, width), query.dtype),
         compiler_params=params(),
         cost_estimate=pl.CostEstimate(
@@ -327,13 +323,15 @@
     kv = lax.axis_index("y") % 2
     own = lax.dynamic_slice_in_dim(prefix_kv[0], kv * HEAD, HEAD, 2)
     other = lax.dynamic_slice_in_dim(prefix_kv[0], (1 - kv) * HEAD, HEAD, 2)
-    shared = [send(other, 1), send(other, -1), send(own, -2)]
+    far, near = send(own, -2), [send(other, 1), send(other, -1)]
     buckets = place(prefix_map, queries, owner_count)
     buckets = buckets.reshape((owner_count * Z_HALVES,) + buckets.shape[2:])
     mine = lax.all_to_all(buckets, plane, split_axis=0, concat_axis=0, tiled=True)
+    mine, far = lax.optimization_barrier((mine, far))
     sent = fan(mine, ring)
+    sent, near = lax.optimization_barrier((sent, near))
     query = lax.all_to_all(sent, "y", split_axis=0, concat_axis=0, tiled=True)
-    partial = attend(query, [own] + shared)
+    partial = attend(query, [own, far] + near)
     partial, queries = lax.optimization_barrier((partial, queries))
     back = lax.all_to_all(partial, "y", split_axis=0, concat_axis=0, tiled=True)
     tails = tail_attend(queries, suffix_kv, suffix_len)

time: 130 us -> 116 us (0.89)
  waiting for transfers between devices: 36.6 us -> 9.95 us
  blocking collectives: 53.4 us -> 70.2 us
  starting transfers between devices: 22.5 us -> 20.3 us
    ppermute x3, waiting for transfers between devices: 26.6 us -> 0.01 us  [send(): return lax.ppermute(array, ('y', 'tp'), pairs)]
    all_to_all x0 -> x1, blocking collectives: none -> 20.8 us  [per_device(): query = lax.all_to_all(sent, 'y', split_axis=0, concat_axis=0, tiled=True)]
    all_to_all x1 -> x0, starting transfers between devices: 6.82 us -> none  [per_device(): query = lax.all_to_all(sent, 'y', split_axis=0, concat_axis=0, tiled=True)]
    all_to_all x1, blocking collectives: 21.5 us -> 17.8 us  [per_device(): back = lax.all_to_all(partial, 'y', split_axis=0, concat_axis=0, tiled=True)]
    all_to_all x1, starting transfers between devices: 6.18 us -> 8.77 us  [per_device(): lax.all_to_all(blended, plane, split_axis=0, concat_axis=0, tiled=True)]
    ppermute x3, starting transfers between devices: 9.54 us -> 11.5 us  [send(): return lax.ppermute(array, ('y', 'tp'), pairs)]
    unnamed x12 -> x10, local copies, waits for them, and re-layouts: 2.21 us -> 0.73 us
  transfers between devices with their start and end apart: 5 -> 4, of which waited for: 3 -> 1; matrix products, arithmetic and copies ran while one was open for 0% -> 0% of each run, Pallas kernels for 1% -> 1%
where the time goes in v6:
time: 116 us
  blocking collectives  70.2 us (61%)
  starting transfers between devices  20.3 us (18%)
  Pallas kernels  13 us (11%)
  waiting for transfers between devices  9.95 us (9%)
  local copies, waits for them, and re-layouts  2.03 us (2%)
    all_to_all x1, blocking collectives, per_device(): lax.all_to_all(buckets, plane, split_axis=0, concat_axis=0, tiled=True)  22.7 us
    all_to_all x1, blocking collectives, per_device(): query = lax.all_to_all(sent, 'y', split_axis=0, concat_axis=0, tiled=True)  20.8 us
    all_to_all x1, blocking collectives, per_device(): back = lax.all_to_all(partial, 'y', split_axis=0, concat_axis=0, tiled=True)  17.8 us
    ppermute x3, starting transfers between devices, send(): return lax.ppermute(array, ('y', 'tp'), pairs)  11.5 us
    all_to_all x1, waiting for transfers between devices, per_device(): lax.all_to_all(blended, plane, split_axis=0, concat_axis=0, tiled=True)  9.95 us
    pallas_call x1, Pallas kernels, attend(): pl.pallas_call(attend_kernel, in_specs=[pl.BlockSpec(memory_space=pltpu.V...  9.81 us
    all_to_all x1, blocking collectives, per_device(): lax.all_to_all(attended, 'tp', split_axis=0, concat_axis=1, tiled=True)  8.86 us
    all_to_all x1, starting transfers between devices, per_device(): lax.all_to_all(blended, plane, split_axis=0, concat_axis=0, tiled=True)  8.77 us
  transfers between devices with their start and end apart: 4, of which 1 were waited for; matrix products, arithmetic and copies ran while one was open for 0% of the time, Pallas kernels for 1%

profile of v6, /device:TPU:1, one launch (start us, length us, event | category | flops | bytes accessed | tf_op | source)
XLA Modules:
  0.0 115.6 jit_solution(13262172876131855601)
XLA Ops:
  0.0 0.0 copy-start.1
  0.0 1.3 %dynamic-slice_bitcast_fusion = (bf16[2,1024,128]{2,1,0:T(8,128)(2,1)S(1)}, bf16[2,1024,128]{2,1,0:T(8,128)(2,1)S(1)}) fusion(bf16[1,2,1024,256]{3,2,1,0:T(8,128)(2,1)} %param.6, s32[]{:T(128)S(6)} %select_n.15, s32[]{:T(128)S(6)} %select_n.14), kind=kLoop, calls=%fused_computation | loop fusion | bytes 2097160 | tf_op jit(solution)/shard_map/dynamic_slice | solution.py:325
  1.3 0.0 copy-start.3
  1.3 5.0 %collective-permute-start = (bf16[2,1024,128]{2,1,0:T(8,128)(2,1)S(1)}, bf16[2,1024,128]{2,1,0:T(8,128)(2,1)S(1)}, u32[]{:S(2)}, u32[]{:S(2)}) collective-permute-start(bf16[2,1024,128]{2,1,0:T(8,128)(2,1)S(1)} %get-tuple-element.26.refs_0_), channel_id=1, source_target_pairs={{0,12},{1,5},{2,14},{3,7},{4,0},{5,9},{6,2},{7,11},{8,4},{9,13},{1... | collective-permute-start | bytes 1572872 | tf_op jit(solution)/shard_map/ppermute | solution.py:315
  6.4 3.2 %collective-permute-start.2 = (bf16[2,1024,128]{2,1,0:T(8,128)(2,1)S(1)}, bf16[2,1024,128]{2,1,0:T(8,128)(2,1)S(1)}, u32[]{:S(2)}, u32[]{:S(2)}) collective-permute-start(bf16[2,1024,128]{2,1,0:T(8,128)(2,1)S(1)} %get-tuple-element.25), channel_id=1, source_target_pairs={{0,14},{1,3},{2,0},{3,5},{4,2},{5,7},{6,4},{7,9},{8,6},{9,11},{10,... | collective-permute-start | bytes 1572872 | tf_op jit(solution)/shard_map/ppermute | solution.py:315
  9.6 3.3 %collective-permute-start.1 = (bf16[2,1024,128]{2,1,0:T(8,128)(2,1)S(1)}, bf16[2,1024,128]{2,1,0:T(8,128)(2,1)S(1)}, u32[]{:S(2)}, u32[]{:S(2)}) collective-permute-start(bf16[2,1024,128]{2,1,0:T(8,128)(2,1)S(1)} %get-tuple-element.25), channel_id=1, source_target_pairs={{0,2},{1,15},{2,4},{3,1},{4,6},{5,3},{6,8},{7,5},{8,10},{9,7},{10,... | collective-permute-start | bytes 1572872 | tf_op jit(solution)/shard_map/ppermute | solution.py:315
  12.9 0.0 copy-done.3
  12.9 0.1 copy.7.owners_ref
  13.0 0.0 copy-done.1
  13.0 0.4 place.1
  13.4 22.7 %all_to_all.39.mine_ref = bf16[32,32,128]{2,1,0:T(8,128)(2,1)S(1)} all-to-all(bf16[32,32,128]{2,1,0:T(8,128)(2,1)S(1)} %bitcast.12), channel_id=1, replica_groups=mesh['prefix'=16,'zh'=2,'y'=8,'tp'=2] {'prefix','zh'}, dimensions={0} | all-to-all | bytes 524288 | tf_op jit(solution)/shard_map/all_to_all | solution.py:329
  36.1 0.0 collective-permute-done.refs_1_
  36.1 0.1 fan.1
  36.1 0.0 collective-permute-done.2.refs_3_
  36.2 0.0 collective-permute-done.1.refs_2_
  36.2 20.8 %all_to_all.40 = bf16[8,16,16,128]{3,2,1,0:T(8,128)(2,1)S(1)} all-to-all(bf16[8,16,16,128]{3,2,1,0:T(8,128)(2,1)S(1)} %fan.1), channel_id=1, replica_groups=mesh['prefix'=16,'zh'=2,'y'=8,'tp'=2] {'y'}, dimensions={0} | all-to-all | bytes 1048576 | tf_op jit(solution)/shard_map/all_to_all | solution.py:333
  57.0 9.8 %attend.1 = bf16[8,17,16,128]{3,2,1,0:T(8,128)(2,1)S(1)} custom-call(bf16[2,1024,128]{2,1,0:T(8,128)(2,1)S(1)} %get-tuple-element.26.refs_0_, bf16[2,1024,128]{2,1,0:T(8,128)(2,1)S(1)} %collective-permute-done.refs_1_, bf16[2,1024,128]{2,1,0:T(8,128)(2,1)S(1)} %collective-permute-done.1.refs_2_, bf16[2,1024,128]{2,1,0:T(8,128)(2,1)S(1)} %collective-permute-done.2.refs_3_, ...), custom_call_target="tpu_custom_call" | custom-call | flops 6442450944 | bytes 1048576 | tf_op jit(solution)/shard_map/attend/pallas_call | solution.py:263
  66.8 17.8 %all_to_all.41.back_ref = bf16[8,17,16,128]{3,2,1,0:T(8,128)(2,1)S(1)} all-to-all(bf16[8,17,16,128]{3,2,1,0:T(8,128)(2,1)S(1)} %attend.1), channel_id=1, replica_groups=mesh['prefix'=16,'zh'=2,'y'=8,'tp'=2] {'y'}, dimensions={0} | all-to-all | bytes 1114112 | tf_op jit(solution)/shard_map/all_to_all | solution.py:336
  84.6 0.0 copy-start
  84.6 1.3 %blend.1 = bf16[32,48,128]{2,1,0:T(8,128)(2,1)} custom-call(bf16[8,17,16,128]{3,2,1,0:T(8,128)(2,1)S(1)} %all_to_all.41.back_ref), custom_call_target="tpu_custom_call" | custom-call | tf_op jit(solution)/shard_map/blend/pallas_call | solution.py:280
  85.9 0.0 copy-start.2
  85.9 8.8 %all-to-all-start.3 = ((bf16[32,48,128]{2,1,0:T(8,128)(2,1)}), bf16[32,48,128]{2,1,0:T(8,128)(2,1)S(1)}, u32[]{:S(2)}, u32[]{:S(2)}) async-start(bf16[32,48,128]{2,1,0:T(8,128)(2,1)} %blend.1), calls=%async_computation.3 | async-start | bytes 786432 | tf_op jit(solution)/shard_map/all_to_all | solution.py:339
  94.7 0.0 copy-done
  94.7 0.0 copy-done.2
  94.7 0.8 tail.1
  95.5 9.9 %all-to-all-done.3 = bf16[32,48,128]{2,1,0:T(8,128)(2,1)S(1)} async-done(((bf16[32,48,128]{2,1,0:T(8,128)(2,1)}), bf16[32,48,128]{2,1,0:T(8,128)(2,1)S(1)}, u32[]{:S(2)}, u32[]{:S(2)}) %all-to-all-start.3) | async-done | bytes 393248 | tf_op jit(solution)/shard_map/all_to_all | solution.py:339
  105.5 0.6 merge.1
  106.1 8.9 %all_to_all.42 = bf16[2,8,2048]{2,1,0:T(8,128)(2,1)S(1)} all-to-all(bf16[2,8,2048]{2,1,0:T(8,128)(2,1)S(1)} %bitcast.14), channel_id=1, replica_groups=mesh['prefix'=16,'zh'=2,'y'=8,'tp'=2] {'tp'}, dimensions={0} | all-to-all | bytes 131072 | tf_op jit(solution)/shard_map/all_to_all | solution.py:342
  115.0 0.6 copy.9
Async XLA Ops:
  0.0 13.0 %copy-start.1 = (bf16[16,2048]{1,0:T(8,128)(2,1)S(1)}, bf16[16,2048]{1,0:T(8,128)(2,1)}, u32[]{:S(2)}) copy-start(bf16[16,2048]{1,0:T(8,128)(2,1)} %queries_ref.2) | copy-start | bytes 196612
  1.3 11.6 %copy-start.3 = (s32[16,1]{0,1:T(1,128)S(1)}, s32[16,1]{0,1:T(1,128)}, u32[]{:S(2)}) copy-start(s32[16,1]{0,1:T(1,128)} %param.8) | copy-start | bytes 196
  1.3 34.7 %collective-permute-start = (bf16[2,1024,128]{2,1,0:T(8,128)(2,1)S(1)}, bf16[2,1024,128]{2,1,0:T(8,128)(2,1)S(1)}, u32[]{:S(2)}, u32[]{:S(2)}) collective-permute-start(bf16[2,1024,128]{2,1,0:T(8,128)(2,1)S(1)} %get-tuple-element.26.refs_0_), channel_id=1, source_target_pairs={{0,12},{1,5},{2,14},{3,7},{4,0},{5,9},{6,2},{7,11},{8,4},{9,13},{1... | collective-permute-start | bytes 1572872 | tf_op jit(solution)/shard_map/ppermute | solution.py:315
  6.4 29.8 %collective-permute-start.2 = (bf16[2,1024,128]{2,1,0:T(8,128)(2,1)S(1)}, bf16[2,1024,128]{2,1,0:T(8,128)(2,1)S(1)}, u32[]{:S(2)}, u32[]{:S(2)}) collective-permute-start(bf16[2,1024,128]{2,1,0:T(8,128)(2,1)S(1)} %get-tuple-element.25), channel_id=1, source_target_pairs={{0,14},{1,3},{2,0},{3,5},{4,2},{5,7},{6,4},{7,9},{8,6},{9,11},{10,... | collective-permute-start | bytes 1572872 | tf_op jit(solution)/shard_map/ppermute | solution.py:315
  9.6 26.6 %collective-permute-start.1 = (bf16[2,1024,128]{2,1,0:T(8,128)(2,1)S(1)}, bf16[2,1024,128]{2,1,0:T(8,128)(2,1)S(1)}, u32[]{:S(2)}, u32[]{:S(2)}) collective-permute-start(bf16[2,1024,128]{2,1,0:T(8,128)(2,1)S(1)} %get-tuple-element.25), channel_id=1, source_target_pairs={{0,2},{1,15},{2,4},{3,1},{4,6},{5,3},{6,8},{7,5},{8,10},{9,7},{10,... | collective-permute-start | bytes 1572872 | tf_op jit(solution)/shard_map/ppermute | solution.py:315
  84.6 10.0 %copy-start = (bf16[16,2,64,256]{3,2,1,0:T(8,128)(2,1)S(1)}, bf16[16,2,64,256]{3,2,1,0:T(8,128)(2,1)}, u32[]{:S(2)}) copy-start(bf16[16,2,64,256]{3,2,1,0:T(8,128)(2,1)} %suffix_ref.1) | copy-start | bytes 3145732
  85.9 8.8 %copy-start.2 = (s32[1,16]{1,0:T(1,128)S(1)}, s32[1,16]{1,0:T(1,128)}, u32[]{:S(2)}) copy-start(s32[1,16]{1,0:T(1,128)} %length_ref.1) | copy-start | bytes 196
  85.9 19.6 %all-to-all-start.3 = ((bf16[32,48,128]{2,1,0:T(8,128)(2,1)}), bf16[32,48,128]{2,1,0:T(8,128)(2,1)S(1)}, u32[]{:S(2)}, u32[]{:S(2)}) async-start(bf16[32,48,128]{2,1,0:T(8,128)(2,1)} %blend.1), calls=%async_computation.3 | async-start | bytes 786432 | tf_op jit(solution)/shard_map/all_to_all | solution.py:339

commit v7 on v6

--- a/solution.py
+++ b/solution.py
@@ -14,7 +14,7 @@
 ROWS = SLOTS * GROUP
 SCALE = HEAD ** (-0.5)
 LOG2E = math.log2(math.e)
-STATS = 16
+STATS = 8
 Z_HALVES = 2
 CLASSES = 4
 VMEM_LIMIT = 48 * 1024 * 1024
@@ -134,13 +134,12 @@
     eye = diagonal(HEAD)
     blocks = HEAD // ROWS
     groups = size // blocks
-    lane = iota((HEAD, HEAD), 1)
     table = back_ref[:, size].astype(jnp.float32)
     for half in range(2):
         for group in range(groups):
             here = slice(group * blocks, (group + 1) * blocks)
             there = slice(half * size + group * blocks, half * size + (group + 1) * blocks)
-            stats = jnp.zeros((HEAD, HEAD), jnp.float32)
+            stats = []
             for kv in range(kvs):
                 members = range(kv + 2 * half, ring, CLASSES)
                 levels = [
@@ -159,10 +158,10 @@
                 out_ref[there, kv * ROWS:(kv + 1) * ROWS] = mixed.astype(out_ref.dtype).reshape(
                     blocks, ROWS, HEAD
                 )
-                column = to_column(top + jnp.log(total), eye)
-                for index, piece in enumerate(pieces_of(column)):
-                    stats = jnp.where(lane == kv * 3 + index, piece, stats)
-            out_ref[there, kvs * ROWS:] = stats.astype(out_ref.dtype).reshape(blocks, STATS, HEAD)
+                stats += pieces_of(top + jnp.log(total))
+            stats.append(jnp.zeros((STATS - len(stats), HEAD), jnp.float32))
+            stats = jnp.concatenate(stats, axis=0).astype(out_ref.dtype)
+            out_ref[there, kvs * ROWS:] = jnp.broadcast_to(stats[None], (blocks, STATS, HEAD))
 
 
 def tail_kernel(queries_ref, suffix_ref, length_ref, out_ref, max_ref, total_ref):
@@ -197,26 +196,35 @@
         total_ref[kv] = jnp.broadcast_to(total, total_ref.shape[1:])
 
 
-def merge_kernel(owners_ref, back_ref, tail_ref, max_ref, total_ref, out_ref):
+def merge_kernel(spot_ref, owners_ref, back_ref, tail_ref, max_ref, total_ref, out_ref):
     requests = owners_ref.shape[0]
     owners, halves, kvs = back_ref.shape[0], back_ref.shape[1], tail_ref.shape[0]
     _, slot = slots_of(owners_ref[...])
     slot = jnp.concatenate([slot] * GROUP, axis=0).astype(jnp.int32)
     row = iota((GROUP * requests, 1), 0)
     lane = iota((1, owners * ROWS), 1)
-    pick = (slot * GROUP + row // requests) == lane
-    pick = jnp.where(pick, 1.0, 0.0).astype(jnp.bfloat16)
+    place_of = slot * GROUP + row // requests
+    pick = jnp.where(place_of == lane, 1.0, 0.0).astype(jnp.bfloat16)
+    stat_lane = iota((1, owners * STATS), 1)
+    owned = stat_lane // STATS == slot // SLOTS
+    wanted = iota((1, HEAD), 1) == spot_ref[0, 0] * ROWS + place_of % ROWS
 
     def picked(half, at):
         part = back_ref[:, half, at * ROWS:(at + 1) * ROWS].reshape(owners * ROWS, HEAD)
         return jnp.dot(pick, part, preferred_element_type=jnp.float32)
 
-    stats = [picked(half, kvs) for half in range(halves)]
+    def level_of(half, kv):
+        table = back_ref[:, half, kvs * ROWS:].astype(jnp.float32).reshape(owners * STATS, HEAD)
+        mine = owned & (stat_lane % STATS // 3 == kv)
+        level = jnp.dot(
+            jnp.where(mine, 1.0, 0.0).astype(jnp.bfloat16),
+            table.astype(jnp.bfloat16),
+            preferred_element_type=jnp.float32,
+        )
+        return jnp.sum(jnp.where(wanted, level, 0.0), axis=1, keepdims=True)
+
     for kv in range(kvs):
-        levels = [
-            stat[:, 3 * kv:3 * kv + 1] + stat[:, 3 * kv + 1:3 * kv + 2] + stat[:, 3 * kv + 2:3 * kv + 3]
-            for stat in stats
-        ]
+        levels = [level_of(half, kv) for half in range(halves)]
         overall = max_ref[kv]
         for level in levels:
             overall = jnp.maximum(overall, level)
@@ -296,13 +304,16 @@
     )(queries, suffix_kv, suffix_len)
 
 
-def merge(owners, back, tail, top, total, shape, dtype):
+def merge(spot, owners, back, tail, top, total, shape, dtype):
+    vmem = pl.BlockSpec(memory_space=pltpu.VMEM)
     return pl.pallas_call(
         merge_kernel,
+        in_specs=[pl.BlockSpec(memory_space=pltpu.SMEM)] + [vmem] * 5,
+        out_specs=vmem,
         out_shape=jax.ShapeDtypeStruct(shape, dtype),
         compiler_params=params(),
         name="merge",
-    )(owners, back, tail, top, total)
+    )(spot, owners, back, tail, top, total)
 
 
 def send(array, step):
@@ -338,7 +349,8 @@
     blended = blend(back, kvs)
     back = lax.all_to_all(blended, plane, split_axis=0, concat_axis=0, tiled=True)
     back = back.reshape((owner_count, Z_HALVES) + back.shape[1:])
-    attended = merge(prefix_map, back, *tails, queries.shape, queries.dtype)
+    spot = (lax.axis_index(plane) % (HEAD // ROWS)).astype(jnp.int32).reshape(1, 1)
+    attended = merge(spot, prefix_map, back, *tails, queries.shape, queries.dtype)
     return lax.all_to_all(attended, "tp", split_axis=0, concat_axis=1, tiled=True)
 
 

time: 116 us -> 115 us (level)
  waiting for transfers between devices: 9.95 us -> 8.78 us
    all_to_all x1, waiting for transfers between devices: 9.95 us -> 8.77 us  [per_device(): lax.all_to_all(blended, plane, split_axis=0, concat_axis=0, tiled=True)]
where the time goes in v7:
time: 115 us
  blocking collectives  70.3 us (61%)
  starting transfers between devices  20.2 us (18%)
  Pallas kernels  12.8 us (11%)
  waiting for transfers between devices  8.78 us (8%)
  local copies, waits for them, and re-layouts  2.66 us (2%)
    all_to_all x1, blocking collectives, per_device(): lax.all_to_all(buckets, plane, split_axis=0, concat_axis=0, tiled=True)  22.7 us
    all_to_all x1, blocking collectives, per_device(): query = lax.all_to_all(sent, 'y', split_axis=0, concat_axis=0, tiled=True)  20.8 us
    all_to_all x1, blocking collectives, per_device(): back = lax.all_to_all(partial, 'y', split_axis=0, concat_axis=0, tiled=True)  17.8 us
    ppermute x3, starting transfers between devices, send(): return lax.ppermute(array, ('y', 'tp'), pairs)  11.5 us
    pallas_call x1, Pallas kernels, attend(): pl.pallas_call(attend_kernel, in_specs=[pl.BlockSpec(memory_space=pltpu.V...  9.81 us
    all_to_all x1, blocking collectives, per_device(): lax.all_to_all(attended, 'tp', split_axis=0, concat_axis=1, tiled=True)  8.99 us
    all_to_all x1, waiting for transfers between devices, per_device(): lax.all_to_all(blended, plane, split_axis=0, concat_axis=0, tiled=True)  8.77 us
    all_to_all x1, starting transfers between devices, per_device(): lax.all_to_all(blended, plane, split_axis=0, concat_axis=0, tiled=True)  8.64 us
  transfers between devices with their start and end apart: 4, of which 1 were waited for; matrix products, arithmetic and copies ran while one was open for 0% of the time, Pallas kernels for 1%

profile of v7, /device:TPU:1, one launch (start us, length us, event | category | flops | bytes accessed | tf_op | source)
XLA Modules:
  0.0 114.8 jit_solution(12993405599398126305)
XLA Ops:
  0.0 0.0 copy-start.1
  0.0 1.3 %dynamic-slice_bitcast_fusion = (bf16[2,1024,128]{2,1,0:T(8,128)(2,1)S(1)}, bf16[2,1024,128]{2,1,0:T(8,128)(2,1)S(1)}) fusion(bf16[1,2,1024,256]{3,2,1,0:T(8,128)(2,1)} %param.6, s32[]{:T(128)S(6)} %select_n.20, s32[]{:T(128)S(6)} %select_n.19), kind=kLoop, calls=%fused_computation | loop fusion | bytes 2097160 | tf_op jit(solution)/shard_map/dynamic_slice | solution.py:336
  1.3 0.0 copy-start.3
  1.3 5.0 %collective-permute-start = (bf16[2,1024,128]{2,1,0:T(8,128)(2,1)S(1)}, bf16[2,1024,128]{2,1,0:T(8,128)(2,1)S(1)}, u32[]{:S(2)}, u32[]{:S(2)}) collective-permute-start(bf16[2,1024,128]{2,1,0:T(8,128)(2,1)S(1)} %get-tuple-element.26.refs_0_), channel_id=1, source_target_pairs={{0,12},{1,5},{2,14},{3,7},{4,0},{5,9},{6,2},{7,11},{8,4},{9,13},{1... | collective-permute-start | bytes 1572872 | tf_op jit(solution)/shard_map/ppermute | solution.py:326
  6.4 3.2 %collective-permute-start.2 = (bf16[2,1024,128]{2,1,0:T(8,128)(2,1)S(1)}, bf16[2,1024,128]{2,1,0:T(8,128)(2,1)S(1)}, u32[]{:S(2)}, u32[]{:S(2)}) collective-permute-start(bf16[2,1024,128]{2,1,0:T(8,128)(2,1)S(1)} %get-tuple-element.25), channel_id=1, source_target_pairs={{0,14},{1,3},{2,0},{3,5},{4,2},{5,7},{6,4},{7,9},{8,6},{9,11},{10,... | collective-permute-start | bytes 1572872 | tf_op jit(solution)/shard_map/ppermute | solution.py:326
  9.6 3.3 %collective-permute-start.1 = (bf16[2,1024,128]{2,1,0:T(8,128)(2,1)S(1)}, bf16[2,1024,128]{2,1,0:T(8,128)(2,1)S(1)}, u32[]{:S(2)}, u32[]{:S(2)}) collective-permute-start(bf16[2,1024,128]{2,1,0:T(8,128)(2,1)S(1)} %get-tuple-element.25), channel_id=1, source_target_pairs={{0,2},{1,15},{2,4},{3,1},{4,6},{5,3},{6,8},{7,5},{8,10},{9,7},{10,... | collective-permute-start | bytes 1572872 | tf_op jit(solution)/shard_map/ppermute | solution.py:326
  12.9 0.0 copy-done.3
  12.9 0.1 copy.7.owners_ref
  13.0 0.0 copy-done.1
  13.0 0.4 place.1
  13.4 22.7 %all_to_all.39.mine_ref = bf16[32,32,128]{2,1,0:T(8,128)(2,1)S(1)} all-to-all(bf16[32,32,128]{2,1,0:T(8,128)(2,1)S(1)} %bitcast.13), channel_id=1, replica_groups=mesh['prefix'=16,'zh'=2,'y'=8,'tp'=2] {'prefix','zh'}, dimensions={0} | all-to-all | bytes 524288 | tf_op jit(solution)/shard_map/all_to_all | solution.py:340
  36.1 0.0 collective-permute-done.refs_1_
  36.1 0.1 fan.1
  36.1 0.0 collective-permute-done.2.refs_3_
  36.2 0.0 collective-permute-done.1.refs_2_
  36.2 20.8 %all_to_all.40 = bf16[8,16,16,128]{3,2,1,0:T(8,128)(2,1)S(1)} all-to-all(bf16[8,16,16,128]{3,2,1,0:T(8,128)(2,1)S(1)} %fan.1), channel_id=1, replica_groups=mesh['prefix'=16,'zh'=2,'y'=8,'tp'=2] {'y'}, dimensions={0} | all-to-all | bytes 1048576 | tf_op jit(solution)/shard_map/all_to_all | solution.py:344
  57.0 9.8 %attend.1 = bf16[8,17,16,128]{3,2,1,0:T(8,128)(2,1)S(1)} custom-call(bf16[2,1024,128]{2,1,0:T(8,128)(2,1)S(1)} %get-tuple-element.26.refs_0_, bf16[2,1024,128]{2,1,0:T(8,128)(2,1)S(1)} %collective-permute-done.refs_1_, bf16[2,1024,128]{2,1,0:T(8,128)(2,1)S(1)} %collective-permute-done.1.refs_2_, bf16[2,1024,128]{2,1,0:T(8,128)(2,1)S(1)} %collective-permute-done.2.refs_3_, ...), custom_call_target="tpu_custom_call" | custom-call | flops 6442450944 | bytes 1048576 | tf_op jit(solution)/shard_map/attend/pallas_call | solution.py:271
  66.8 17.8 %all_to_all.41.back_ref = bf16[8,17,16,128]{3,2,1,0:T(8,128)(2,1)S(1)} all-to-all(bf16[8,17,16,128]{3,2,1,0:T(8,128)(2,1)S(1)} %attend.1), channel_id=1, replica_groups=mesh['prefix'=16,'zh'=2,'y'=8,'tp'=2] {'y'}, dimensions={0} | all-to-all | bytes 1114112 | tf_op jit(solution)/shard_map/all_to_all | solution.py:347
  84.6 0.0 copy-start
  84.6 1.1 blend.1
  85.7 8.6 %all-to-all-start.3 = ((bf16[32,40,128]{2,1,0:T(8,128)(2,1)}), bf16[32,40,128]{2,1,0:T(8,128)(2,1)S(1)}, u32[]{:S(2)}, u32[]{:S(2)}) async-start(bf16[32,40,128]{2,1,0:T(8,128)(2,1)} %blend.1), calls=%async_computation.3 | async-start | bytes 655360 | tf_op jit(solution)/shard_map/all_to_all | solution.py:350
  94.4 0.0 copy-start.2
  94.4 0.0 copy-done
  94.4 0.6 copy-done.2
  95.1 0.8 tail.1
  95.9 8.8 %all-to-all-done.3 = bf16[32,40,128]{2,1,0:T(8,128)(2,1)S(1)} async-done(((bf16[32,40,128]{2,1,0:T(8,128)(2,1)}), bf16[32,40,128]{2,1,0:T(8,128)(2,1)S(1)}, u32[]{:S(2)}, u32[]{:S(2)}) %all-to-all-start.3) | async-done | bytes 327712 | tf_op jit(solution)/shard_map/all_to_all | solution.py:350
  104.7 0.6 merge.1
  105.2 9.0 %all_to_all.42 = bf16[2,8,2048]{2,1,0:T(8,128)(2,1)S(1)} all-to-all(bf16[2,8,2048]{2,1,0:T(8,128)(2,1)S(1)} %bitcast.15), channel_id=1, replica_groups=mesh['prefix'=16,'zh'=2,'y'=8,'tp'=2] {'tp'}, dimensions={0} | all-to-all | bytes 131072 | tf_op jit(solution)/shard_map/all_to_all | solution.py:354
  114.2 0.6 copy.9
Async XLA Ops:
  0.0 13.0 %copy-start.1 = (bf16[16,2048]{1,0:T(8,128)(2,1)S(1)}, bf16[16,2048]{1,0:T(8,128)(2,1)}, u32[]{:S(2)}) copy-start(bf16[16,2048]{1,0:T(8,128)(2,1)} %queries_ref.2) | copy-start | bytes 196612
  1.3 11.6 %copy-start.3 = (s32[16,1]{0,1:T(1,128)S(1)}, s32[16,1]{0,1:T(1,128)}, u32[]{:S(2)}) copy-start(s32[16,1]{0,1:T(1,128)} %param.8) | copy-start | bytes 196
  1.3 34.7 %collective-permute-start = (bf16[2,1024,128]{2,1,0:T(8,128)(2,1)S(1)}, bf16[2,1024,128]{2,1,0:T(8,128)(2,1)S(1)}, u32[]{:S(2)}, u32[]{:S(2)}) collective-permute-start(bf16[2,1024,128]{2,1,0:T(8,128)(2,1)S(1)} %get-tuple-element.26.refs_0_), channel_id=1, source_target_pairs={{0,12},{1,5},{2,14},{3,7},{4,0},{5,9},{6,2},{7,11},{8,4},{9,13},{1... | collective-permute-start | bytes 1572872 | tf_op jit(solution)/shard_map/ppermute | solution.py:326
  6.4 29.8 %collective-permute-start.2 = (bf16[2,1024,128]{2,1,0:T(8,128)(2,1)S(1)}, bf16[2,1024,128]{2,1,0:T(8,128)(2,1)S(1)}, u32[]{:S(2)}, u32[]{:S(2)}) collective-permute-start(bf16[2,1024,128]{2,1,0:T(8,128)(2,1)S(1)} %get-tuple-element.25), channel_id=1, source_target_pairs={{0,14},{1,3},{2,0},{3,5},{4,2},{5,7},{6,4},{7,9},{8,6},{9,11},{10,... | collective-permute-start | bytes 1572872 | tf_op jit(solution)/shard_map/ppermute | solution.py:326
  9.6 26.6 %collective-permute-start.1 = (bf16[2,1024,128]{2,1,0:T(8,128)(2,1)S(1)}, bf16[2,1024,128]{2,1,0:T(8,128)(2,1)S(1)}, u32[]{:S(2)}, u32[]{:S(2)}) collective-permute-start(bf16[2,1024,128]{2,1,0:T(8,128)(2,1)S(1)} %get-tuple-element.25), channel_id=1, source_target_pairs={{0,2},{1,15},{2,4},{3,1},{4,6},{5,3},{6,8},{7,5},{8,10},{9,7},{10,... | collective-permute-start | bytes 1572872 | tf_op jit(solution)/shard_map/ppermute | solution.py:326
  84.6 9.8 %copy-start = (bf16[16,2,64,256]{3,2,1,0:T(8,128)(2,1)S(1)}, bf16[16,2,64,256]{3,2,1,0:T(8,128)(2,1)}, u32[]{:S(2)}) copy-start(bf16[16,2,64,256]{3,2,1,0:T(8,128)(2,1)} %suffix_ref.1) | copy-start | bytes 3145732
  85.7 18.9 %all-to-all-start.3 = ((bf16[32,40,128]{2,1,0:T(8,128)(2,1)}), bf16[32,40,128]{2,1,0:T(8,128)(2,1)S(1)}, u32[]{:S(2)}, u32[]{:S(2)}) async-start(bf16[32,40,128]{2,1,0:T(8,128)(2,1)} %blend.1), calls=%async_computation.3 | async-start | bytes 655360 | tf_op jit(solution)/shard_map/all_to_all | solution.py:350
  94.4 0.7 copy-start.2
